TPU v7x, 256 devices: a whole 4x4x8 slice. The times are simulated.
256 devices in a mesh: rows: 64 (over x, z, core), rhs: 4 (over y).
Axes of the slice: x: 4, y: 4, z: 8, core: 2. Of those that a mesh axis runs over, the one named last changes fastest.
Arguments:
- right_sides: float32 [4, 65536, 512], P(None, 'rows', 'rhs'), may hold values from -6 to 6
- butterfly_diagonals: float32 [2, 4, 65536], P(None, None, 'rows'), may hold values from 0.5 to 2
- band_rows: float32 [1024, 4, 65536], P(None, None, ('rows', 'rhs')), may hold values from -0.1875 to 0.1875
- diag_inverse: float32 [1024, 1024], replicated, as said below
- band_block: int32 [1], replicated, may hold values from 0 to 254
Outputs:
- updated_sides: float32 [4, 65536, 512], P(None, 'rows', 'rhs')
Inputs may be any that keep to these rules, and one draw needn't show every extreme that they name: `diag_inverse`: upper triangular with diagonal entries between 0.5 and 1.
All inputs are finite; a program needn't handle non-finite values.
Results may differ from a plain program's by a relative error of at most 0.000082.
Values sent between devices are 32-bit elements; how exact they have to be, the bound alone decides.
No kernel may reach another device: no remote copies, remote signals or barrier semaphores. Data moves between devices by JAX's collectives and lax.ppermute only.
A program may use at most 128 MiB of HBM per device.

v0:
```python
import jax
import jax.numpy as jnp
from jax import lax
from jax.sharding import PartitionSpec as P


def from_partner(value, axis, distance):
    mask = 2**distance
    pairs = [(source, source ^ mask) for source in range(lax.axis_size(axis))]
    return lax.ppermute(value, axis, pairs)


def broadcast(array, axis, root):
    mine = lax.axis_index(axis) == root
    return lax.psum(jnp.where(mine, array, jnp.zeros_like(array)), axis)


def apply_level(values, partner, coefs, mine, bit):
    factor = 1.0 / jnp.sqrt(jnp.float32(2.0))
    is_lower = mine >> bit & 1 == 1
    mixed = jnp.where(is_lower, partner - values, values + partner)
    return coefs[:, :, None] * mixed * factor


def per_device(right_sides, butterfly_diagonals, band_rows, diag_inverse, band_block):
    parts = lax.axis_size("rows")
    top_bit = parts.bit_length() - 1
    mine = lax.axis_index("rows")
    cycles = right_sides.shape[0]
    partner = from_partner(right_sides, "rows", top_bit - 1)
    moved = apply_level(right_sides, partner, butterfly_diagonals[0], mine, top_bit - 1)
    partner = from_partner(moved, "rows", top_bit - 2)
    moved = apply_level(moved, partner, butterfly_diagonals[1], mine, top_bit - 2)
    start = band_block[0]
    owner_cycle = start // parts
    owner = start % parts
    band_rhs = lax.dynamic_index_in_dim(moved, owner_cycle, 0, keepdims=False)
    solved = jnp.dot(
        diag_inverse.T,
        band_rhs,
        precision=lax.Precision.HIGHEST,
        preferred_element_type=jnp.float32,
    )
    solved = broadcast(solved, "rows", owner)
    all_solved = lax.all_gather(solved, "rhs", axis=1, tiled=True)
    partial_update = jnp.einsum(
        "bck,bn->ckn",
        band_rows,
        all_solved,
        precision=lax.Precision.HIGHEST,
        preferred_element_type=jnp.float32,
    )
    update = lax.all_to_all(partial_update, "rhs", split_axis=2, concat_axis=1, tiled=True)
    index = (jnp.arange(cycles, dtype=jnp.int32) * parts + mine)[:, None, None]
    return jnp.where(index == start, solved[None], jnp.where(index > start, moved - update, moved))


def solution(mesh):
    return jax.shard_map(
        per_device,
        mesh=mesh,
        in_specs=(
            P(None, "rows", "rhs"),
            P(None, None, "rows"),
            P(None, None, ("rows", "rhs")),
            P(),
            P(),
        ),
        out_specs=P(None, "rows", "rhs"),
        check_vma=False,
    )
```

profile of v0, /device:TPU:1, one launch (start us, length us, event | category | flops | bytes accessed | tf_op | source)
XLA Modules:
  0.0 386.3 jit_solution(4957429985234655281)
XLA Ops:
  6.5 0.0 all-reduce.2.cloned.1.call-start
  6.5 3.6 collective-permute-start
  10.1 0.7 slice_bitcast_fusion.1
  10.8 43.9 %collective-permute-done = f32[4,1024,128]{2,1,0:T(8,128)S(1)} collective-permute-done((f32[4,1024,128]{2,1,0:T(8,128)}, f32[4,1024,128]{2,1,0:T(8,128)S(1)}, u32[]{:S(2)}, u32[]{:S(2)}) %collective-permute-start) | collective-permute-done | bytes 2097184 | tf_op jit(solution)/shard_map/ppermute | solution.py:10
  54.7 0.0 copy-start.2
  54.7 1.3 copy-done.2
  56.0 2.5 multiply_multiply_fusion.1
  58.6 0.0 copy-start
  58.6 2.2 collective-permute-start.1
  61.4 43.5 %collective-permute-done.1 = f32[4,1024,128]{2,1,0:T(8,128)} collective-permute-done((f32[4,1024,128]{2,1,0:T(8,128)S(1)}, f32[4,1024,128]{2,1,0:T(8,128)}, u32[]{:S(2)}, u32[]{:S(2)}) %collective-permute-start.1) | collective-permute-done | bytes 2097184 | tf_op jit(solution)/shard_map/ppermute | solution.py:10
  105.0 0.0 copy-done
  105.0 0.0 copy-start.1
  105.0 2.7 multiply_multiply_fusion
  107.7 0.7 copy-done.1
  108.4 3.2 fusion.9
  111.6 0.0 all-reduce.2.cloned.1.call-update
  111.6 0.0 all-gather.2.cloned.1.call-start
  111.7 184.4 %all-reduce.2.cloned.1.call-done = f32[1024,128]{0,1:T(8,128)} async-done(((f32[1024,128]{0,1:T(8,128)}), f32[1024,128]{0,1:T(8,128)}) %all-reduce.2.cloned.1.call-update) | async-done | bytes 524304 | tf_op jit(solution)/shard_map/psum | solution.py:15
  296.1 0.0 all-gather.2.cloned.1.call-update
  296.1 34.6 %all-gather.2.cloned.1.call-done = f32[1024,512]{0,1:T(8,128)} async-done(((f32[1024,128]{0,1:T(8,128)}), f32[1024,512]{0,1:T(8,128)}) %all-gather.2.cloned.1.call-update) | async-done | bytes 2097168 | tf_op jit(solution)/shard_map/all_gather | solution.py:45
  330.7 9.6 %fusion.4 = f32[4,256,512]{1,2,0:T(8,128)S(1)} fusion(f32[1024,4,256]{2,1,0:T(4,128)} %param.7, f32[1024,512]{0,1:T(8,128)} %all-gather.2.cloned.1.call-done), kind=kOutput, calls=%fused_computation.7 | convolution fusion | flops 6442450944 | bytes 8388608 | tf_op jit(solution)/shard_map/bck,bn->ckn/dot_general | solution.py:46
  340.3 2.7 copy.11
  342.9 0.0 copy-start.3
  342.9 4.6 %all-to-all-start = ((f32[4,256,512]{1,0,2:T(4,128)}), f32[4,256,512]{1,0,2:T(4,128)}, u32[]{:S(2)}, u32[]{:S(2)}) async-start(f32[4,256,512]{1,0,2:T(4,128)} %copy.11), calls=%async_computation | async-start | bytes 4194304 | tf_op jit(solution)/shard_map/all_to_all | solution.py:53
  347.5 0.0 copy-done.3
  347.5 0.2 copy.9
  347.7 25.6 %all-to-all-done = f32[4,256,512]{1,0,2:T(4,128)} async-done(((f32[4,256,512]{1,0,2:T(4,128)}), f32[4,256,512]{1,0,2:T(4,128)}, u32[]{:S(2)}, u32[]{:S(2)}) %all-to-all-start) | async-done | bytes 2097184 | tf_op jit(solution)/shard_map/all_to_all | solution.py:53
  373.3 2.9 copy.12
  376.2 3.3 fusion.2
  (1 shorter events, 0.0 us)
Async XLA Ops:
  6.5 289.6 %all-reduce.2.cloned.1.call-start = ((), (), s32[]{:S(2)}) async-start(), calls=%async_computation.1 | async-start | bytes 1048576 | tf_op jit(solution)/shard_map/psum | solution.py:15
  6.5 48.2 %collective-permute-start = (f32[4,1024,128]{2,1,0:T(8,128)}, f32[4,1024,128]{2,1,0:T(8,128)S(1)}, u32[]{:S(2)}, u32[]{:S(2)}) collective-permute-start(f32[4,1024,128]{2,1,0:T(8,128)} %param.5), channel_id=1, source_target_pairs={{0,128},{4,132},{8,136},{12,140},{16,144},{20,148},{24,152},{28,15... | collective-permute-start | bytes 6291464 | tf_op jit(solution)/shard_map/ppermute | solution.py:10
  54.7 1.3 copy-start.2
  58.6 46.4 %copy-start = (f32[4,1024,128]{2,1,0:T(8,128)}, f32[4,1024,128]{2,1,0:T(8,128)S(1)}, u32[]{:S(2)}) copy-start(f32[4,1024,128]{2,1,0:T(8,128)S(1)} %multiply_multiply_fusion.1) | copy-start | bytes 6291460
  58.6 46.3 %collective-permute-start.1 = (f32[4,1024,128]{2,1,0:T(8,128)S(1)}, f32[4,1024,128]{2,1,0:T(8,128)}, u32[]{:S(2)}, u32[]{:S(2)}) collective-permute-start(f32[4,1024,128]{2,1,0:T(8,128)S(1)} %multiply_multiply_fusion.1), channel_id=1, source_target_pairs={{0,64},{4,68},{8,72},{12,76},{16,80},{20,84},{24,88},{28,92},{32,9... | collective-permute-start | bytes 6291464 | tf_op jit(solution)/shard_map/ppermute | solution.py:10
  105.0 3.5 copy-start.1
  111.6 219.0 %all-gather.2.cloned.1.call-start = ((), (), s32[]{:S(2)}) async-start(), calls=%async_computation.2 | async-start | bytes 2621440 | tf_op jit(solution)/shard_map/all_gather | solution.py:45
  342.9 4.6 %copy-start.3 = (f32[1024,128]{0,1:T(8,128)S(1)}, f32[1024,128]{0,1:T(8,128)}, u32[]{:S(2)}) copy-start(f32[1024,128]{0,1:T(8,128)} %all-reduce.2.cloned.1.call-done) | copy-start | bytes 1572868
  342.9 30.4 %all-to-all-start = ((f32[4,256,512]{1,0,2:T(4,128)}), f32[4,256,512]{1,0,2:T(4,128)}, u32[]{:S(2)}, u32[]{:S(2)}) async-start(f32[4,256,512]{1,0,2:T(4,128)} %copy.11), calls=%async_computation | async-start | bytes 4194304 | tf_op jit(solution)/shard_map/all_to_all | solution.py:53
Sparse Core Ops, SparseCore 0:
  111.8 184.2 all-reduce.1
  297.9 32.7 all-gather.1
where the time goes:
time: 387 us; the launch traced here: 386 us
  waiting for transfers between devices  332 us (86%)
  between operations  14.2 us (4%)
  matrix products  12.8 us (3%)
  starting transfers between devices  10.4 us (3%)
  local copies, waits for them, and re-layouts  8.57 us (2%)
  other arithmetic  8.5 us (2%)
    psum x1, waiting for transfers between devices, broadcast(): return lax.psum(jnp.where(mine, array, jnp.zeros_like(array)), axis)  184 us
    ppermute x2, waiting for transfers between devices, from_partner(): return lax.ppermute(value, axis, pairs)  87.4 us
    all_gather x1, waiting for transfers between devices, per_device(): all_solved = lax.all_gather(solved, 'rhs', axis=1, tiled=True)  34.6 us
    all_to_all x1, waiting for transfers between devices, per_device(): lax.all_to_all(partial_update, 'rhs', split_axis=2, concat_axis=1, tiled=...  25.6 us
    dot_general x1, matrix products, per_device(): jnp.einsum('bck,bn->ckn', band_rows, all_solved, precision=lax.Precision....  9.57 us
  transfers between devices with their start and end apart: 5, of which 5 were waited for; matrix products, arithmetic and copies ran while one was open for 0% of the time, Pallas kernels for 0%

commit v1 on v0

v1 whole, which is shorter than its diff:
```python
import functools
import jax
import jax.numpy as jnp
from jax import lax
from jax.experimental import pallas as pl
from jax.experimental.pallas import tpu as pltpu
from jax.sharding import PartitionSpec as P

NX, NZ, NC, NY = 4, 8, 2, 4
NB = 1024
HALF = 16
F32 = jnp.float32
BF16 = jnp.bfloat16


def row_perm(move):
    pairs = []
    for x in range(NX):
        for z in range(NZ):
            for c in range(NC):
                a, b, d = move(x, z, c)
                pairs.append(((x * NZ + z) * NC + c, ((a % NX) * NZ + b % NZ) * NC + d))
    return pairs


def shift_x(v, s):
    return lax.ppermute(v, "rows", row_perm(lambda x, z, c: (x + s, z, c)))


def shift_z(v, s):
    return lax.ppermute(v, "rows", row_perm(lambda x, z, c: (x, z + s, c)))


def other_core(v):
    return lax.ppermute(v, "rows", row_perm(lambda x, z, c: (x, z, 1 - c)))


def shift_y(v, s):
    return lax.ppermute(v, "rhs", [(i, (i + s) % NY) for i in range(NY)])


X_GROUPS = [[(x * NZ + z) * NC + c for x in range(NX)] for z in range(NZ) for c in range(NC)]


def exchange_x(v):
    return lax.all_to_all(v, "rows", 0, 0, axis_index_groups=X_GROUPS, tiled=True)


def params(mib):
    return pltpu.CompilerParams(vmem_limit_bytes=mib << 20)


def prep_kernel(info, slab, diag, out):
    cycle = info[0] // (NX * NZ * NC)
    flipped = slab[0].T
    for i in range(NX):
        out[i, :32, :] = flipped[32 * i : 32 * i + 32]
        out[i, 32:33, :] = diag[0, pl.ds(cycle, 1), :]
        out[i, 33:34, :] = diag[1, pl.ds(cycle, 1), :]
        out[i, 34:40, :] = jnp.zeros((6, NB), F32)


def prep(info, right_sides, diag):
    return pl.pallas_call(
        prep_kernel,
        grid_spec=pltpu.PrefetchScalarGridSpec(
            num_scalar_prefetch=1,
            grid=(1,),
            in_specs=[
                pl.BlockSpec((1, NB, 128), lambda i, s: (s[0] // (NX * NZ * NC), 0, 0)),
                pl.BlockSpec((2, 4, NB), lambda i, s: (0, 0, 0)),
            ],
            out_specs=pl.BlockSpec((NX, 40, NB), lambda i, s: (0, 0, 0)),
        ),
        out_shape=jax.ShapeDtypeStruct((NX, 40, NB), F32),
        compiler_params=params(16),
        name="prep",
    )(info, right_sides, diag)


def solve_kernel(info, got, inverse, out):
    x0 = info[0] % (NX * NZ * NC) // (NZ * NC)
    high = x0 & 2
    sign_high = jnp.where(high == 0, 1.0, -1.0).astype(F32)
    sign_low = jnp.where((x0 & 1) == 0, 1.0, -1.0).astype(F32)
    level = [
        got[high | p, 32:33, :] * (got[p, :32, :] + sign_high * got[p + 2, :32, :])
        for p in range(2)
    ]
    sides = got[x0, 33:34, :] * (0.5 * (level[0] + sign_low * level[1]))
    out[...] = jnp.dot(
        sides, inverse[...], precision=lax.Precision.HIGHEST, preferred_element_type=F32
    )


def solve(info, got, inverse):
    return pl.pallas_call(
        solve_kernel,
        grid_spec=pltpu.PrefetchScalarGridSpec(
            num_scalar_prefetch=1,
            grid=(4,),
            in_specs=[
                pl.BlockSpec((NX, 40, NB), lambda i, s: (0, 0, 0)),
                pl.BlockSpec((NB, 256), lambda i, s: (0, i)),
            ],
            out_specs=pl.BlockSpec((32, 256), lambda i, s: (0, i)),
        ),
        out_shape=jax.ShapeDtypeStruct((32, NB), F32),
        compiler_params=params(24),
        name="solve",
    )(info, got, inverse)


def split(v):
    top = v.astype(BF16)
    return top, (v - top.astype(F32)).astype(BF16)


def band_kernel(rows, top, low):
    for c in range(4):
        a, b = split(rows[:, c, :])
        top[c] = a
        low[c] = b


def split_band(band_rows):
    spec = pl.BlockSpec((4, 256, 256), lambda i: (0, i, 0))
    shape = jax.ShapeDtypeStruct((4, NB, 256), BF16)
    return pl.pallas_call(
        band_kernel,
        grid=(4,),
        in_specs=[pl.BlockSpec((256, 4, 256), lambda i: (i, 0, 0))],
        out_specs=[spec, spec],
        out_shape=[shape, shape],
        compiler_params=params(24),
        name="split_band",
    )(band_rows)


def update_kernel(info, *refs):
    own, other = refs[0:4], refs[4:8]
    top, low = refs[8:10]
    outs, mine = refs[10:14], refs[14]
    left_top, left_low = refs[15:17]

    @pl.when(pl.program_id(0) == 0)
    def _():
        x, core = info[1], info[3]
        for t in range(NX):
            for h in range(NC):
                base = 32 * ((x - t + NX) % NX) + HALF * (core ^ h)
                for s in range(NY):
                    piece = (other if h else own)[t][HALF * s : HALF * s + HALF, :]
                    a, b = split(piece)
                    at = pl.ds(pl.multiple_of(128 * s + base, HALF), HALF)
                    left_top[at, :] = a
                    left_low[at, :] = b
                    if s == 0:
                        mine[pl.ds(pl.multiple_of(base, HALF), HALF), :] = piece

    for s in range(NY):
        at = slice(128 * s, 128 * s + 128)
        outs[s][...] = (
            jnp.dot(left_top[at, :], low[0], preferred_element_type=F32)
            + jnp.dot(left_low[at, :], top[0], preferred_element_type=F32)
            + jnp.dot(left_top[at, :], top[0], preferred_element_type=F32)
        )


def update(info, own, other, top, low):
    whole = pl.BlockSpec((64, NB), lambda i, s: (0, 0))
    band = pl.BlockSpec((1, NB, 256), lambda i, s: (i, 0, 0))
    part = pl.BlockSpec((128, 256), lambda i, s: (0, i))
    shape = jax.ShapeDtypeStruct((128, NB), F32)
    return pl.pallas_call(
        update_kernel,
        grid_spec=pltpu.PrefetchScalarGridSpec(
            num_scalar_prefetch=1,
            grid=(4,),
            in_specs=[whole] * 8 + [band] * 2,
            out_specs=[part] * 4 + [pl.BlockSpec((128, NB), lambda i, s: (0, 0))],
            scratch_shapes=[pltpu.VMEM((512, NB), BF16)] * 2,
        ),
        out_shape=[shape] * 5,
        compiler_params=params(32),
        name="update",
    )(info, *own, *other, top, low)


def mid_kernel(got, out):
    level1 = [got[j, NB : NB + 8, :].T for j in range(NX)]
    level2 = [0.5 * got[j, NB + 8 : NB + 16, :].T for j in range(NX)]
    for i in range(NB // 128):
        at = slice(128 * i, 128 * i + 128)
        a, b, c, d = [got[j, at, :] for j in range(NX)]
        first = [a + c, b + d, a - c, b - d]
        first = [level1[j][:, i : i + 1] * first[j] for j in range(NX)]
        a, b, c, d = first
        second = [a + b, a - b, c + d, c - d]
        for j in range(NX):
            out[j, at, :] = level2[j][:, i : i + 1] * second[j]


def mid(got):
    return pl.pallas_call(
        mid_kernel,
        out_shape=jax.ShapeDtypeStruct((NX, NB, 128), F32),
        compiler_params=params(24),
        name="mid",
    )(got)


def last_kernel(info, moved, mine, *refs):
    parts, out = refs[:4], refs[4]
    start, x, z, core, y = [info[i] for i in range(5)]
    index = pl.program_id(0) * (NX * NZ * NC) + (x * NZ + z) * NC + core

    @pl.when(index < start)
    def _():
        out[...] = moved[...]

    @pl.when(index == start)
    def _():
        out[0] = mine[...].T

    @pl.when(index > start)
    def _():
        for s in range(NY):
            at = pl.ds(pl.multiple_of(256 * ((y + s) % NY), 256), 256)
            out[0, at, :] = moved[0, at, :] - parts[s][...].T


def last(info, moved, mine, parts):
    block = pl.BlockSpec((1, NB, 128), lambda i, s: (i, 0, 0))
    return pl.pallas_call(
        last_kernel,
        grid_spec=pltpu.PrefetchScalarGridSpec(
            num_scalar_prefetch=1,
            grid=(4,),
            in_specs=[block, pl.BlockSpec((128, NB), lambda i, s: (0, 0))]
            + [pl.BlockSpec((128, 256), lambda i, s: (0, i))] * 4,
            out_specs=block,
        ),
        out_shape=jax.ShapeDtypeStruct((4, NB, 128), F32),
        compiler_params=params(24),
        name="last",
    )(info, moved, mine, *parts)


def per_device(right_sides, butterfly_diagonals, band_rows, diag_inverse, band_block):
    place = lax.axis_index("rows")
    y = lax.axis_index("rhs")
    x, z, core = place // (NZ * NC), place // NC % NZ, place % NC
    start = band_block[0]
    info = jnp.stack([start, x, z, core, y]).astype(jnp.int32)
    z0 = start % (NX * NZ * NC) // NC % NZ
    core0 = start % NC

    message = prep(info, right_sides, butterfly_diagonals)
    got = exchange_x(message)
    packed = jnp.concatenate(
        [right_sides, butterfly_diagonals.transpose(1, 0, 2).reshape(4, 16, 128)], axis=1
    )
    packed = lax.optimization_barrier((packed, message))[0]
    mixed = exchange_x(packed)
    top, low = split_band(band_rows)

    piece = solve(info, got, diag_inverse)
    halves = piece.reshape(NC, HALF, NB)
    from_other = other_core(lax.dynamic_index_in_dim(halves, 1 - core, 0, keepdims=False))
    half = jnp.where(core == core0, lax.dynamic_index_in_dim(halves, core, 0, keepdims=False), from_other)

    ahead = (z - z0) % NZ
    up, down = shift_z(half, 1), shift_z(half, -1)
    half = jnp.where(ahead == 1, up, jnp.where(ahead == NZ - 1, down, half))
    up, down = shift_z(half, 3), shift_z(half, -3)
    half = jnp.where(
        (ahead >= 2) & (ahead <= 4), up, jnp.where((ahead == 5) | (ahead == 6), down, half)
    )

    line = jnp.concatenate([half] + [shift_y(half, s) for s in range(1, NY)], axis=0)
    own = [line] + [shift_x(line, t) for t in range(1, NX)]
    other = [other_core(v) for v in own]

    parts = update(info, own, other, top, low)
    mine = parts[4]
    parts = [parts[0]] + [shift_y(parts[s], -s) for s in range(1, NY)]
    moved = exchange_x(mid(mixed))
    return last(info, moved, mine, parts)


def solution(mesh):
    return jax.shard_map(
        per_device,
        mesh=mesh,
        in_specs=(
            P(None, "rows", "rhs"),
            P(None, None, "rows"),
            P(None, None, ("rows", "rhs")),
            P(),
            P(),
        ),
        out_specs=P(None, "rows", "rhs"),
        check_vma=False,
    )
```

time: 387 us -> 150 us (0.39)
  waiting for transfers between devices: 332 us -> 45.3 us
  starting transfers between devices: 10.4 us -> 60.2 us
  Pallas kernels: 0 us -> 27.8 us
  between operations: 14.2 us -> 0.87 us
  matrix products: 12.8 us -> 0 us
  other arithmetic: 8.5 us -> 1.56 us
  local copies, waits for them, and re-layouts: 8.57 us -> 13.7 us
    psum x1 -> x0, waiting for transfers between devices: 184 us -> none  [broadcast(): return lax.psum(jnp.where(mine, array, jnp.zeros_like(array)), axis)]
    ppermute x2 -> x18, waiting for transfers between devices: 87.4 us -> 30.4 us  [the longest x6 26 us: shift_y(): return lax.ppermute(v, 'rhs', [(i, (i + s) % NY) for i in range(NY)])]
    ppermute x2 -> x18, starting transfers between devices: 5.73 us -> 48.1 us  [the longest x5 16.6 us: other_core(): return lax.ppermute(v, 'rows', row_perm(lambda x, z, c: (x, z, 1 - c)))]
    all_gather x1 -> x0, waiting for transfers between devices: 34.6 us -> none  [per_device(): all_solved = lax.all_gather(solved, 'rhs', axis=1, tiled=True)]
    pallas_call x0 -> x6, Pallas kernels: none -> 27.8 us  [the longest x1 13 us: split_band(): pl.pallas_call(band_kernel, grid=(4,), in_specs=[pl.BlockSpec((256, 4, 25...]
    dot_general x2 -> x0, matrix products: 12.8 us -> none  [the longest x1 9.57 us: per_device(): jnp.einsum('bck,bn->ckn', band_rows, all_solved, precision=lax.Precision....]
    unnamed x8 -> x26, local copies, waits for them, and re-layouts: 2.08 us -> 13.6 us
    all_to_all x1 -> x3, waiting for transfers between devices: 25.6 us -> 14.9 us  [exchange_x(): lax.all_to_all(v, 'rows', 0, 0, axis_index_groups=X_GROUPS, tiled=True)]
  transfers between devices with their start and end apart: 5 -> 21, of which waited for: 5 -> 9; matrix products, arithmetic and copies ran while one was open for 0% -> 1% of each run, Pallas kernels for 0% -> 16%
where the time goes in v1:
time: 150 us; the launch traced here: 149 us
  starting transfers between devices  60.2 us (40%)
  waiting for transfers between devices  45.3 us (30%)
  Pallas kernels  27.8 us (19%)
  local copies, waits for them, and re-layouts  13.7 us (9%)
  other arithmetic  1.56 us (1%)
    ppermute x6, waiting for transfers between devices, shift_y(): return lax.ppermute(v, 'rhs', [(i, (i + s) % NY) for i in range(NY)])  26 us
    ppermute x5, starting transfers between devices, other_core(): return lax.ppermute(v, 'rows', row_perm(lambda x, z, c: (x, z, 1 - c)))  16.6 us
    all_to_all x3, waiting for transfers between devices, exchange_x(): lax.all_to_all(v, 'rows', 0, 0, axis_index_groups=X_GROUPS, tiled=True)  14.9 us
    ppermute x4, starting transfers between devices, shift_z(): return lax.ppermute(v, 'rows', row_perm(lambda x, z, c: (x, z + s, c)))  14.8 us
    unnamed x26, local copies, waits for them, and re-layouts  13.6 us
    pallas_call x1, Pallas kernels, split_band(): pl.pallas_call(band_kernel, grid=(4,), in_specs=[pl.BlockSpec((256, 4, 25...  13 us
    all_to_all x3, starting transfers between devices, exchange_x(): lax.all_to_all(v, 'rows', 0, 0, axis_index_groups=X_GROUPS, tiled=True)  12.1 us
    ppermute x6, starting transfers between devices, shift_y(): return lax.ppermute(v, 'rhs', [(i, (i + s) % NY) for i in range(NY)])  11.4 us
  transfers between devices with their start and end apart: 21, of which 9 were waited for; matrix products, arithmetic and copies ran while one was open for 1% of the time, Pallas kernels for 16%

profile of v1, /device:TPU:1, one launch (start us, length us, event | category | flops | bytes accessed | tf_op | source)
XLA Modules:
  0.0 149.4 jit_solution(6390191756140993696)
XLA Ops:
  0.7 0.1 stack.19.info
  0.8 1.6 %copy-done = f32[4,1024,128]{2,1,0:T(8,128)S(1)} copy-done((f32[4,1024,128]{2,1,0:T(8,128)S(1)}, f32[4,1024,128]{2,1,0:T(8,128)}, u32[]{:S(2)}) %copy-start) | copy-done | bytes 2097176
  2.4 0.8 copy-done.11
  3.1 1.6 %prep.1 = f32[4,40,1024]{2,1,0:T(8,128)} custom-call(s32[5]{0:T(128)S(1)} %stack.19.info, f32[4,1024,128]{2,1,0:T(8,128)S(1)} %copy-done, f32[2,4,1024]{2,1,0:T(4,128)S(1)} %copy-done.11), custom_call_target="tpu_custom_call" | custom-call | tf_op jit(solution)/shard_map/prep/pallas_call | solution.py:64
  4.7 4.8 %all-to-all-start.2 = ((f32[4,40,1024]{2,1,0:T(8,128)}), f32[4,40,1024]{2,1,0:T(8,128)S(1)}, u32[]{:S(2)}, u32[]{:S(2)}) async-start(f32[4,40,1024]{2,1,0:T(8,128)} %prep.1), calls=%async_computation.2 | async-start | bytes 1310720 | tf_op jit(solution)/shard_map/all_to_all | solution.py:46
  9.6 0.0 copy-done.12
  9.6 1.5 %pad_maximum_fusion = f32[4,1040,128]{2,1,0:T(8,128)} fusion(f32[4,16,128]{2,1,0:T(8,128)S(1)} %reshape.6, f32[4,1024,128]{2,1,0:T(8,128)S(1)} %copy-done.1), kind=kLoop, calls=%fused_computation | loop fusion | flops 532480 | bytes 4259840 | tf_op jit(solution)/shard_map/concatenate | solution.py:261
  11.1 7.2 %all-to-all-done.2.got = f32[4,40,1024]{2,1,0:T(8,128)S(1)} async-done(((f32[4,40,1024]{2,1,0:T(8,128)}), f32[4,40,1024]{2,1,0:T(8,128)S(1)}, u32[]{:S(2)}, u32[]{:S(2)}) %all-to-all-start.2) | async-done | bytes 655392 | tf_op jit(solution)/shard_map/all_to_all | solution.py:46
  18.3 3.6 %all-to-all-start = ((f32[4,1040,128]{2,1,0:T(8,128)}), f32[4,1040,128]{2,1,0:T(8,128)S(1)}, u32[]{:S(2)}, u32[]{:S(2)}) async-start(f32[4,1040,128]{2,1,0:T(8,128)} %pad_maximum_fusion), calls=%async_computation | async-start | bytes 4259840 | tf_op jit(solution)/shard_map/all_to_all | solution.py:46
  21.9 0.0 copy-start.3
  22.0 2.2 %copy-done.3 = f32[1024,1024]{1,0:T(8,128)S(1)} copy-done((f32[1024,1024]{1,0:T(8,128)S(1)}, f32[1024,1024]{1,0:T(8,128)}, u32[]{:S(2)}) %copy-start.3) | copy-done | bytes 4194328
  24.1 3.8 %solve.1 = f32[32,1024]{1,0:T(8,128)S(1)} custom-call(s32[5]{0:T(128)S(1)} %stack.19.info, f32[4,40,1024]{2,1,0:T(8,128)S(1)} %all-to-all-done.2.got, f32[1024,1024]{1,0:T(8,128)S(1)} %copy-done.3), custom_call_target="tpu_custom_call" | custom-call | tf_op jit(solution)/shard_map/solve/pallas_call | solution.py:97
  28.0 3.2 %collective-permute-start = (f32[16,1024]{1,0:T(8,128)S(1)}, f32[16,1024]{1,0:T(8,128)S(1)}, u32[]{:S(2)}, u32[]{:S(2)}) collective-permute-start(f32[16,1024]{1,0:T(8,128)S(1)} %dynamic-slice_bitcast_fusion), channel_id=1, source_target_pairs={{0,4},{4,0},{8,12},{12,8},{16,20},{20,16},{24,28},{28,24},{32,36},... | collective-permute-start | bytes 196616 | tf_op jit(solution)/shard_map/ppermute | solution.py:35
  31.1 0.9 collective-permute-done
  32.0 1.7 %collective-permute-start.1 = (f32[16,1024]{1,0:T(8,128)S(1)}, f32[16,1024]{1,0:T(8,128)S(1)}, u32[]{:S(2)}, u32[]{:S(2)}) collective-permute-start(f32[16,1024]{1,0:T(8,128)S(1)} %bitcast_select_fusion), channel_id=1, source_target_pairs={{0,8},{4,12},{8,16},{12,20},{16,24},{20,28},{24,32},{28,36},{32,40... | collective-permute-start | bytes 196616 | tf_op jit(solution)/shard_map/ppermute | solution.py:31
  33.8 4.0 %collective-permute-start.2 = (f32[16,1024]{1,0:T(8,128)S(1)}, f32[16,1024]{1,0:T(8,128)S(1)}, u32[]{:S(2)}, u32[]{:S(2)}) collective-permute-start(f32[16,1024]{1,0:T(8,128)S(1)} %bitcast_select_fusion), channel_id=1, source_target_pairs={{0,56},{4,60},{8,0},{12,4},{16,8},{20,12},{24,16},{28,20},{32,24},... | collective-permute-start | bytes 196616 | tf_op jit(solution)/shard_map/ppermute | solution.py:31
  37.8 7.8 %all-to-all-done.got = f32[4,1040,128]{2,1,0:T(8,128)S(1)} async-done(((f32[4,1040,128]{2,1,0:T(8,128)}), f32[4,1040,128]{2,1,0:T(8,128)S(1)}, u32[]{:S(2)}, u32[]{:S(2)}) %all-to-all-start) | async-done | bytes 2129952 | tf_op jit(solution)/shard_map/all_to_all | solution.py:46
  45.5 1.4 mid.1
  47.0 0.0 copy-start.2
  47.0 1.3 copy-done.2
  48.3 3.6 %all-to-all-start.1 = ((f32[4,1024,128]{2,1,0:T(8,128)}), f32[4,1024,128]{2,1,0:T(8,128)S(1)}, u32[]{:S(2)}, u32[]{:S(2)}) async-start(f32[4,1024,128]{2,1,0:T(8,128)} %copy-done.2), calls=%async_computation.1 | async-start | bytes 4194304 | tf_op jit(solution)/shard_map/all_to_all | solution.py:46
  51.9 0.0 collective-permute-done.1
  51.9 0.0 collective-permute-done.2
  52.0 6.8 %collective-permute-start.3 = (f32[16,1024]{1,0:T(8,128)S(1)}, f32[16,1024]{1,0:T(8,128)S(1)}, u32[]{:S(2)}, u32[]{:S(2)}) collective-permute-start(f32[16,1024]{1,0:T(8,128)S(1)} %select_select_fusion.1), channel_id=1, source_target_pairs={{0,24},{4,28},{8,32},{12,36},{16,40},{20,44},{24,48},{28,52},{32,5... | collective-permute-start | bytes 196616 | tf_op jit(solution)/shard_map/ppermute | solution.py:31
  58.8 2.2 %collective-permute-start.4 = (f32[16,1024]{1,0:T(8,128)S(1)}, f32[16,1024]{1,0:T(8,128)S(1)}, u32[]{:S(2)}, u32[]{:S(2)}) collective-permute-start(f32[16,1024]{1,0:T(8,128)S(1)} %select_select_fusion.1), channel_id=1, source_target_pairs={{0,40},{4,44},{8,48},{12,52},{16,56},{20,60},{24,0},{28,4},{32,8},... | collective-permute-start | bytes 196616 | tf_op jit(solution)/shard_map/ppermute | solution.py:31
  61.0 1.8 %collective-permute-done.3 = f32[16,1024]{1,0:T(8,128)S(1)} collective-permute-done((f32[16,1024]{1,0:T(8,128)S(1)}, f32[16,1024]{1,0:T(8,128)S(1)}, u32[]{:S(2)}, u32[]{:S(2)}) %collective-permute-start.3) | collective-permute-done | bytes 65568 | tf_op jit(solution)/shard_map/ppermute | solution.py:31
  62.8 1.7 %collective-permute-done.4 = f32[16,1024]{1,0:T(8,128)S(1)} collective-permute-done((f32[16,1024]{1,0:T(8,128)S(1)}, f32[16,1024]{1,0:T(8,128)S(1)}, u32[]{:S(2)}, u32[]{:S(2)}) %collective-permute-start.4) | collective-permute-done | bytes 65568 | tf_op jit(solution)/shard_map/ppermute | solution.py:31
  64.5 1.4 collective-permute-start.5
  65.8 2.6 %collective-permute-start.6 = (f32[16,1024]{1,0:T(8,128)S(1)}, f32[16,1024]{1,0:T(8,128)S(1)}, u32[]{:S(2)}, u32[]{:S(2)}) collective-permute-start(f32[16,1024]{1,0:T(8,128)S(1)} %select_select_fusion), channel_id=1, source_target_pairs={{0,2},{1,3},{2,0},{3,1},{4,6},{5,7},{6,4},{7,5},{8,10},{9,11},{10,... | collective-permute-start | bytes 196616 | tf_op jit(solution)/shard_map/ppermute | solution.py:39
  68.5 1.1 collective-permute-start.7
  69.5 0.0 collective-permute-done.5
  69.5 1.3 collective-permute-done.6
  70.8 0.8 collective-permute-done.7
  71.6 1.8 %collective-permute-start.8 = (f32[64,1024]{1,0:T(8,128)S(1)}, f32[64,1024]{1,0:T(8,128)S(1)}, u32[]{:S(2)}, u32[]{:S(2)}) collective-permute-start(f32[64,1024]{1,0:T(8,128)S(1)} %pad_maximum_fusion.1.refs_0_), channel_id=1, source_target_pairs={{0,64},{4,68},{8,72},{12,76},{16,80},{20,84},{24,88},{28,92},{32,9... | collective-permute-start | bytes 786440 | tf_op jit(solution)/shard_map/ppermute | solution.py:27
  73.4 2.4 %collective-permute-start.9 = (f32[64,1024]{1,0:T(8,128)S(1)}, f32[64,1024]{1,0:T(8,128)S(1)}, u32[]{:S(2)}, u32[]{:S(2)}) collective-permute-start(f32[64,1024]{1,0:T(8,128)S(1)} %pad_maximum_fusion.1.refs_0_), channel_id=1, source_target_pairs={{0,128},{4,132},{8,136},{12,140},{16,144},{20,148},{24,152},{28,15... | collective-permute-start | bytes 786440 | tf_op jit(solution)/shard_map/ppermute | solution.py:27
  75.8 1.2 collective-permute-start.10
  76.9 7.1 %collective-permute-start.11 = (f32[64,1024]{1,0:T(8,128)S(1)}, f32[64,1024]{1,0:T(8,128)S(1)}, u32[]{:S(2)}, u32[]{:S(2)}) collective-permute-start(f32[64,1024]{1,0:T(8,128)S(1)} %pad_maximum_fusion.1.refs_0_), channel_id=1, source_target_pairs={{0,4},{4,0},{8,12},{12,8},{16,20},{20,16},{24,28},{28,24},{32,36},... | collective-permute-start | bytes 786440 | tf_op jit(solution)/shard_map/ppermute | solution.py:35
  84.1 0.0 collective-permute-done.8.refs_1_
  84.1 3.5 %collective-permute-start.12 = (f32[64,1024]{1,0:T(8,128)S(1)}, f32[64,1024]{1,0:T(8,128)S(1)}, u32[]{:S(2)}, u32[]{:S(2)}) collective-permute-start(f32[64,1024]{1,0:T(8,128)S(1)} %collective-permute-done.8.refs_1_), channel_id=1, source_target_pairs={{0,4},{4,0},{8,12},{12,8},{16,20},{20,16},{24,28},{28,24},{32,36},... | collective-permute-start | bytes 786440 | tf_op jit(solution)/shard_map/ppermute | solution.py:35
  87.6 0.0 collective-permute-done.9.refs_2_
  87.6 2.8 %collective-permute-start.13 = (f32[64,1024]{1,0:T(8,128)S(1)}, f32[64,1024]{1,0:T(8,128)S(1)}, u32[]{:S(2)}, u32[]{:S(2)}) collective-permute-start(f32[64,1024]{1,0:T(8,128)S(1)} %collective-permute-done.9.refs_2_), channel_id=1, source_target_pairs={{0,4},{4,0},{8,12},{12,8},{16,20},{20,16},{24,28},{28,24},{32,36},... | collective-permute-start | bytes 786440 | tf_op jit(solution)/shard_map/ppermute | solution.py:35
  90.4 0.0 collective-permute-done.10.refs_3_
  90.4 0.0 collective-permute-start.14
  90.4 2.2 %copy-done.4 = f32[1024,4,256]{2,1,0:T(4,128)S(1)} copy-done((f32[1024,4,256]{2,1,0:T(4,128)S(1)}, f32[1024,4,256]{2,1,0:T(4,128)}, u32[]{:S(2)}) %copy-start.4) | copy-done | bytes 4194328
  92.6 13.0 %split_band.1 = (bf16[4,1024,256]{2,1,0:T(8,128)(2,1)S(1)}, bf16[4,1024,256]{2,1,0:T(8,128)(2,1)S(1)}) custom-call(f32[1024,4,256]{2,1,0:T(4,128)S(1)} %copy-done.4), custom_call_target="tpu_custom_call" | custom-call | tf_op jit(solution)/shard_map/split_band/pallas_call | solution.py:129
  105.6 0.0 collective-permute-done.11.refs_4_
  105.6 0.0 collective-permute-done.12.refs_5_
  105.6 0.0 collective-permute-done.13.refs_6_
  105.6 0.0 collective-permute-done.14.refs_7_
  105.6 5.2 %update.1 = (f32[128,1024]{1,0:T(8,128)S(1)}, f32[128,1024]{1,0:T(8,128)S(1)}, f32[128,1024]{1,0:T(8,128)S(1)}, f32[128,1024]{1,0:T(8,128)S(1)}, f32[128,1024]{1,0:T(8,128)S(1)}) custom-call(s32[5]{0:T(128)S(1)} %stack.19.info, f32[64,1024]{1,0:T(8,128)S(1)} %pad_maximum_fusion.1.refs_0_, f32[64,1024]{1,0:T(8,128)S(1)} %collective-permute-done.8.refs_1_, ...), custom_call_target="tpu_custom_call" | custom-call | tf_op jit(solution)/shard_map/update/pallas_call | solution.py:175
  110.8 5.3 %collective-permute-start.15 = (f32[128,1024]{1,0:T(8,128)S(1)}, f32[128,1024]{1,0:T(8,128)S(1)}, u32[]{:S(2)}, u32[]{:S(2)}) collective-permute-start(f32[128,1024]{1,0:T(8,128)S(1)} %get-tuple-element.18), channel_id=1, source_target_pairs={{0,3},{1,0},{2,1},{3,2},{4,7},{5,4},{6,5},{7,6},{8,11},{9,8},{10,9... | collective-permute-start | bytes 1572872 | tf_op jit(solution)/shard_map/ppermute | solution.py:39
  116.1 0.3 collective-permute-start.16
  116.4 0.7 collective-permute-start.17
  117.1 20.8 %collective-permute-done.15.refs_1_ = f32[128,1024]{1,0:T(8,128)S(1)} collective-permute-done((f32[128,1024]{1,0:T(8,128)S(1)}, f32[128,1024]{1,0:T(8,128)S(1)}, u32[]{:S(2)}, u32[]{:S(2)}) %collective-permute-start.15) | collective-permute-done | bytes 524320 | tf_op jit(solution)/shard_map/ppermute | solution.py:39
  138.0 0.8 copy-done.5
  138.8 0.0 collective-permute-done.16.refs_2_
  138.8 0.8 copy-done.7
  139.6 3.1 %collective-permute-done.17.refs_3_ = f32[128,1024]{1,0:T(8,128)S(1)} collective-permute-done((f32[128,1024]{1,0:T(8,128)S(1)}, f32[128,1024]{1,0:T(8,128)S(1)}, u32[]{:S(2)}, u32[]{:S(2)}) %collective-permute-start.17) | collective-permute-done | bytes 524320 | tf_op jit(solution)/shard_map/ppermute | solution.py:39
  142.7 0.8 copy-done.9
  143.5 0.0 all-to-all-done.1.moved
  143.5 1.0 copy-done.6
  144.5 1.0 copy-done.8
  145.6 1.0 copy-done.10
  146.6 2.8 %last.1 = f32[4,1024,128]{2,1,0:T(8,128)} custom-call(s32[5]{0:T(128)S(1)} %stack.19.info, f32[4,1024,128]{2,1,0:T(8,128)S(1)} %all-to-all-done.1.moved, f32[128,1024]{1,0:T(8,128)S(1)} %get-tuple-element.16.mine, f32[128,1024]{1,0:T(8,128)S(1)} %get-tuple-element.17.refs_0_, f32[128,1024]{1,0:T(8,128)S(1)} %copy-done.6, f32[128,1024]{1,0:T(8,128)S(1)} %copy-done.8, ...), custom_call_target="tpu_custom_call" | custom-call | tf_op jit(solution)/shard_map/last/pallas_call | solution.py:235
  (19 shorter events, 0.1 us)
Async XLA Ops:
  0.0 9.6 %copy-start.12 = (f32[2,4,1024]{2,1,0:T(4,128)S(1)}, f32[2,4,1024]{2,1,0:T(4,128)}, u32[]{:S(2)}) copy-start(f32[2,4,1024]{2,1,0:T(4,128)} %diag.1) | copy-start | bytes 98308
  0.8 1.6 %copy-start = (f32[4,1024,128]{2,1,0:T(8,128)S(1)}, f32[4,1024,128]{2,1,0:T(8,128)}, u32[]{:S(2)}) copy-start(f32[4,1024,128]{2,1,0:T(8,128)} %slab.1) | copy-start | bytes 6291460
  2.4 0.8 copy-start.11
  3.1 6.5 %copy-start.1 = (f32[4,1024,128]{2,1,0:T(8,128)S(1)}, f32[4,1024,128]{2,1,0:T(8,128)}, u32[]{:S(2)}) copy-start(f32[4,1024,128]{2,1,0:T(8,128)} %slab.1) | copy-start | bytes 6291460
  4.7 13.6 %all-to-all-start.2 = ((f32[4,40,1024]{2,1,0:T(8,128)}), f32[4,40,1024]{2,1,0:T(8,128)S(1)}, u32[]{:S(2)}, u32[]{:S(2)}) async-start(f32[4,40,1024]{2,1,0:T(8,128)} %prep.1), calls=%async_computation.2 | async-start | bytes 1310720 | tf_op jit(solution)/shard_map/all_to_all | solution.py:46
  18.3 27.2 %all-to-all-start = ((f32[4,1040,128]{2,1,0:T(8,128)}), f32[4,1040,128]{2,1,0:T(8,128)S(1)}, u32[]{:S(2)}, u32[]{:S(2)}) async-start(f32[4,1040,128]{2,1,0:T(8,128)} %pad_maximum_fusion), calls=%async_computation | async-start | bytes 4259840 | tf_op jit(solution)/shard_map/all_to_all | solution.py:46
  21.9 2.2 %copy-start.3 = (f32[1024,1024]{1,0:T(8,128)S(1)}, f32[1024,1024]{1,0:T(8,128)}, u32[]{:S(2)}) copy-start(f32[1024,1024]{1,0:T(8,128)} %inverse.1) | copy-start | bytes 12582916
  28.0 4.1 %collective-permute-start = (f32[16,1024]{1,0:T(8,128)S(1)}, f32[16,1024]{1,0:T(8,128)S(1)}, u32[]{:S(2)}, u32[]{:S(2)}) collective-permute-start(f32[16,1024]{1,0:T(8,128)S(1)} %dynamic-slice_bitcast_fusion), channel_id=1, source_target_pairs={{0,4},{4,0},{8,12},{12,8},{16,20},{20,16},{24,28},{28,24},{32,36},... | collective-permute-start | bytes 196616 | tf_op jit(solution)/shard_map/ppermute | solution.py:35
  32.0 19.9 %collective-permute-start.1 = (f32[16,1024]{1,0:T(8,128)S(1)}, f32[16,1024]{1,0:T(8,128)S(1)}, u32[]{:S(2)}, u32[]{:S(2)}) collective-permute-start(f32[16,1024]{1,0:T(8,128)S(1)} %bitcast_select_fusion), channel_id=1, source_target_pairs={{0,8},{4,12},{8,16},{12,20},{16,24},{20,28},{24,32},{28,36},{32,40... | collective-permute-start | bytes 196616 | tf_op jit(solution)/shard_map/ppermute | solution.py:31
  33.8 18.2 %collective-permute-start.2 = (f32[16,1024]{1,0:T(8,128)S(1)}, f32[16,1024]{1,0:T(8,128)S(1)}, u32[]{:S(2)}, u32[]{:S(2)}) collective-permute-start(f32[16,1024]{1,0:T(8,128)S(1)} %bitcast_select_fusion), channel_id=1, source_target_pairs={{0,56},{4,60},{8,0},{12,4},{16,8},{20,12},{24,16},{28,20},{32,24},... | collective-permute-start | bytes 196616 | tf_op jit(solution)/shard_map/ppermute | solution.py:31
  47.0 1.3 copy-start.2
  48.3 95.2 %all-to-all-start.1 = ((f32[4,1024,128]{2,1,0:T(8,128)}), f32[4,1024,128]{2,1,0:T(8,128)S(1)}, u32[]{:S(2)}, u32[]{:S(2)}) async-start(f32[4,1024,128]{2,1,0:T(8,128)} %copy-done.2), calls=%async_computation.1 | async-start | bytes 4194304 | tf_op jit(solution)/shard_map/all_to_all | solution.py:46
  52.0 10.8 %collective-permute-start.3 = (f32[16,1024]{1,0:T(8,128)S(1)}, f32[16,1024]{1,0:T(8,128)S(1)}, u32[]{:S(2)}, u32[]{:S(2)}) collective-permute-start(f32[16,1024]{1,0:T(8,128)S(1)} %select_select_fusion.1), channel_id=1, source_target_pairs={{0,24},{4,28},{8,32},{12,36},{16,40},{20,44},{24,48},{28,52},{32,5... | collective-permute-start | bytes 196616 | tf_op jit(solution)/shard_map/ppermute | solution.py:31
  58.8 5.7 %collective-permute-start.4 = (f32[16,1024]{1,0:T(8,128)S(1)}, f32[16,1024]{1,0:T(8,128)S(1)}, u32[]{:S(2)}, u32[]{:S(2)}) collective-permute-start(f32[16,1024]{1,0:T(8,128)S(1)} %select_select_fusion.1), channel_id=1, source_target_pairs={{0,40},{4,44},{8,48},{12,52},{16,56},{20,60},{24,0},{28,4},{32,8},... | collective-permute-start | bytes 196616 | tf_op jit(solution)/shard_map/ppermute | solution.py:31
  64.5 5.1 %collective-permute-start.5 = (f32[16,1024]{1,0:T(8,128)S(1)}, f32[16,1024]{1,0:T(8,128)S(1)}, u32[]{:S(2)}, u32[]{:S(2)}) collective-permute-start(f32[16,1024]{1,0:T(8,128)S(1)} %select_select_fusion), channel_id=1, source_target_pairs={{0,1},{1,2},{2,3},{3,0},{4,5},{5,6},{6,7},{7,4},{8,9},{9,10},{10,1... | collective-permute-start | bytes 196616 | tf_op jit(solution)/shard_map/ppermute | solution.py:39
  65.8 5.0 %collective-permute-start.6 = (f32[16,1024]{1,0:T(8,128)S(1)}, f32[16,1024]{1,0:T(8,128)S(1)}, u32[]{:S(2)}, u32[]{:S(2)}) collective-permute-start(f32[16,1024]{1,0:T(8,128)S(1)} %select_select_fusion), channel_id=1, source_target_pairs={{0,2},{1,3},{2,0},{3,1},{4,6},{5,7},{6,4},{7,5},{8,10},{9,11},{10,... | collective-permute-start | bytes 196616 | tf_op jit(solution)/shard_map/ppermute | solution.py:39
  68.5 3.1 %collective-permute-start.7 = (f32[16,1024]{1,0:T(8,128)S(1)}, f32[16,1024]{1,0:T(8,128)S(1)}, u32[]{:S(2)}, u32[]{:S(2)}) collective-permute-start(f32[16,1024]{1,0:T(8,128)S(1)} %select_select_fusion), channel_id=1, source_target_pairs={{0,3},{1,0},{2,1},{3,2},{4,7},{5,4},{6,5},{7,6},{8,11},{9,8},{10,9... | collective-permute-start | bytes 196616 | tf_op jit(solution)/shard_map/ppermute | solution.py:39
  71.6 12.5 %collective-permute-start.8 = (f32[64,1024]{1,0:T(8,128)S(1)}, f32[64,1024]{1,0:T(8,128)S(1)}, u32[]{:S(2)}, u32[]{:S(2)}) collective-permute-start(f32[64,1024]{1,0:T(8,128)S(1)} %pad_maximum_fusion.1.refs_0_), channel_id=1, source_target_pairs={{0,64},{4,68},{8,72},{12,76},{16,80},{20,84},{24,88},{28,92},{32,9... | collective-permute-start | bytes 786440 | tf_op jit(solution)/shard_map/ppermute | solution.py:27
  73.4 14.2 %collective-permute-start.9 = (f32[64,1024]{1,0:T(8,128)S(1)}, f32[64,1024]{1,0:T(8,128)S(1)}, u32[]{:S(2)}, u32[]{:S(2)}) collective-permute-start(f32[64,1024]{1,0:T(8,128)S(1)} %pad_maximum_fusion.1.refs_0_), channel_id=1, source_target_pairs={{0,128},{4,132},{8,136},{12,140},{16,144},{20,148},{24,152},{28,15... | collective-permute-start | bytes 786440 | tf_op jit(solution)/shard_map/ppermute | solution.py:27
  75.8 14.6 %collective-permute-start.10 = (f32[64,1024]{1,0:T(8,128)S(1)}, f32[64,1024]{1,0:T(8,128)S(1)}, u32[]{:S(2)}, u32[]{:S(2)}) collective-permute-start(f32[64,1024]{1,0:T(8,128)S(1)} %pad_maximum_fusion.1.refs_0_), channel_id=1, source_target_pairs={{0,192},{4,196},{8,200},{12,204},{16,208},{20,212},{24,216},{28,22... | collective-permute-start | bytes 786440 | tf_op jit(solution)/shard_map/ppermute | solution.py:27
  76.9 28.6 %collective-permute-start.11 = (f32[64,1024]{1,0:T(8,128)S(1)}, f32[64,1024]{1,0:T(8,128)S(1)}, u32[]{:S(2)}, u32[]{:S(2)}) collective-permute-start(f32[64,1024]{1,0:T(8,128)S(1)} %pad_maximum_fusion.1.refs_0_), channel_id=1, source_target_pairs={{0,4},{4,0},{8,12},{12,8},{16,20},{20,16},{24,28},{28,24},{32,36},... | collective-permute-start | bytes 786440 | tf_op jit(solution)/shard_map/ppermute | solution.py:35
  84.1 21.5 %collective-permute-start.12 = (f32[64,1024]{1,0:T(8,128)S(1)}, f32[64,1024]{1,0:T(8,128)S(1)}, u32[]{:S(2)}, u32[]{:S(2)}) collective-permute-start(f32[64,1024]{1,0:T(8,128)S(1)} %collective-permute-done.8.refs_1_), channel_id=1, source_target_pairs={{0,4},{4,0},{8,12},{12,8},{16,20},{20,16},{24,28},{28,24},{32,36},... | collective-permute-start | bytes 786440 | tf_op jit(solution)/shard_map/ppermute | solution.py:35
  87.6 18.0 %collective-permute-start.13 = (f32[64,1024]{1,0:T(8,128)S(1)}, f32[64,1024]{1,0:T(8,128)S(1)}, u32[]{:S(2)}, u32[]{:S(2)}) collective-permute-start(f32[64,1024]{1,0:T(8,128)S(1)} %collective-permute-done.9.refs_2_), channel_id=1, source_target_pairs={{0,4},{4,0},{8,12},{12,8},{16,20},{20,16},{24,28},{28,24},{32,36},... | collective-permute-start | bytes 786440 | tf_op jit(solution)/shard_map/ppermute | solution.py:35
  90.4 15.2 %collective-permute-start.14 = (f32[64,1024]{1,0:T(8,128)S(1)}, f32[64,1024]{1,0:T(8,128)S(1)}, u32[]{:S(2)}, u32[]{:S(2)}) collective-permute-start(f32[64,1024]{1,0:T(8,128)S(1)} %collective-permute-done.10.refs_3_), channel_id=1, source_target_pairs={{0,4},{4,0},{8,12},{12,8},{16,20},{20,16},{24,28},{28,24},{32,36},... | collective-permute-start | bytes 786440 | tf_op jit(solution)/shard_map/ppermute | solution.py:35
  90.4 2.2 %copy-start.4 = (f32[1024,4,256]{2,1,0:T(4,128)S(1)}, f32[1024,4,256]{2,1,0:T(4,128)}, u32[]{:S(2)}) copy-start(f32[1024,4,256]{2,1,0:T(4,128)} %rows.1) | copy-start | bytes 12582916
  110.8 27.2 %collective-permute-start.15 = (f32[128,1024]{1,0:T(8,128)S(1)}, f32[128,1024]{1,0:T(8,128)S(1)}, u32[]{:S(2)}, u32[]{:S(2)}) collective-permute-start(f32[128,1024]{1,0:T(8,128)S(1)} %get-tuple-element.18), channel_id=1, source_target_pairs={{0,3},{1,0},{2,1},{3,2},{4,7},{5,4},{6,5},{7,6},{8,11},{9,8},{10,9... | collective-permute-start | bytes 1572872 | tf_op jit(solution)/shard_map/ppermute | solution.py:39
  116.1 22.7 %collective-permute-start.16 = (f32[128,1024]{1,0:T(8,128)S(1)}, f32[128,1024]{1,0:T(8,128)S(1)}, u32[]{:S(2)}, u32[]{:S(2)}) collective-permute-start(f32[128,1024]{1,0:T(8,128)S(1)} %get-tuple-element.19), channel_id=1, source_target_pairs={{0,2},{1,3},{2,0},{3,1},{4,6},{5,7},{6,4},{7,5},{8,10},{9,11},{10,... | collective-permute-start | bytes 1572872 | tf_op jit(solution)/shard_map/ppermute | solution.py:39
  116.4 26.2 %collective-permute-start.17 = (f32[128,1024]{1,0:T(8,128)S(1)}, f32[128,1024]{1,0:T(8,128)S(1)}, u32[]{:S(2)}, u32[]{:S(2)}) collective-permute-start(f32[128,1024]{1,0:T(8,128)S(1)} %get-tuple-element.20), channel_id=1, source_target_pairs={{0,1},{1,2},{2,3},{3,0},{4,5},{5,6},{6,7},{7,4},{8,9},{9,10},{10,1... | collective-permute-start | bytes 1572872 | tf_op jit(solution)/shard_map/ppermute | solution.py:39
  138.0 0.8 copy-start.5
  138.8 0.8 copy-start.7
  142.7 0.8 copy-start.9
  143.5 1.0 copy-start.6
  144.5 1.0 copy-start.8
  145.6 1.0 copy-start.10

commit v2 on v0

v2 whole, which is shorter than its diff:
```python
import functools
import jax
import jax.numpy as jnp
from jax import lax
from jax.experimental import pallas as pl
from jax.experimental.pallas import tpu as pltpu
from jax.sharding import PartitionSpec as P

NX, NZ, NC, NY = 4, 8, 2, 4
NB = 1024
HALF = 16
F32 = jnp.float32
BF16 = jnp.bfloat16


def row_perm(move):
    pairs = []
    for x in range(NX):
        for z in range(NZ):
            for c in range(NC):
                a, b, d = move(x, z, c)
                pairs.append(((x * NZ + z) * NC + c, ((a % NX) * NZ + b % NZ) * NC + d))
    return pairs


def flip_x(v, m):
    return lax.ppermute(v, "rows", row_perm(lambda x, z, c: (x ^ m, z, c))) if m else v


def flip_z(v, m):
    return lax.ppermute(v, "rows", row_perm(lambda x, z, c: (x, z ^ m, c)))


def flip_y(v, m):
    return lax.ppermute(v, "rhs", [(i, i ^ m) for i in range(NY)]) if m else v


X_GROUPS = [[(x * NZ + z) * NC + c for x in range(NX)] for z in range(NZ) for c in range(NC)]


def exchange_x(v):
    return lax.all_to_all(v, "rows", 0, 0, axis_index_groups=X_GROUPS, tiled=True)


def other_core(v):
    return lax.ppermute(v, "rows", row_perm(lambda x, z, c: (x, z, 1 - c)))


def far(*values):
    return [pltpu.with_memory_space_constraint(v, pltpu.HBM) for v in values]


def params(mib):
    return pltpu.CompilerParams(vmem_limit_bytes=mib << 20)


ANY = pl.BlockSpec(memory_space=pl.ANY)


def whole(*shape):
    return pl.BlockSpec(shape, lambda i, s: (0,) * len(shape))


def call(body, name, grid, info, args, in_specs, out_specs, out_shape, mib, scratch=(), hint=0):
    cost = pl.CostEstimate(flops=hint, bytes_accessed=1 << 20, transcendentals=0)
    return pl.pallas_call(
        body,
        grid_spec=pltpu.PrefetchScalarGridSpec(
            num_scalar_prefetch=1,
            grid=(grid,),
            in_specs=in_specs,
            out_specs=out_specs,
            scratch_shapes=list(scratch),
        ),
        out_shape=out_shape,
        compiler_params=params(mib),
        cost_estimate=cost if hint else None,
        name=name,
    )(info, *args)


def prep_kernel(info, slab, diag, *refs):
    outs, flipped = refs[:NX], refs[NX]
    cycle, x = info[0] // (NX * NZ * NC), info[1]
    flipped[...] = slab[0].T
    for s in range(NX):
        to = x ^ s
        outs[s][:32, :] = flipped[pl.ds(pl.multiple_of(32 * to, 32), 32), :]
        for level in range(2):
            outs[s][32 + level : 33 + level, :] = diag[level, pl.ds(cycle, 1), :]
            outs[s][34 + level : 35 + level, :] = diag[level, pl.ds(to, 1), :]
        outs[s][36:40, :] = jnp.zeros((4, 256), F32)


def prep(info, right_sides, diag):
    return call(
        prep_kernel,
        "prep",
        4,
        info,
        far(right_sides, diag),
        [
            pl.BlockSpec((1, 256, 128), lambda i, s: (s[0] // (NX * NZ * NC), i, 0)),
            pl.BlockSpec((2, 4, 256), lambda i, s: (0, 0, i)),
        ],
        [pl.BlockSpec((40, 256), lambda i, s: (0, i))] * NX,
        [jax.ShapeDtypeStruct((40, NB), F32)] * NX,
        12,
        [pltpu.VMEM((128, 256), F32)],
    )


def split(v):
    top = v.astype(BF16)
    return top, (v - top.astype(F32)).astype(BF16)


TOKEN = jax.ShapeDtypeStruct((8, 128), F32)


def split_band_kernel(info, rows, token, top, low, mark):
    mark[...] = jnp.zeros((8, 128), F32)
    for c in range(4):
        for half in range(2):
            a, b = split(rows[pl.ds(4 * half + c, 256, stride=8), :])
            top[c, :, 128 * half : 128 * half + 128] = a
            low[c, :, 128 * half : 128 * half + 128] = b


def split_band(info, band_rows, token):
    view = band_rows.reshape(NB, 4, 2, 128).transpose(0, 2, 1, 3).reshape(8 * NB, 128)
    spec = pl.BlockSpec((4, 256, 256), lambda i, s: (0, i, 0))
    return call(
        split_band_kernel,
        "split_band",
        4,
        info,
        (view, token),
        [pl.BlockSpec((2048, 128), lambda i, s: (i, 0)), ANY],
        [spec, spec, whole(8, 128)],
        [pltpu.HBM((4, NB, 256), BF16)] * 2 + [TOKEN],
        12,
    )


def product(a, b):
    return jnp.dot(a, b, preferred_element_type=F32)


def solve_kernel(info, *refs):
    pieces, inverse = refs[:4], refs[4]
    keep, send, got, top, low, full = refs[6:]
    step = pl.program_id(0)
    x, core = info[1], info[3]

    @pl.when(step == 0)
    def _():
        for s in range(NX):
            got[x ^ s] = pieces[s][...]
        x0 = info[0] % (NX * NZ * NC) // (NZ * NC)
        high = x0 & 2
        sign_high = jnp.where(high == 0, 1.0, -1.0).astype(F32)
        sign_low = jnp.where((x0 & 1) == 0, 1.0, -1.0).astype(F32)
        level = [
            got[high | p, 32:33, :] * (got[p, :32, :] + sign_high * got[p + 2, :32, :])
            for p in range(2)
        ]
        top[...], low[...] = split(
            got[x0, 33:34, :] * (0.5 * (level[0] + sign_low * level[1]))
        )

    for i in range(4):

        @pl.when(step == i)
        def _():
            depth = 256 * (i + 1)
            a, b = split(inverse[:depth, :])
            full[...] = (
                product(top[:, :depth], b)
                + product(low[:, :depth], a)
                + product(top[:, :depth], a)
            )

    keep[...] = full[pl.ds(pl.multiple_of(HALF * core, HALF), HALF), :]
    send[...] = full[pl.ds(pl.multiple_of(HALF * (1 - core), HALF), HALF), :]


def solve(info, pieces, inverse, token):
    part = pl.BlockSpec((HALF, 256), lambda i, s: (0, i))
    return call(
        solve_kernel,
        "solve",
        4,
        info,
        (*pieces, *far(inverse), token),
        [whole(40, NB)] * NX + [pl.BlockSpec((NB, 256), lambda i, s: (0, i)), ANY],
        [part] * 2,
        [jax.ShapeDtypeStruct((HALF, NB), F32)] * 2,
        12,
        [
            pltpu.VMEM((NX, 40, NB), F32),
            pltpu.VMEM((32, NB), BF16),
            pltpu.VMEM((32, NB), BF16),
            pltpu.VMEM((32, 256), F32),
        ],
    )


def update_kernel(n, info, *refs):
    own, other = refs[:n], refs[n : 2 * n]
    top, low = refs[2 * n : 2 * n + 2]
    outs, mine = refs[2 * n + 3 : 3 * n + 3], refs[3 * n + 3]
    left = refs[3 * n + 4]
    rows = 128 * n

    @pl.when(pl.program_id(0) == 0)
    def _():
        x, core = info[1], info[3]
        for t in range(NX):
            for h in range(NC):
                base = 32 * (x ^ t) + HALF * (core ^ h)
                for s in range(n):
                    piece = (other if h else own)[s][HALF * t : HALF * t + HALF, :]
                    a, b = split(piece)
                    left[pl.ds(pl.multiple_of(128 * s + base, HALF), HALF), :] = a
                    left[pl.ds(pl.multiple_of(rows + 128 * s + base, HALF), HALF), :] = b
                    if s == 0:
                        mine[pl.ds(pl.multiple_of(base, HALF), HALF), :] = piece

    both = product(left[...], top[0])
    done = product(left[:rows, :], low[0]) + both[rows:] + both[:rows]
    for s in range(n):
        outs[s][...] = done[128 * s : 128 * s + 128]


def update(info, own, other, top, low, token):
    n = len(own)
    band = pl.BlockSpec((1, NB, 256), lambda i, s: (i, 0, 0))
    return call(
        functools.partial(update_kernel, n),
        "update",
        4,
        info,
        (*own, *other, *far(top, low), token),
        [whole(64, NB)] * (2 * n) + [band] * 2 + [ANY],
        [pl.BlockSpec((128, 256), lambda i, s: (0, i))] * n + [whole(128, NB)],
        [jax.ShapeDtypeStruct((128, NB), F32)] * (n + 1),
        12,
        [pltpu.VMEM((256 * n, NB), BF16)],
        1,
    )


def mid_kernel(info, *refs):
    got, pieces, outs, mark = refs[0], refs[1:5], refs[6:10], refs[10]
    mark[...] = jnp.zeros((8, 128), F32)
    x = info[1]
    high = [jnp.where((x ^ s) & 2 == 0, 1.0, -1.0).astype(F32) for s in range(NX)]
    low = [jnp.where((x ^ s) & 1 == 0, 1.0, -1.0).astype(F32) for s in range(NX)]
    for i in range(NB // 128):
        at = slice(128 * i, 128 * i + 128)
        scale = [pieces[s][:, at].T for s in range(NX)]
        v = [got[x ^ s, at, :] for s in range(NX)]
        v = [scale[s][:, 2:3] * (v[s ^ 2] + high[s] * v[s]) for s in range(NX)]
        for s in range(NX):
            outs[s][at, :] = (0.5 * scale[s][:, 3:4]) * (v[s ^ 1] + low[s] * v[s])


def mid(info, got, pieces, token):
    return call(
        mid_kernel,
        "mid",
        1,
        info,
        (got, *far(*pieces), token),
        [whole(NX, NB, 128)]
        + [pl.BlockSpec((8, NB), lambda i, s: (4, 0))] * NX
        + [ANY],
        [whole(NB, 128)] * NX + [whole(8, 128)],
        [jax.ShapeDtypeStruct((NB, 128), F32)] * NX + [TOKEN],
        12,
        hint=10**10,
    )


def last_kernel(info, *refs):
    moved, mine, parts, out = refs[:4], refs[4], refs[5:9], refs[9]
    start, x, z, core, y = [info[i] for i in range(5)]
    step = pl.program_id(0)
    index = (x ^ step) * (NX * NZ * NC) + (x * NZ + z) * NC + core

    for s in range(NX):

        @pl.when((step == s) & (index < start))
        def _():
            out[0] = moved[s][...]

        @pl.when((step == s) & (index > start))
        def _():
            for q in range(NY):
                at = pl.ds(pl.multiple_of(256 * (y ^ q), 256), 256)
                out[0, at, :] = moved[s][at, :] - parts[q][...].T

    @pl.when(index == start)
    def _():
        out[0] = mine[...].T


def last(info, moved, mine, parts):
    return call(
        last_kernel,
        "last",
        NX,
        info,
        (*moved, mine, *parts),
        [whole(NB, 128)] * NX
        + [whole(128, NB)]
        + [pl.BlockSpec((128, 256), lambda i, s: (0, s[1] ^ i))] * NY,
        pl.BlockSpec((1, NB, 128), lambda i, s: (s[1] ^ i, 0, 0)),
        jax.ShapeDtypeStruct((4, NB, 128), F32),
        12,
    )


def after(value, token):
    return lax.optimization_barrier((value, token))[0]


def per_device(right_sides, butterfly_diagonals, band_rows, diag_inverse, band_block):
    place = lax.axis_index("rows")
    y = lax.axis_index("rhs")
    x, z, core = place // (NZ * NC), place // NC % NZ, place % NC
    start = band_block[0]
    info = jnp.stack([start, x, z, core, y]).astype(jnp.int32)
    z0 = start % (NX * NZ * NC) // NC % NZ
    core0 = start % NC

    message = prep(info, right_sides, butterfly_diagonals)
    pieces = [flip_x(message[s], s) for s in range(NX)]
    top, low, ready = split_band(info, band_rows, message[0])
    mixed = exchange_x(after(right_sides, (pieces, ready)))

    half, other_half = solve(info, pieces, diag_inverse, ready)
    half = jnp.where(core == core0, half, other_core(other_half))

    away = z ^ z0
    got = [flip_z(half, m) for m in (1, 2, 3)]
    for m in (1, 2, 3):
        half = jnp.where(away == m, got[m - 1], half)
    half = jnp.where(away >= 4, flip_z(half, 6), half)

    line = jnp.concatenate([half] + [flip_x(half, t) for t in range(1, NX)], axis=0)
    own = [flip_y(line, s) for s in range(NY)]
    *blocks, mixed_done = mid(info, mixed, pieces, line)
    moved = [flip_x(v, s) for s, v in enumerate(blocks)]

    other = [other_core(after(v, mixed_done)) for v in own[1:]]
    one, two, three, token = update(info, own[1:], other, top, low, mixed_done)
    rest = after(own[0], moved)
    zero, mine = update(info, [rest], [other_core(rest)], top, low, token)
    parts = [zero, flip_y(one, 1), flip_y(two, 2), flip_y(three, 3)]
    return last(info, moved, mine, parts)


def solution(mesh):
    return jax.shard_map(
        per_device,
        mesh=mesh,
        in_specs=(
            P(None, "rows", "rhs"),
            P(None, None, "rows"),
            P(None, None, ("rows", "rhs")),
            P(),
            P(),
        ),
        out_specs=P(None, "rows", "rhs"),
        check_vma=False,
    )
```

time: 387 us -> 110 us (0.28)
  waiting for transfers between devices: 332 us -> 39.4 us
  starting transfers between devices: 10.4 us -> 40.6 us
  Pallas kernels: 0 us -> 26.6 us
  between operations: 14.2 us -> 0.8 us
  matrix products: 12.8 us -> 0 us
  other arithmetic: 8.5 us -> 0.05 us
  local copies, waits for them, and re-layouts: 8.57 us -> 2.29 us
    psum x1 -> x0, waiting for transfers between devices: 184 us -> none  [broadcast(): return lax.psum(jnp.where(mine, array, jnp.zeros_like(array)), axis)]
    ppermute x2 -> x24, waiting for transfers between devices: 87.4 us -> 39.4 us  [the longest x9 20 us: flip_x(): lax.ppermute(v, 'rows', row_perm(lambda x, z, c: (x ^ m, z, c)))]
    all_gather x1 -> x0, waiting for transfers between devices: 34.6 us -> none  [per_device(): all_solved = lax.all_gather(solved, 'rhs', axis=1, tiled=True)]
    ppermute x2 -> x24, starting transfers between devices: 5.73 us -> 36.9 us  [the longest x9 10.9 us: flip_x(): lax.ppermute(v, 'rows', row_perm(lambda x, z, c: (x ^ m, z, c)))]
    pallas_call x0 -> x7, Pallas kernels: none -> 26.6 us  [call(): pl.pallas_call(body, grid_spec=pltpu.PrefetchScalarGridSpec(num_scalar_pr...]
    all_to_all x1, waiting for transfers between devices: 25.6 us -> 0.01 us  [exchange_x(): lax.all_to_all(v, 'rows', 0, 0, axis_index_groups=X_GROUPS, tiled=True)]
    dot_general x2 -> x0, matrix products: 12.8 us -> none  [the longest x1 9.57 us: per_device(): jnp.einsum('bck,bn->ckn', band_rows, all_solved, precision=lax.Precision....]
    mul x2 -> x0, other arithmetic: 5.23 us -> none  [apply_level(): return coefs[:, :, None] * mixed * factor]
  transfers between devices with their start and end apart: 5 -> 25, of which waited for: 5 -> 14; matrix products, arithmetic and copies ran while one was open for 0% -> 0% of each run, Pallas kernels for 0% -> 19%
where the time goes in v2:
time: 110 us
  starting transfers between devices  40.6 us (37%)
  waiting for transfers between devices  39.4 us (36%)
  Pallas kernels  26.6 us (24%)
  local copies, waits for them, and re-layouts  2.29 us (2%)
    pallas_call x7, Pallas kernels, call(): pl.pallas_call(body, grid_spec=pltpu.PrefetchScalarGridSpec(num_scalar_pr...  26.6 us
    ppermute x9, waiting for transfers between devices, flip_x(): lax.ppermute(v, 'rows', row_perm(lambda x, z, c: (x ^ m, z, c)))  20 us
    ppermute x9, starting transfers between devices, flip_x(): lax.ppermute(v, 'rows', row_perm(lambda x, z, c: (x ^ m, z, c)))  10.9 us
    ppermute x6, waiting for transfers between devices, flip_y(): return lax.ppermute(v, 'rhs', [(i, i ^ m) for i in range(NY)]) if m else v  10.4 us
    ppermute x6, starting transfers between devices, flip_y(): return lax.ppermute(v, 'rhs', [(i, i ^ m) for i in range(NY)]) if m else v  10.3 us
    ppermute x4, starting transfers between devices, flip_z(): return lax.ppermute(v, 'rows', row_perm(lambda x, z, c: (x, z ^ m, c)))  9.94 us
    ppermute x4, waiting for transfers between devices, flip_z(): return lax.ppermute(v, 'rows', row_perm(lambda x, z, c: (x, z ^ m, c)))  6.97 us
    ppermute x5, starting transfers between devices, other_core(): return lax.ppermute(v, 'rows', row_perm(lambda x, z, c: (x, z, 1 - c)))  5.84 us
  transfers between devices with their start and end apart: 25, of which 14 were waited for; matrix products, arithmetic and copies ran while one was open for 0% of the time, Pallas kernels for 19%

profile of v2, /device:TPU:1, one launch (start us, length us, event | category | flops | bytes accessed | tf_op | source)
XLA Modules:
  0.0 109.7 jit_solution(7416144495429176597)
XLA Ops:
  0.7 0.1 stack.19.info
  0.7 2.8 %prep.1 = (f32[40,1024]{1,0:T(8,128)S(1)}, f32[40,1024]{1,0:T(8,128)S(1)}, f32[40,1024]{1,0:T(8,128)S(1)}, f32[40,1024]{1,0:T(8,128)S(1)}) custom-call(s32[5]{0:T(128)S(1)} %stack.19.info, f32[4,1024,128]{2,1,0:T(8,128)} %slab.1, f32[2,4,1024]{2,1,0:T(4,128)} %diag.1), custom_call_target="tpu_custom_call" | custom-call | tf_op jit(solution)/shard_map/prep/pallas_call | solution.py:66
  3.6 0.0 copy-start.1
  3.6 2.1 %collective-permute-start = (f32[40,1024]{1,0:T(8,128)S(1)}, f32[40,1024]{1,0:T(8,128)S(1)}, u32[]{:S(2)}, u32[]{:S(2)}) collective-permute-start(f32[40,1024]{1,0:T(8,128)S(1)} %get-tuple-element.31), channel_id=1, source_target_pairs={{0,64},{4,68},{8,72},{12,76},{16,80},{20,84},{24,88},{28,92},{32,9... | collective-permute-start | bytes 491528 | tf_op jit(solution)/shard_map/ppermute | solution.py:27
  5.7 2.5 %collective-permute-start.1 = (f32[40,1024]{1,0:T(8,128)S(1)}, f32[40,1024]{1,0:T(8,128)S(1)}, u32[]{:S(2)}, u32[]{:S(2)}) collective-permute-start(f32[40,1024]{1,0:T(8,128)S(1)} %get-tuple-element.32), channel_id=1, source_target_pairs={{0,128},{4,132},{8,136},{12,140},{16,144},{20,148},{24,152},{28,15... | collective-permute-start | bytes 491528 | tf_op jit(solution)/shard_map/ppermute | solution.py:27
  8.2 0.0 collective-permute-start.2
  8.2 2.2 %copy-done = f32[1024,4,256]{2,1,0:T(4,128)S(1)} copy-done((f32[1024,4,256]{2,1,0:T(4,128)S(1)}, f32[1024,4,256]{2,1,0:T(4,128)}, u32[]{:S(2)}) %copy-start) | copy-done | bytes 4194328
  10.4 3.5 %split_band.1 = (bf16[4,1024,256]{2,1,0:T(8,128)(2,1)}, bf16[4,1024,256]{2,1,0:T(8,128)(2,1)}, f32[8,128]{1,0:T(8,128)S(1)}) custom-call(s32[5]{0:T(128)S(1)} %stack.19.info, f32[8192,128]{1,0:T(8,128)S(1)} %bitcast.13, f32[40,1024]{1,0:T(8,128)S(1)} %get-tuple-element.30.token.refs_0_.refs_1_), custom_call_target="tpu_custom_call" | custom-call | tf_op jit(solution)/shard_map/split_band/pallas_call | solution.py:66
  13.9 0.0 collective-permute-done.refs_1_.refs_2_
  13.9 1.4 %collective-permute-done.1.refs_2_.refs_3_ = f32[40,1024]{1,0:T(8,128)S(1)} collective-permute-done((f32[40,1024]{1,0:T(8,128)S(1)}, f32[40,1024]{1,0:T(8,128)S(1)}, u32[]{:S(2)}, u32[]{:S(2)}) %collective-permute-start.1) | collective-permute-done | bytes 163872 | tf_op jit(solution)/shard_map/ppermute | solution.py:27
  15.3 2.7 %collective-permute-done.2.refs_3_.refs_4_ = f32[40,1024]{1,0:T(8,128)S(1)} collective-permute-done((f32[40,1024]{1,0:T(8,128)S(1)}, f32[40,1024]{1,0:T(8,128)S(1)}, u32[]{:S(2)}, u32[]{:S(2)}) %collective-permute-start.2) | collective-permute-done | bytes 163872 | tf_op jit(solution)/shard_map/ppermute | solution.py:27
  18.0 3.6 %all-to-all-start = ((f32[4,1024,128]{2,1,0:T(8,128)}), f32[4,1024,128]{2,1,0:T(8,128)S(1)}, u32[]{:S(2)}, u32[]{:S(2)}) async-start(f32[4,1024,128]{2,1,0:T(8,128)} %slab.1), calls=%async_computation | async-start | bytes 4194304 | tf_op jit(solution)/shard_map/all_to_all | solution.py:42
  21.7 0.0 copy-done.1
  21.7 0.0 copy-done.2
  21.7 0.0 copy-done.3
  21.7 0.0 copy-done.4
  21.7 4.1 %solve.1 = (f32[16,1024]{1,0:T(8,128)S(1)}, f32[16,1024]{1,0:T(8,128)S(1)}) custom-call(s32[5]{0:T(128)S(1)} %stack.19.info, f32[40,1024]{1,0:T(8,128)S(1)} %get-tuple-element.30.token.refs_0_.refs_1_, f32[40,1024]{1,0:T(8,128)S(1)} %collective-permute-done.refs_1_.refs_2_, f32[40,1024]{1,0:T(8,128)S(1)} %collective-permute-done.1.refs_2_.refs_3_, ...), custom_call_target="tpu_custom_call" | custom-call | tf_op jit(solution)/shard_map/solve/pallas_call | solution.py:66
  25.8 1.4 %collective-permute-start.3 = (f32[16,1024]{1,0:T(8,128)S(1)}, f32[16,1024]{1,0:T(8,128)S(1)}, u32[]{:S(2)}, u32[]{:S(2)}) collective-permute-start(f32[16,1024]{1,0:T(8,128)S(1)} %get-tuple-element.37), channel_id=1, source_target_pairs={{0,4},{4,0},{8,12},{12,8},{16,20},{20,16},{24,28},{28,24},{32,36},... | collective-permute-start | bytes 196616 | tf_op jit(solution)/shard_map/ppermute | solution.py:46
  27.2 0.9 collective-permute-done.3
  28.1 1.7 %collective-permute-start.6 = (f32[16,1024]{1,0:T(8,128)S(1)}, f32[16,1024]{1,0:T(8,128)S(1)}, u32[]{:S(2)}, u32[]{:S(2)}) collective-permute-start(f32[16,1024]{1,0:T(8,128)S(1)} %broadcast_select_fusion), channel_id=1, source_target_pairs={{0,8},{4,12},{8,0},{12,4},{16,24},{20,28},{24,16},{28,20},{32,40},... | collective-permute-start | bytes 196616 | tf_op jit(solution)/shard_map/ppermute | solution.py:31
  29.8 3.0 %collective-permute-start.5 = (f32[16,1024]{1,0:T(8,128)S(1)}, f32[16,1024]{1,0:T(8,128)S(1)}, u32[]{:S(2)}, u32[]{:S(2)}) collective-permute-start(f32[16,1024]{1,0:T(8,128)S(1)} %broadcast_select_fusion), channel_id=1, source_target_pairs={{0,16},{4,20},{8,24},{12,28},{16,0},{20,4},{24,8},{28,12},{32,48},... | collective-permute-start | bytes 196616 | tf_op jit(solution)/shard_map/ppermute | solution.py:31
  32.8 0.0 collective-permute-start.4
  32.8 0.0 collective-permute-done.6
  32.8 2.2 %collective-permute-done.5 = f32[16,1024]{1,0:T(8,128)S(1)} collective-permute-done((f32[16,1024]{1,0:T(8,128)S(1)}, f32[16,1024]{1,0:T(8,128)S(1)}, u32[]{:S(2)}, u32[]{:S(2)}) %collective-permute-start.5) | collective-permute-done | bytes 65568 | tf_op jit(solution)/shard_map/ppermute | solution.py:31
  35.0 2.8 %collective-permute-done.4 = f32[16,1024]{1,0:T(8,128)S(1)} collective-permute-done((f32[16,1024]{1,0:T(8,128)S(1)}, f32[16,1024]{1,0:T(8,128)S(1)}, u32[]{:S(2)}, u32[]{:S(2)}) %collective-permute-start.4) | collective-permute-done | bytes 65568 | tf_op jit(solution)/shard_map/ppermute | solution.py:31
  37.8 5.2 %collective-permute-start.7 = (f32[16,1024]{1,0:T(8,128)S(1)}, f32[16,1024]{1,0:T(8,128)S(1)}, u32[]{:S(2)}, u32[]{:S(2)}) collective-permute-start(f32[16,1024]{1,0:T(8,128)S(1)} %select_select_fusion), channel_id=1, source_target_pairs={{0,48},{4,52},{8,56},{12,60},{16,32},{20,36},{24,40},{28,44},{32,1... | collective-permute-start | bytes 196616 | tf_op jit(solution)/shard_map/ppermute | solution.py:31
  43.1 2.0 %collective-permute-done.7 = f32[16,1024]{1,0:T(8,128)S(1)} collective-permute-done((f32[16,1024]{1,0:T(8,128)S(1)}, f32[16,1024]{1,0:T(8,128)S(1)}, u32[]{:S(2)}, u32[]{:S(2)}) %collective-permute-start.7) | collective-permute-done | bytes 65568 | tf_op jit(solution)/shard_map/ppermute | solution.py:31
  45.0 2.7 %collective-permute-start.10 = (f32[16,1024]{1,0:T(8,128)S(1)}, f32[16,1024]{1,0:T(8,128)S(1)}, u32[]{:S(2)}, u32[]{:S(2)}) collective-permute-start(f32[16,1024]{1,0:T(8,128)S(1)} %broadcast_select_fusion.1), channel_id=1, source_target_pairs={{0,192},{4,196},{8,200},{12,204},{16,208},{20,212},{24,216},{28,22... | collective-permute-start | bytes 196616 | tf_op jit(solution)/shard_map/ppermute | solution.py:27
  47.7 0.4 collective-permute-start.9
  48.1 0.3 collective-permute-start.8
  48.4 1.0 collective-permute-done.10
  49.4 3.0 %collective-permute-done.9 = f32[16,1024]{1,0:T(8,128)S(1)} collective-permute-done((f32[16,1024]{1,0:T(8,128)S(1)}, f32[16,1024]{1,0:T(8,128)S(1)}, u32[]{:S(2)}, u32[]{:S(2)}) %collective-permute-start.9) | collective-permute-done | bytes 65568 | tf_op jit(solution)/shard_map/ppermute | solution.py:27
  52.5 0.0 collective-permute-done.8
  52.5 2.8 %collective-permute-start.17 = (f32[64,1024]{1,0:T(8,128)S(1)}, f32[64,1024]{1,0:T(8,128)S(1)}, u32[]{:S(2)}, u32[]{:S(2)}) collective-permute-start(f32[64,1024]{1,0:T(8,128)S(1)} %pad_maximum_fusion.refs_5_.refs_0_), channel_id=1, source_target_pairs={{0,3},{1,2},{2,1},{3,0},{4,7},{5,6},{6,5},{7,4},{8,11},{9,10},{10,... | collective-permute-start | bytes 786440 | tf_op jit(solution)/shard_map/ppermute | solution.py:35
  55.3 0.3 collective-permute-start.16
  55.7 0.3 collective-permute-start.15
  56.0 0.0 all-to-all-done.refs_0_
  56.0 3.1 %mid.1 = (f32[1024,128]{1,0:T(8,128)S(1)}, f32[1024,128]{1,0:T(8,128)S(1)}, f32[1024,128]{1,0:T(8,128)S(1)}, f32[1024,128]{1,0:T(8,128)S(1)}, f32[8,128]{1,0:T(8,128)S(1)}) custom-call(s32[5]{0:T(128)S(1)} %stack.19.info, f32[4,1024,128]{2,1,0:T(8,128)S(1)} %all-to-all-done.refs_0_, f32[40,1024]{1,0:T(8,128)} %copy-done.1, f32[40,1024]{1,0:T(8,128)} %copy-done.2, ...), custom_call_target="tpu_custom_call" | custom-call | flops 10000000000 | bytes 1048576 | tf_op jit(solution)/shard_map/mid/pallas_call | solution.py:66
  59.1 6.5 %collective-permute-done.17.refs_2_ = f32[64,1024]{1,0:T(8,128)S(1)} collective-permute-done((f32[64,1024]{1,0:T(8,128)S(1)}, f32[64,1024]{1,0:T(8,128)S(1)}, u32[]{:S(2)}, u32[]{:S(2)}) %collective-permute-start.17) | collective-permute-done | bytes 262176 | tf_op jit(solution)/shard_map/ppermute | solution.py:35
  65.6 1.9 %collective-permute-start.20 = (f32[64,1024]{1,0:T(8,128)S(1)}, f32[64,1024]{1,0:T(8,128)S(1)}, u32[]{:S(2)}, u32[]{:S(2)}) collective-permute-start(f32[64,1024]{1,0:T(8,128)S(1)} %collective-permute-done.17.refs_2_), channel_id=1, source_target_pairs={{0,4},{4,0},{8,12},{12,8},{16,20},{20,16},{24,28},{28,24},{32,36},... | collective-permute-start | bytes 786440 | tf_op jit(solution)/shard_map/ppermute | solution.py:46
  67.4 0.0 collective-permute-start.11
  67.5 0.0 collective-permute-done.16.refs_1_
  67.5 0.9 collective-permute-start.19
  68.4 0.0 collective-permute-done.15.refs_0_
  68.4 0.6 collective-permute-start.18
  68.9 1.6 %collective-permute-start.12 = (f32[1024,128]{1,0:T(8,128)S(1)}, f32[1024,128]{1,0:T(8,128)S(1)}, u32[]{:S(2)}, u32[]{:S(2)}) collective-permute-start(f32[1024,128]{1,0:T(8,128)S(1)} %get-tuple-element.40), channel_id=1, source_target_pairs={{0,128},{4,132},{8,136},{12,140},{16,144},{20,148},{24,152},{28,15... | collective-permute-start | bytes 1572872 | tf_op jit(solution)/shard_map/ppermute | solution.py:27
  70.6 0.0 collective-permute-done.20.refs_5_
  70.6 1.2 %collective-permute-start.13 = (f32[1024,128]{1,0:T(8,128)S(1)}, f32[1024,128]{1,0:T(8,128)S(1)}, u32[]{:S(2)}, u32[]{:S(2)}) collective-permute-start(f32[1024,128]{1,0:T(8,128)S(1)} %get-tuple-element.41), channel_id=1, source_target_pairs={{0,192},{4,196},{8,200},{12,204},{16,208},{20,212},{24,216},{28,22... | collective-permute-start | bytes 1572872 | tf_op jit(solution)/shard_map/ppermute | solution.py:27
  71.8 0.0 collective-permute-done.19.refs_4_
  71.8 0.0 collective-permute-done.18.refs_3_
  71.8 5.8 %update.2 = (f32[128,1024]{1,0:T(8,128)S(1)}, f32[128,1024]{1,0:T(8,128)S(1)}, f32[128,1024]{1,0:T(8,128)S(1)}, f32[128,1024]{1,0:T(8,128)S(1)}) custom-call(s32[5]{0:T(128)S(1)} %stack.19.info, f32[64,1024]{1,0:T(8,128)S(1)} %collective-permute-done.15.refs_0_, f32[64,1024]{1,0:T(8,128)S(1)} %collective-permute-done.16.refs_1_, ...), custom_call_target="tpu_custom_call" | custom-call | flops 1 | bytes 1048576 | tf_op jit(solution)/shard_map/update/pallas_call | solution.py:66
  77.6 0.7 collective-permute-start.21
  78.3 4.0 %collective-permute-start.22 = (f32[128,1024]{1,0:T(8,128)S(1)}, f32[128,1024]{1,0:T(8,128)S(1)}, u32[]{:S(2)}, u32[]{:S(2)}) collective-permute-start(f32[128,1024]{1,0:T(8,128)S(1)} %get-tuple-element.53), channel_id=1, source_target_pairs={{0,2},{1,3},{2,0},{3,1},{4,6},{5,7},{6,4},{7,5},{8,10},{9,11},{10,... | collective-permute-start | bytes 1572872 | tf_op jit(solution)/shard_map/ppermute | solution.py:35
  82.3 0.0 collective-permute-done.11.refs_1_
  82.3 2.1 %collective-permute-start.23 = (f32[128,1024]{1,0:T(8,128)S(1)}, f32[128,1024]{1,0:T(8,128)S(1)}, u32[]{:S(2)}, u32[]{:S(2)}) collective-permute-start(f32[128,1024]{1,0:T(8,128)S(1)} %get-tuple-element.54), channel_id=1, source_target_pairs={{0,3},{1,2},{2,1},{3,0},{4,7},{5,6},{6,5},{7,4},{8,11},{9,10},{10,... | collective-permute-start | bytes 1572872 | tf_op jit(solution)/shard_map/ppermute | solution.py:35
  84.4 8.5 %collective-permute-done.12.refs_2_ = f32[1024,128]{1,0:T(8,128)S(1)} collective-permute-done((f32[1024,128]{1,0:T(8,128)S(1)}, f32[1024,128]{1,0:T(8,128)S(1)}, u32[]{:S(2)}, u32[]{:S(2)}) %collective-permute-start.12) | collective-permute-done | bytes 524320 | tf_op jit(solution)/shard_map/ppermute | solution.py:27
  92.9 3.4 %collective-permute-done.13.refs_3_ = f32[1024,128]{1,0:T(8,128)S(1)} collective-permute-done((f32[1024,128]{1,0:T(8,128)S(1)}, f32[1024,128]{1,0:T(8,128)S(1)}, u32[]{:S(2)}, u32[]{:S(2)}) %collective-permute-start.13) | collective-permute-done | bytes 524320 | tf_op jit(solution)/shard_map/ppermute | solution.py:27
  96.3 1.1 %collective-permute-start.14 = (f32[64,1024]{1,0:T(8,128)S(1)}, f32[64,1024]{1,0:T(8,128)S(1)}, u32[]{:S(2)}, u32[]{:S(2)}) collective-permute-start(f32[64,1024]{1,0:T(8,128)S(1)} %pad_maximum_fusion.refs_5_.refs_0_), channel_id=1, source_target_pairs={{0,4},{4,0},{8,12},{12,8},{16,20},{20,16},{24,28},{28,24},{32,36},... | collective-permute-start | bytes 786440 | tf_op jit(solution)/shard_map/ppermute | solution.py:46
  97.4 1.2 %collective-permute-done.14.refs_1_ = f32[64,1024]{1,0:T(8,128)S(1)} collective-permute-done((f32[64,1024]{1,0:T(8,128)S(1)}, f32[64,1024]{1,0:T(8,128)S(1)}, u32[]{:S(2)}, u32[]{:S(2)}) %collective-permute-start.14) | collective-permute-done | bytes 262176 | tf_op jit(solution)/shard_map/ppermute | solution.py:46
  98.6 4.3 %update.3 = (f32[128,1024]{1,0:T(8,128)S(1)}, f32[128,1024]{1,0:T(8,128)S(1)}) custom-call(s32[5]{0:T(128)S(1)} %stack.19.info, f32[64,1024]{1,0:T(8,128)S(1)} %pad_maximum_fusion.refs_5_.refs_0_, f32[64,1024]{1,0:T(8,128)S(1)} %collective-permute-done.14.refs_1_, bf16[4,1024,256]{2,1,0:T(8,128)(2,1)} %get-tuple-element.43.refs_6_.refs_2_, ...), custom_call_target="tpu_custom_call" | custom-call | flops 1 | bytes 1048576 | tf_op jit(solution)/shard_map/update/pallas_call | solution.py:66
  102.9 0.0 collective-permute-done.21.refs_6_
  102.9 1.8 %collective-permute-done.22.refs_7_ = f32[128,1024]{1,0:T(8,128)S(1)} collective-permute-done((f32[128,1024]{1,0:T(8,128)S(1)}, f32[128,1024]{1,0:T(8,128)S(1)}, u32[]{:S(2)}, u32[]{:S(2)}) %collective-permute-start.22) | collective-permute-done | bytes 524320 | tf_op jit(solution)/shard_map/ppermute | solution.py:35
  104.7 2.0 %collective-permute-done.23.refs_8_ = f32[128,1024]{1,0:T(8,128)S(1)} collective-permute-done((f32[128,1024]{1,0:T(8,128)S(1)}, f32[128,1024]{1,0:T(8,128)S(1)}, u32[]{:S(2)}, u32[]{:S(2)}) %collective-permute-start.23) | collective-permute-done | bytes 524320 | tf_op jit(solution)/shard_map/ppermute | solution.py:35
  106.8 3.0 %last.1 = f32[4,1024,128]{2,1,0:T(8,128)} custom-call(s32[5]{0:T(128)S(1)} %stack.19.info, f32[1024,128]{1,0:T(8,128)S(1)} %get-tuple-element.38.refs_0_, f32[1024,128]{1,0:T(8,128)S(1)} %collective-permute-done.11.refs_1_, f32[1024,128]{1,0:T(8,128)S(1)} %collective-permute-done.12.refs_2_, f32[1024,128]{1,0:T(8,128)S(1)} %collective-permute-done.13.refs_3_, ...), custom_call_target="tpu_custom_call" | custom-call | tf_op jit(solution)/shard_map/last/pallas_call | solution.py:66
  (8 shorter events, 0.1 us)
Async XLA Ops:
  3.6 18.1 %copy-start.1 = (f32[40,1024]{1,0:T(8,128)}, f32[40,1024]{1,0:T(8,128)S(1)}, u32[]{:S(2)}) copy-start(f32[40,1024]{1,0:T(8,128)S(1)} %get-tuple-element.30.token.refs_0_.refs_1_) | copy-start | bytes 491524
  3.6 10.3 %collective-permute-start = (f32[40,1024]{1,0:T(8,128)S(1)}, f32[40,1024]{1,0:T(8,128)S(1)}, u32[]{:S(2)}, u32[]{:S(2)}) collective-permute-start(f32[40,1024]{1,0:T(8,128)S(1)} %get-tuple-element.31), channel_id=1, source_target_pairs={{0,64},{4,68},{8,72},{12,76},{16,80},{20,84},{24,88},{28,92},{32,9... | collective-permute-start | bytes 491528 | tf_op jit(solution)/shard_map/ppermute | solution.py:27
  5.7 9.6 %collective-permute-start.1 = (f32[40,1024]{1,0:T(8,128)S(1)}, f32[40,1024]{1,0:T(8,128)S(1)}, u32[]{:S(2)}, u32[]{:S(2)}) collective-permute-start(f32[40,1024]{1,0:T(8,128)S(1)} %get-tuple-element.32), channel_id=1, source_target_pairs={{0,128},{4,132},{8,136},{12,140},{16,144},{20,148},{24,152},{28,15... | collective-permute-start | bytes 491528 | tf_op jit(solution)/shard_map/ppermute | solution.py:27
  8.2 9.9 %collective-permute-start.2 = (f32[40,1024]{1,0:T(8,128)S(1)}, f32[40,1024]{1,0:T(8,128)S(1)}, u32[]{:S(2)}, u32[]{:S(2)}) collective-permute-start(f32[40,1024]{1,0:T(8,128)S(1)} %get-tuple-element.33), channel_id=1, source_target_pairs={{0,192},{4,196},{8,200},{12,204},{16,208},{20,212},{24,216},{28,22... | collective-permute-start | bytes 491528 | tf_op jit(solution)/shard_map/ppermute | solution.py:27
  8.2 2.2 %copy-start = (f32[1024,4,256]{2,1,0:T(4,128)S(1)}, f32[1024,4,256]{2,1,0:T(4,128)}, u32[]{:S(2)}) copy-start(f32[1024,4,256]{2,1,0:T(4,128)} %param.7) | copy-start | bytes 12582916
  13.9 7.8 %copy-start.2 = (f32[40,1024]{1,0:T(8,128)}, f32[40,1024]{1,0:T(8,128)S(1)}, u32[]{:S(2)}) copy-start(f32[40,1024]{1,0:T(8,128)S(1)} %collective-permute-done.refs_1_.refs_2_) | copy-start | bytes 491524
  15.3 6.4 %copy-start.3 = (f32[40,1024]{1,0:T(8,128)}, f32[40,1024]{1,0:T(8,128)S(1)}, u32[]{:S(2)}) copy-start(f32[40,1024]{1,0:T(8,128)S(1)} %collective-permute-done.1.refs_2_.refs_3_) | copy-start | bytes 491524
  18.0 3.7 %copy-start.4 = (f32[40,1024]{1,0:T(8,128)}, f32[40,1024]{1,0:T(8,128)S(1)}, u32[]{:S(2)}) copy-start(f32[40,1024]{1,0:T(8,128)S(1)} %collective-permute-done.2.refs_3_.refs_4_) | copy-start | bytes 491524
  18.0 37.9 %all-to-all-start = ((f32[4,1024,128]{2,1,0:T(8,128)}), f32[4,1024,128]{2,1,0:T(8,128)S(1)}, u32[]{:S(2)}, u32[]{:S(2)}) async-start(f32[4,1024,128]{2,1,0:T(8,128)} %slab.1), calls=%async_computation | async-start | bytes 4194304 | tf_op jit(solution)/shard_map/all_to_all | solution.py:42
  25.8 2.3 %collective-permute-start.3 = (f32[16,1024]{1,0:T(8,128)S(1)}, f32[16,1024]{1,0:T(8,128)S(1)}, u32[]{:S(2)}, u32[]{:S(2)}) collective-permute-start(f32[16,1024]{1,0:T(8,128)S(1)} %get-tuple-element.37), channel_id=1, source_target_pairs={{0,4},{4,0},{8,12},{12,8},{16,20},{20,16},{24,28},{28,24},{32,36},... | collective-permute-start | bytes 196616 | tf_op jit(solution)/shard_map/ppermute | solution.py:46
  28.1 4.7 %collective-permute-start.6 = (f32[16,1024]{1,0:T(8,128)S(1)}, f32[16,1024]{1,0:T(8,128)S(1)}, u32[]{:S(2)}, u32[]{:S(2)}) collective-permute-start(f32[16,1024]{1,0:T(8,128)S(1)} %broadcast_select_fusion), channel_id=1, source_target_pairs={{0,8},{4,12},{8,0},{12,4},{16,24},{20,28},{24,16},{28,20},{32,40},... | collective-permute-start | bytes 196616 | tf_op jit(solution)/shard_map/ppermute | solution.py:31
  29.8 5.2 %collective-permute-start.5 = (f32[16,1024]{1,0:T(8,128)S(1)}, f32[16,1024]{1,0:T(8,128)S(1)}, u32[]{:S(2)}, u32[]{:S(2)}) collective-permute-start(f32[16,1024]{1,0:T(8,128)S(1)} %broadcast_select_fusion), channel_id=1, source_target_pairs={{0,16},{4,20},{8,24},{12,28},{16,0},{20,4},{24,8},{28,12},{32,48},... | collective-permute-start | bytes 196616 | tf_op jit(solution)/shard_map/ppermute | solution.py:31
  32.8 5.0 %collective-permute-start.4 = (f32[16,1024]{1,0:T(8,128)S(1)}, f32[16,1024]{1,0:T(8,128)S(1)}, u32[]{:S(2)}, u32[]{:S(2)}) collective-permute-start(f32[16,1024]{1,0:T(8,128)S(1)} %broadcast_select_fusion), channel_id=1, source_target_pairs={{0,24},{4,28},{8,16},{12,20},{16,8},{20,12},{24,0},{28,4},{32,56},... | collective-permute-start | bytes 196616 | tf_op jit(solution)/shard_map/ppermute | solution.py:31
  37.8 7.2 %collective-permute-start.7 = (f32[16,1024]{1,0:T(8,128)S(1)}, f32[16,1024]{1,0:T(8,128)S(1)}, u32[]{:S(2)}, u32[]{:S(2)}) collective-permute-start(f32[16,1024]{1,0:T(8,128)S(1)} %select_select_fusion), channel_id=1, source_target_pairs={{0,48},{4,52},{8,56},{12,60},{16,32},{20,36},{24,40},{28,44},{32,1... | collective-permute-start | bytes 196616 | tf_op jit(solution)/shard_map/ppermute | solution.py:31
  45.0 4.4 %collective-permute-start.10 = (f32[16,1024]{1,0:T(8,128)S(1)}, f32[16,1024]{1,0:T(8,128)S(1)}, u32[]{:S(2)}, u32[]{:S(2)}) collective-permute-start(f32[16,1024]{1,0:T(8,128)S(1)} %broadcast_select_fusion.1), channel_id=1, source_target_pairs={{0,192},{4,196},{8,200},{12,204},{16,208},{20,212},{24,216},{28,22... | collective-permute-start | bytes 196616 | tf_op jit(solution)/shard_map/ppermute | solution.py:27
  47.7 4.7 %collective-permute-start.9 = (f32[16,1024]{1,0:T(8,128)S(1)}, f32[16,1024]{1,0:T(8,128)S(1)}, u32[]{:S(2)}, u32[]{:S(2)}) collective-permute-start(f32[16,1024]{1,0:T(8,128)S(1)} %broadcast_select_fusion.1), channel_id=1, source_target_pairs={{0,128},{4,132},{8,136},{12,140},{16,144},{20,148},{24,152},{28,15... | collective-permute-start | bytes 196616 | tf_op jit(solution)/shard_map/ppermute | solution.py:27
  48.1 4.3 %collective-permute-start.8 = (f32[16,1024]{1,0:T(8,128)S(1)}, f32[16,1024]{1,0:T(8,128)S(1)}, u32[]{:S(2)}, u32[]{:S(2)}) collective-permute-start(f32[16,1024]{1,0:T(8,128)S(1)} %broadcast_select_fusion.1), channel_id=1, source_target_pairs={{0,64},{4,68},{8,72},{12,76},{16,80},{20,84},{24,88},{28,92},{32,9... | collective-permute-start | bytes 196616 | tf_op jit(solution)/shard_map/ppermute | solution.py:27
  52.5 13.1 %collective-permute-start.17 = (f32[64,1024]{1,0:T(8,128)S(1)}, f32[64,1024]{1,0:T(8,128)S(1)}, u32[]{:S(2)}, u32[]{:S(2)}) collective-permute-start(f32[64,1024]{1,0:T(8,128)S(1)} %pad_maximum_fusion.refs_5_.refs_0_), channel_id=1, source_target_pairs={{0,3},{1,2},{2,1},{3,0},{4,7},{5,6},{6,5},{7,4},{8,11},{9,10},{10,... | collective-permute-start | bytes 786440 | tf_op jit(solution)/shard_map/ppermute | solution.py:35
  55.3 12.1 %collective-permute-start.16 = (f32[64,1024]{1,0:T(8,128)S(1)}, f32[64,1024]{1,0:T(8,128)S(1)}, u32[]{:S(2)}, u32[]{:S(2)}) collective-permute-start(f32[64,1024]{1,0:T(8,128)S(1)} %pad_maximum_fusion.refs_5_.refs_0_), channel_id=1, source_target_pairs={{0,2},{1,3},{2,0},{3,1},{4,6},{5,7},{6,4},{7,5},{8,10},{9,11},{10,... | collective-permute-start | bytes 786440 | tf_op jit(solution)/shard_map/ppermute | solution.py:35
  55.7 12.7 %collective-permute-start.15 = (f32[64,1024]{1,0:T(8,128)S(1)}, f32[64,1024]{1,0:T(8,128)S(1)}, u32[]{:S(2)}, u32[]{:S(2)}) collective-permute-start(f32[64,1024]{1,0:T(8,128)S(1)} %pad_maximum_fusion.refs_5_.refs_0_), channel_id=1, source_target_pairs={{0,1},{1,0},{2,3},{3,2},{4,5},{5,4},{6,7},{7,6},{8,9},{9,8},{10,11... | collective-permute-start | bytes 786440 | tf_op jit(solution)/shard_map/ppermute | solution.py:35
  65.6 5.0 %collective-permute-start.20 = (f32[64,1024]{1,0:T(8,128)S(1)}, f32[64,1024]{1,0:T(8,128)S(1)}, u32[]{:S(2)}, u32[]{:S(2)}) collective-permute-start(f32[64,1024]{1,0:T(8,128)S(1)} %collective-permute-done.17.refs_2_), channel_id=1, source_target_pairs={{0,4},{4,0},{8,12},{12,8},{16,20},{20,16},{24,28},{28,24},{32,36},... | collective-permute-start | bytes 786440 | tf_op jit(solution)/shard_map/ppermute | solution.py:46
  67.4 14.9 %collective-permute-start.11 = (f32[1024,128]{1,0:T(8,128)S(1)}, f32[1024,128]{1,0:T(8,128)S(1)}, u32[]{:S(2)}, u32[]{:S(2)}) collective-permute-start(f32[1024,128]{1,0:T(8,128)S(1)} %get-tuple-element.39), channel_id=1, source_target_pairs={{0,64},{4,68},{8,72},{12,76},{16,80},{20,84},{24,88},{28,92},{32,9... | collective-permute-start | bytes 1572872 | tf_op jit(solution)/shard_map/ppermute | solution.py:27
  67.5 4.4 %collective-permute-start.19 = (f32[64,1024]{1,0:T(8,128)S(1)}, f32[64,1024]{1,0:T(8,128)S(1)}, u32[]{:S(2)}, u32[]{:S(2)}) collective-permute-start(f32[64,1024]{1,0:T(8,128)S(1)} %collective-permute-done.16.refs_1_), channel_id=1, source_target_pairs={{0,4},{4,0},{8,12},{12,8},{16,20},{20,16},{24,28},{28,24},{32,36},... | collective-permute-start | bytes 786440 | tf_op jit(solution)/shard_map/ppermute | solution.py:46
  68.4 3.5 %collective-permute-start.18 = (f32[64,1024]{1,0:T(8,128)S(1)}, f32[64,1024]{1,0:T(8,128)S(1)}, u32[]{:S(2)}, u32[]{:S(2)}) collective-permute-start(f32[64,1024]{1,0:T(8,128)S(1)} %collective-permute-done.15.refs_0_), channel_id=1, source_target_pairs={{0,4},{4,0},{8,12},{12,8},{16,20},{20,16},{24,28},{28,24},{32,36},... | collective-permute-start | bytes 786440 | tf_op jit(solution)/shard_map/ppermute | solution.py:46
  68.9 23.9 %collective-permute-start.12 = (f32[1024,128]{1,0:T(8,128)S(1)}, f32[1024,128]{1,0:T(8,128)S(1)}, u32[]{:S(2)}, u32[]{:S(2)}) collective-permute-start(f32[1024,128]{1,0:T(8,128)S(1)} %get-tuple-element.40), channel_id=1, source_target_pairs={{0,128},{4,132},{8,136},{12,140},{16,144},{20,148},{24,152},{28,15... | collective-permute-start | bytes 1572872 | tf_op jit(solution)/shard_map/ppermute | solution.py:27
  70.6 25.7 %collective-permute-start.13 = (f32[1024,128]{1,0:T(8,128)S(1)}, f32[1024,128]{1,0:T(8,128)S(1)}, u32[]{:S(2)}, u32[]{:S(2)}) collective-permute-start(f32[1024,128]{1,0:T(8,128)S(1)} %get-tuple-element.41), channel_id=1, source_target_pairs={{0,192},{4,196},{8,200},{12,204},{16,208},{20,212},{24,216},{28,22... | collective-permute-start | bytes 1572872 | tf_op jit(solution)/shard_map/ppermute | solution.py:27
  77.6 25.2 %collective-permute-start.21 = (f32[128,1024]{1,0:T(8,128)S(1)}, f32[128,1024]{1,0:T(8,128)S(1)}, u32[]{:S(2)}, u32[]{:S(2)}) collective-permute-start(f32[128,1024]{1,0:T(8,128)S(1)} %get-tuple-element.52), channel_id=1, source_target_pairs={{0,1},{1,0},{2,3},{3,2},{4,5},{5,4},{6,7},{7,6},{8,9},{9,8},{10,11... | collective-permute-start | bytes 1572872 | tf_op jit(solution)/shard_map/ppermute | solution.py:35
  78.3 26.4 %collective-permute-start.22 = (f32[128,1024]{1,0:T(8,128)S(1)}, f32[128,1024]{1,0:T(8,128)S(1)}, u32[]{:S(2)}, u32[]{:S(2)}) collective-permute-start(f32[128,1024]{1,0:T(8,128)S(1)} %get-tuple-element.53), channel_id=1, source_target_pairs={{0,2},{1,3},{2,0},{3,1},{4,6},{5,7},{6,4},{7,5},{8,10},{9,11},{10,... | collective-permute-start | bytes 1572872 | tf_op jit(solution)/shard_map/ppermute | solution.py:35
  82.3 24.5 %collective-permute-start.23 = (f32[128,1024]{1,0:T(8,128)S(1)}, f32[128,1024]{1,0:T(8,128)S(1)}, u32[]{:S(2)}, u32[]{:S(2)}) collective-permute-start(f32[128,1024]{1,0:T(8,128)S(1)} %get-tuple-element.54), channel_id=1, source_target_pairs={{0,3},{1,2},{2,1},{3,0},{4,7},{5,6},{6,5},{7,4},{8,11},{9,10},{10,... | collective-permute-start | bytes 1572872 | tf_op jit(solution)/shard_map/ppermute | solution.py:35
  96.3 2.3 %collective-permute-start.14 = (f32[64,1024]{1,0:T(8,128)S(1)}, f32[64,1024]{1,0:T(8,128)S(1)}, u32[]{:S(2)}, u32[]{:S(2)}) collective-permute-start(f32[64,1024]{1,0:T(8,128)S(1)} %pad_maximum_fusion.refs_5_.refs_0_), channel_id=1, source_target_pairs={{0,4},{4,0},{8,12},{12,8},{16,20},{20,16},{24,28},{28,24},{32,36},... | collective-permute-start | bytes 786440 | tf_op jit(solution)/shard_map/ppermute | solution.py:46

commit v3 on v2

--- a/solution.py
+++ b/solution.py
@@ -9,6 +9,7 @@
 NX, NZ, NC, NY = 4, 8, 2, 4
 NB = 1024
 HALF = 16
+OWN_HINT = 2 * 10**9
 F32 = jnp.float32
 BF16 = jnp.bfloat16
 
@@ -61,7 +62,7 @@
     return pl.BlockSpec(shape, lambda i, s: (0,) * len(shape))
 
 
-def call(body, name, grid, info, args, in_specs, out_specs, out_shape, mib, scratch=(), hint=0):
+def call(body, name, grid, info, args, in_specs, out_specs, out_shape, mib, scratch=(), hint=0, aliases={}):
     cost = pl.CostEstimate(flops=hint, bytes_accessed=1 << 20, transcendentals=0)
     return pl.pallas_call(
         body,
@@ -73,6 +74,7 @@
             scratch_shapes=list(scratch),
         ),
         out_shape=out_shape,
+        input_output_aliases=aliases,
         compiler_params=params(mib),
         cost_estimate=cost if hint else None,
         name=name,
@@ -118,28 +120,50 @@
 TOKEN = jax.ShapeDtypeStruct((8, 128), F32)
 
 
-def split_band_kernel(info, rows, token, top, low, mark):
+def split_band_kernel(info, rows, token, top, low, mark, near, near_top, near_low, came, went):
     mark[...] = jnp.zeros((8, 128), F32)
-    for c in range(4):
-        for half in range(2):
-            a, b = split(rows[pl.ds(4 * half + c, 256, stride=8), :])
-            top[c, :, 128 * half : 128 * half + 128] = a
-            low[c, :, 128 * half : 128 * half + 128] = b
+    copies = []
+    for i in range(4):
+        part = pl.ds(2048 * i, 2048)
+        copies.append(pltpu.make_async_copy(rows.at[part], near.at[part], came.at[i]))
+        copies[i].start()
+    sent = []
+    for i in range(4):
+        copies[i].wait()
+        part = slice(256 * i, 256 * i + 256)
+        for c in range(4):
+            for half in range(2):
+                a, b = split(near[pl.ds(2048 * i + 4 * half + c, 256, stride=8), :])
+                at = slice(256 * c + 128 * half, 256 * c + 128 * half + 128)
+                near_top[part, at] = a
+                near_low[part, at] = b
+        part = pl.ds(256 * i, 256)
+        for j, (here, there) in enumerate(((near_top, top), (near_low, low))):
+            sent.append(pltpu.make_async_copy(here.at[part], there.at[part], went.at[j, i]))
+            sent[-1].start()
+    for copy in sent:
+        copy.wait()
 
 
 def split_band(info, band_rows, token):
     view = band_rows.reshape(NB, 4, 2, 128).transpose(0, 2, 1, 3).reshape(8 * NB, 128)
-    spec = pl.BlockSpec((4, 256, 256), lambda i, s: (0, i, 0))
     return call(
         split_band_kernel,
         "split_band",
-        4,
-        info,
-        (view, token),
-        [pl.BlockSpec((2048, 128), lambda i, s: (i, 0)), ANY],
-        [spec, spec, whole(8, 128)],
-        [pltpu.HBM((4, NB, 256), BF16)] * 2 + [TOKEN],
+        1,
+        info,
+        (*far(view), token),
+        [ANY] * 2,
+        [ANY] * 2 + [whole(8, 128)],
+        [pltpu.HBM((NB, NB), BF16)] * 2 + [TOKEN],
         12,
+        [
+            pltpu.VMEM((8 * NB, 128), F32),
+            pltpu.VMEM((NB, NB), BF16),
+            pltpu.VMEM((NB, NB), BF16),
+            pltpu.SemaphoreType.DMA((4,)),
+            pltpu.SemaphoreType.DMA((2, 4)),
+        ],
     )
 
 
@@ -149,105 +173,115 @@
 
 def solve_kernel(info, *refs):
     pieces, inverse = refs[:4], refs[4]
-    keep, send, got, top, low, full = refs[6:]
-    step = pl.program_id(0)
+    keep, send, got, near, full, done = refs[6:]
+    copies = []
+    for i in range(4):
+        part = (pl.ds(0, 256 * (i + 1)), pl.ds(256 * i, 256))
+        copies.append(pltpu.make_async_copy(inverse.at[part], near.at[part], done.at[i]))
+        copies[i].start()
     x, core = info[1], info[3]
-
-    @pl.when(step == 0)
-    def _():
-        for s in range(NX):
-            got[x ^ s] = pieces[s][...]
-        x0 = info[0] % (NX * NZ * NC) // (NZ * NC)
-        high = x0 & 2
-        sign_high = jnp.where(high == 0, 1.0, -1.0).astype(F32)
-        sign_low = jnp.where((x0 & 1) == 0, 1.0, -1.0).astype(F32)
-        level = [
-            got[high | p, 32:33, :] * (got[p, :32, :] + sign_high * got[p + 2, :32, :])
-            for p in range(2)
-        ]
-        top[...], low[...] = split(
-            got[x0, 33:34, :] * (0.5 * (level[0] + sign_low * level[1]))
+    for s in range(NX):
+        got[x ^ s] = pieces[s][...]
+    x0 = info[0] % (NX * NZ * NC) // (NZ * NC)
+    high = x0 & 2
+    sign_high = jnp.where(high == 0, 1.0, -1.0).astype(F32)
+    sign_low = jnp.where((x0 & 1) == 0, 1.0, -1.0).astype(F32)
+    level = [
+        got[high | p, 32:33, :] * (got[p, :32, :] + sign_high * got[p + 2, :32, :])
+        for p in range(2)
+    ]
+    top, low = split(got[x0, 33:34, :] * (0.5 * (level[0] + sign_low * level[1])))
+    for i in range(4):
+        depth, at = 256 * (i + 1), slice(256 * i, 256 * i + 256)
+        copies[i].wait()
+        a, b = split(near[:depth, at])
+        full[:, at] = (
+            product(top[:, :depth], b) + product(low[:, :depth], a) + product(top[:, :depth], a)
         )
-
-    for i in range(4):
-
-        @pl.when(step == i)
-        def _():
-            depth = 256 * (i + 1)
-            a, b = split(inverse[:depth, :])
-            full[...] = (
-                product(top[:, :depth], b)
-                + product(low[:, :depth], a)
-                + product(top[:, :depth], a)
-            )
-
     keep[...] = full[pl.ds(pl.multiple_of(HALF * core, HALF), HALF), :]
     send[...] = full[pl.ds(pl.multiple_of(HALF * (1 - core), HALF), HALF), :]
 
 
 def solve(info, pieces, inverse, token):
-    part = pl.BlockSpec((HALF, 256), lambda i, s: (0, i))
     return call(
         solve_kernel,
         "solve",
-        4,
+        1,
         info,
         (*pieces, *far(inverse), token),
-        [whole(40, NB)] * NX + [pl.BlockSpec((NB, 256), lambda i, s: (0, i)), ANY],
-        [part] * 2,
+        [whole(40, NB)] * NX + [ANY] * 2,
+        [whole(HALF, NB)] * 2,
         [jax.ShapeDtypeStruct((HALF, NB), F32)] * 2,
         12,
         [
             pltpu.VMEM((NX, 40, NB), F32),
-            pltpu.VMEM((32, NB), BF16),
-            pltpu.VMEM((32, NB), BF16),
-            pltpu.VMEM((32, 256), F32),
+            pltpu.VMEM((NB, NB), F32),
+            pltpu.VMEM((32, NB), F32),
+            pltpu.SemaphoreType.DMA((4,)),
         ],
+        70 * 10**9,
     )
 
 
 def update_kernel(n, info, *refs):
     own, other = refs[:n], refs[n : 2 * n]
-    top, low = refs[2 * n : 2 * n + 2]
+    far_top, far_low = refs[2 * n : 2 * n + 2]
     outs, mine = refs[2 * n + 3 : 3 * n + 3], refs[3 * n + 3]
-    left = refs[3 * n + 4]
-    rows = 128 * n
-
-    @pl.when(pl.program_id(0) == 0)
-    def _():
-        x, core = info[1], info[3]
-        for t in range(NX):
-            for h in range(NC):
-                base = 32 * (x ^ t) + HALF * (core ^ h)
-                for s in range(n):
-                    piece = (other if h else own)[s][HALF * t : HALF * t + HALF, :]
-                    a, b = split(piece)
-                    left[pl.ds(pl.multiple_of(128 * s + base, HALF), HALF), :] = a
-                    left[pl.ds(pl.multiple_of(rows + 128 * s + base, HALF), HALF), :] = b
-                    if s == 0:
-                        mine[pl.ds(pl.multiple_of(base, HALF), HALF), :] = piece
-
-    both = product(left[...], top[0])
-    done = product(left[:rows, :], low[0]) + both[rows:] + both[:rows]
-    for s in range(n):
-        outs[s][...] = done[128 * s : 128 * s + 128]
-
-
-def update(info, own, other, top, low, token):
+    left_top, left_low, top, low, done = refs[3 * n + 4 :]
+    copies = []
+    for c in range(2):
+        at = (slice(None), pl.ds(512 * c, 512))
+        copies.append(
+            [
+                pltpu.make_async_copy(far_top.at[at], top.at[at], done.at[0, c]),
+                pltpu.make_async_copy(far_low.at[at], low.at[at], done.at[1, c]),
+            ]
+        )
+        for copy in copies[c]:
+            copy.start()
+    x, core = info[1], info[3]
+    for t in range(NX):
+        for h in range(NC):
+            base = 32 * (x ^ t) + HALF * (core ^ h)
+            for s in range(n):
+                piece = (other if h else own)[s][HALF * t : HALF * t + HALF, :]
+                at = pl.ds(pl.multiple_of(128 * s + base, HALF), HALF)
+                left_top[at, :], left_low[at, :] = split(piece)
+                if s == 0:
+                    mine[pl.ds(pl.multiple_of(base, HALF), HALF), :] = piece
+    for c in range(2):
+        for copy in copies[c]:
+            copy.wait()
+        at = slice(512 * c, 512 * c + 512)
+        result = (
+            product(left_top[...], low[:, at])
+            + product(left_low[...], top[:, at])
+            + product(left_top[...], top[:, at])
+        )
+        for s in range(n):
+            outs[s][:, at] = result[128 * s : 128 * s + 128]
+
+
+def update(info, own, other, top, low, token, hint):
     n = len(own)
-    band = pl.BlockSpec((1, NB, 256), lambda i, s: (i, 0, 0))
     return call(
         functools.partial(update_kernel, n),
         "update",
-        4,
+        1,
         info,
         (*own, *other, *far(top, low), token),
-        [whole(64, NB)] * (2 * n) + [band] * 2 + [ANY],
-        [pl.BlockSpec((128, 256), lambda i, s: (0, i))] * n + [whole(128, NB)],
+        [whole(64, NB)] * (2 * n) + [ANY] * 3,
+        [whole(128, NB)] * (n + 1),
         [jax.ShapeDtypeStruct((128, NB), F32)] * (n + 1),
-        12,
-        [pltpu.VMEM((256 * n, NB), BF16)],
-        1,
+        20,
+        [
+            pltpu.VMEM((128 * n, NB), BF16),
+            pltpu.VMEM((128 * n, NB), BF16),
+            pltpu.VMEM((NB, NB), BF16),
+            pltpu.VMEM((NB, NB), BF16),
+            pltpu.SemaphoreType.DMA((2, 2)),
+        ],
+        hint,
     )
 
 
@@ -283,11 +317,14 @@
     )
 
 
+def block_index(info, step):
+    return ((info[1] ^ step) * NX + info[1]) * (NZ * NC) + info[2] * NC + info[3]
+
+
 def last_kernel(info, *refs):
     moved, mine, parts, out = refs[:4], refs[4], refs[5:9], refs[9]
-    start, x, z, core, y = [info[i] for i in range(5)]
     step = pl.program_id(0)
-    index = (x ^ step) * (NX * NZ * NC) + (x * NZ + z) * NC + core
+    start, index = info[0], block_index(info, step)
 
     for s in range(NX):
 
@@ -298,7 +335,7 @@
         @pl.when((step == s) & (index > start))
         def _():
             for q in range(NY):
-                at = pl.ds(pl.multiple_of(256 * (y ^ q), 256), 256)
+                at = pl.ds(pl.multiple_of(256 * (info[4] ^ q), 256), 256)
                 out[0, at, :] = moved[s][at, :] - parts[q][...].T
 
     @pl.when(index == start)
@@ -338,7 +375,7 @@
     message = prep(info, right_sides, butterfly_diagonals)
     pieces = [flip_x(message[s], s) for s in range(NX)]
     top, low, ready = split_band(info, band_rows, message[0])
-    mixed = exchange_x(after(right_sides, (pieces, ready)))
+    mixed = exchange_x(after(right_sides, ready))
 
     half, other_half = solve(info, pieces, diag_inverse, ready)
     half = jnp.where(core == core0, half, other_core(other_half))
@@ -350,14 +387,17 @@
     half = jnp.where(away >= 4, flip_z(half, 6), half)
 
     line = jnp.concatenate([half] + [flip_x(half, t) for t in range(1, NX)], axis=0)
-    own = [flip_y(line, s) for s in range(NY)]
     *blocks, mixed_done = mid(info, mixed, pieces, line)
     moved = [flip_x(v, s) for s, v in enumerate(blocks)]
 
-    other = [other_core(after(v, mixed_done)) for v in own[1:]]
-    one, two, three, token = update(info, own[1:], other, top, low, mixed_done)
-    rest = after(own[0], moved)
-    zero, mine = update(info, [rest], [other_core(rest)], top, low, token)
+    one, three = flip_y(line, 1), flip_y(line, 3)
+    two = flip_y(after(line, (one, three, mixed_done)), 2)
+    cross = [other_core(after(v, mixed_done)) for v in (one, three)]
+    one, three, token = update(info, [one, three], cross, top, low, mixed_done, 1)
+    two = after(two, token)
+    two, token = update(info, [two], [other_core(two)], top, low, token, 1)
+    line = after(line, moved)
+    zero, mine = update(info, [line], [other_core(line)], top, low, token, OWN_HINT)
     parts = [zero, flip_y(one, 1), flip_y(two, 2), flip_y(three, 3)]
     return last(info, moved, mine, parts)
 

time: 110 us -> 99.9 us (0.908)
  waiting for transfers between devices: 39.4 us -> 28.6 us
  starting transfers between devices: 40.6 us -> 43.1 us
  local copies, waits for them, and re-layouts: 2.29 us -> 0.1 us
    ppermute x6, waiting for transfers between devices: 10.4 us -> 4.62 us  [flip_y(): return lax.ppermute(v, 'rhs', [(i, i ^ m) for i in range(NY)]) if m else v]
    ppermute x9, waiting for transfers between devices: 20 us -> 14.8 us  [flip_x(): lax.ppermute(v, 'rows', row_perm(lambda x, z, c: (x ^ m, z, c)))]
    ppermute x5, starting transfers between devices: 5.84 us -> 10.5 us  [other_core(): return lax.ppermute(v, 'rows', row_perm(lambda x, z, c: (x, z, 1 - c)))]
    ppermute x6, starting transfers between devices: 10.3 us -> 7.14 us  [flip_y(): return lax.ppermute(v, 'rhs', [(i, i ^ m) for i in range(NY)]) if m else v]
    unnamed x10 -> x8, local copies, waits for them, and re-layouts: 2.2 us -> 0.02 us
    pallas_call x7 -> x8, Pallas kernels: 26.6 us -> 27.1 us  [call(): pl.pallas_call(body, grid_spec=pltpu.PrefetchScalarGridSpec(num_scalar_pr...]
  transfers between devices with their start and end apart: 25 -> 25, of which waited for: 14 -> 14; matrix products, arithmetic and copies ran while one was open for 0% -> 0% of each run, Pallas kernels for 19% -> 21%
where the time goes in v3:
time: 99.9 us; the launch traced here: 99.7 us
  starting transfers between devices  43.1 us (43%)
  waiting for transfers between devices  28.6 us (29%)
  Pallas kernels  27.1 us (27%)
    pallas_call x8, Pallas kernels, call(): pl.pallas_call(body, grid_spec=pltpu.PrefetchScalarGridSpec(num_scalar_pr...  27.1 us
    ppermute x9, waiting for transfers between devices, flip_x(): lax.ppermute(v, 'rows', row_perm(lambda x, z, c: (x ^ m, z, c)))  14.8 us
    ppermute x9, starting transfers between devices, flip_x(): lax.ppermute(v, 'rows', row_perm(lambda x, z, c: (x ^ m, z, c)))  11.8 us
    ppermute x5, starting transfers between devices, other_core(): return lax.ppermute(v, 'rows', row_perm(lambda x, z, c: (x, z, 1 - c)))  10.5 us
    ppermute x4, starting transfers between devices, flip_z(): return lax.ppermute(v, 'rows', row_perm(lambda x, z, c: (x, z ^ m, c)))  9.73 us
    ppermute x6, starting transfers between devices, flip_y(): return lax.ppermute(v, 'rhs', [(i, i ^ m) for i in range(NY)]) if m else v  7.14 us
    ppermute x4, waiting for transfers between devices, flip_z(): return lax.ppermute(v, 'rows', row_perm(lambda x, z, c: (x, z ^ m, c)))  6.97 us
    ppermute x6, waiting for transfers between devices, flip_y(): return lax.ppermute(v, 'rhs', [(i, i ^ m) for i in range(NY)]) if m else v  4.62 us
  transfers between devices with their start and end apart: 25, of which 14 were waited for; matrix products, arithmetic and copies ran while one was open for 0% of the time, Pallas kernels for 21%

profile of v3, /device:TPU:1, one launch (start us, length us, event | category | flops | bytes accessed | tf_op | source)
XLA Modules:
  0.0 99.7 jit_solution(6479738354496013808)
XLA Ops:
  0.7 0.1 stack.19.info
  0.7 2.8 %prep.1 = (f32[40,1024]{1,0:T(8,128)S(1)}, f32[40,1024]{1,0:T(8,128)S(1)}, f32[40,1024]{1,0:T(8,128)S(1)}, f32[40,1024]{1,0:T(8,128)S(1)}) custom-call(s32[5]{0:T(128)S(1)} %stack.19.info, f32[4,1024,128]{2,1,0:T(8,128)} %slab.1, f32[2,4,1024]{2,1,0:T(4,128)} %diag.1), custom_call_target="tpu_custom_call" | custom-call | tf_op jit(solution)/shard_map/prep/pallas_call | solution.py:67
  3.6 0.0 copy-start
  3.6 2.1 %collective-permute-start = (f32[40,1024]{1,0:T(8,128)S(1)}, f32[40,1024]{1,0:T(8,128)S(1)}, u32[]{:S(2)}, u32[]{:S(2)}) collective-permute-start(f32[40,1024]{1,0:T(8,128)S(1)} %get-tuple-element.35), channel_id=1, source_target_pairs={{0,64},{4,68},{8,72},{12,76},{16,80},{20,84},{24,88},{28,92},{32,9... | collective-permute-start | bytes 491528 | tf_op jit(solution)/shard_map/ppermute | solution.py:28
  5.7 2.5 %collective-permute-start.1 = (f32[40,1024]{1,0:T(8,128)S(1)}, f32[40,1024]{1,0:T(8,128)S(1)}, u32[]{:S(2)}, u32[]{:S(2)}) collective-permute-start(f32[40,1024]{1,0:T(8,128)S(1)} %get-tuple-element.36), channel_id=1, source_target_pairs={{0,128},{4,132},{8,136},{12,140},{16,144},{20,148},{24,152},{28,15... | collective-permute-start | bytes 491528 | tf_op jit(solution)/shard_map/ppermute | solution.py:28
  8.2 0.0 collective-permute-start.2
  8.2 4.2 %split_band.1 = (bf16[1024,1024]{1,0:T(8,128)(2,1)}, bf16[1024,1024]{1,0:T(8,128)(2,1)}, f32[8,128]{1,0:T(8,128)S(1)}) custom-call(s32[5]{0:T(128)S(1)} %stack.19.info, f32[8192,128]{1,0:T(8,128)} %bitcast.13, f32[40,1024]{1,0:T(8,128)S(1)} %get-tuple-element.32.token.refs_0_.refs_1_), custom_call_target="tpu_custom_call" | custom-call | tf_op jit(solution)/shard_map/split_band/pallas_call | solution.py:67
  12.5 3.9 %all-to-all-start = ((f32[4,1024,128]{2,1,0:T(8,128)}), f32[4,1024,128]{2,1,0:T(8,128)S(1)}, u32[]{:S(2)}, u32[]{:S(2)}) async-start(f32[4,1024,128]{2,1,0:T(8,128)} %slab.1), calls=%async_computation | async-start | bytes 4194304 | tf_op jit(solution)/shard_map/all_to_all | solution.py:43
  16.4 0.0 collective-permute-done.refs_1_.refs_2_
  16.4 0.0 collective-permute-done.1.refs_2_.refs_3_
  16.4 0.0 copy-start.2
  16.4 1.6 %collective-permute-done.2.refs_3_.refs_4_ = f32[40,1024]{1,0:T(8,128)S(1)} collective-permute-done((f32[40,1024]{1,0:T(8,128)S(1)}, f32[40,1024]{1,0:T(8,128)S(1)}, u32[]{:S(2)}, u32[]{:S(2)}) %collective-permute-start.2) | collective-permute-done | bytes 163872 | tf_op jit(solution)/shard_map/ppermute | solution.py:28
  18.0 0.0 copy-done
  18.0 3.0 %solve.1 = (f32[16,1024]{1,0:T(8,128)S(1)}, f32[16,1024]{1,0:T(8,128)S(1)}) custom-call(s32[5]{0:T(128)S(1)} %stack.19.info, f32[40,1024]{1,0:T(8,128)S(1)} %get-tuple-element.32.token.refs_0_.refs_1_, f32[40,1024]{1,0:T(8,128)S(1)} %collective-permute-done.refs_1_.refs_2_, f32[40,1024]{1,0:T(8,128)S(1)} %collective-permute-done.1.refs_2_.refs_3_, ...), custom_call_target="tpu_custom_call" | custom-call | flops 70000001024 | bytes 1048576 | tf_op jit(solution)/shard_map/solve/pallas_call | solution.py:67
  21.0 0.0 copy-done.1
  21.0 0.0 copy-done.2
  21.0 1.6 %collective-permute-start.3 = (f32[16,1024]{1,0:T(8,128)S(1)}, f32[16,1024]{1,0:T(8,128)S(1)}, u32[]{:S(2)}, u32[]{:S(2)}) collective-permute-start(f32[16,1024]{1,0:T(8,128)S(1)} %get-tuple-element.39), channel_id=1, source_target_pairs={{0,4},{4,0},{8,12},{12,8},{16,20},{20,16},{24,28},{28,24},{32,36},... | collective-permute-start | bytes 196616 | tf_op jit(solution)/shard_map/ppermute | solution.py:47
  22.6 0.9 collective-permute-done.3
  23.6 1.5 %collective-permute-start.6 = (f32[16,1024]{1,0:T(8,128)S(1)}, f32[16,1024]{1,0:T(8,128)S(1)}, u32[]{:S(2)}, u32[]{:S(2)}) collective-permute-start(f32[16,1024]{1,0:T(8,128)S(1)} %broadcast_select_fusion), channel_id=1, source_target_pairs={{0,8},{4,12},{8,0},{12,4},{16,24},{20,28},{24,16},{28,20},{32,40},... | collective-permute-start | bytes 196616 | tf_op jit(solution)/shard_map/ppermute | solution.py:32
  25.1 3.0 %collective-permute-start.5 = (f32[16,1024]{1,0:T(8,128)S(1)}, f32[16,1024]{1,0:T(8,128)S(1)}, u32[]{:S(2)}, u32[]{:S(2)}) collective-permute-start(f32[16,1024]{1,0:T(8,128)S(1)} %broadcast_select_fusion), channel_id=1, source_target_pairs={{0,16},{4,20},{8,24},{12,28},{16,0},{20,4},{24,8},{28,12},{32,48},... | collective-permute-start | bytes 196616 | tf_op jit(solution)/shard_map/ppermute | solution.py:32
  28.1 0.0 collective-permute-start.4
  28.1 0.0 collective-permute-done.6
  28.1 2.2 %collective-permute-done.5 = f32[16,1024]{1,0:T(8,128)S(1)} collective-permute-done((f32[16,1024]{1,0:T(8,128)S(1)}, f32[16,1024]{1,0:T(8,128)S(1)}, u32[]{:S(2)}, u32[]{:S(2)}) %collective-permute-start.5) | collective-permute-done | bytes 65568 | tf_op jit(solution)/shard_map/ppermute | solution.py:32
  30.3 2.8 %collective-permute-done.4 = f32[16,1024]{1,0:T(8,128)S(1)} collective-permute-done((f32[16,1024]{1,0:T(8,128)S(1)}, f32[16,1024]{1,0:T(8,128)S(1)}, u32[]{:S(2)}, u32[]{:S(2)}) %collective-permute-start.4) | collective-permute-done | bytes 65568 | tf_op jit(solution)/shard_map/ppermute | solution.py:32
  33.1 5.2 %collective-permute-start.7 = (f32[16,1024]{1,0:T(8,128)S(1)}, f32[16,1024]{1,0:T(8,128)S(1)}, u32[]{:S(2)}, u32[]{:S(2)}) collective-permute-start(f32[16,1024]{1,0:T(8,128)S(1)} %select_select_fusion), channel_id=1, source_target_pairs={{0,48},{4,52},{8,56},{12,60},{16,32},{20,36},{24,40},{28,44},{32,1... | collective-permute-start | bytes 196616 | tf_op jit(solution)/shard_map/ppermute | solution.py:32
  38.3 2.0 %collective-permute-done.7 = f32[16,1024]{1,0:T(8,128)S(1)} collective-permute-done((f32[16,1024]{1,0:T(8,128)S(1)}, f32[16,1024]{1,0:T(8,128)S(1)}, u32[]{:S(2)}, u32[]{:S(2)}) %collective-permute-start.7) | collective-permute-done | bytes 65568 | tf_op jit(solution)/shard_map/ppermute | solution.py:32
  40.3 1.9 %collective-permute-start.10 = (f32[16,1024]{1,0:T(8,128)S(1)}, f32[16,1024]{1,0:T(8,128)S(1)}, u32[]{:S(2)}, u32[]{:S(2)}) collective-permute-start(f32[16,1024]{1,0:T(8,128)S(1)} %broadcast_select_fusion.1), channel_id=1, source_target_pairs={{0,192},{4,196},{8,200},{12,204},{16,208},{20,212},{24,216},{28,22... | collective-permute-start | bytes 196616 | tf_op jit(solution)/shard_map/ppermute | solution.py:28
  42.2 0.3 collective-permute-start.9
  42.5 1.1 %collective-permute-start.8 = (f32[16,1024]{1,0:T(8,128)S(1)}, f32[16,1024]{1,0:T(8,128)S(1)}, u32[]{:S(2)}, u32[]{:S(2)}) collective-permute-start(f32[16,1024]{1,0:T(8,128)S(1)} %broadcast_select_fusion.1), channel_id=1, source_target_pairs={{0,64},{4,68},{8,72},{12,76},{16,80},{20,84},{24,88},{28,92},{32,9... | collective-permute-start | bytes 196616 | tf_op jit(solution)/shard_map/ppermute | solution.py:28
  43.6 1.1 %collective-permute-done.10 = f32[16,1024]{1,0:T(8,128)S(1)} collective-permute-done((f32[16,1024]{1,0:T(8,128)S(1)}, f32[16,1024]{1,0:T(8,128)S(1)}, u32[]{:S(2)}, u32[]{:S(2)}) %collective-permute-start.10) | collective-permute-done | bytes 65568 | tf_op jit(solution)/shard_map/ppermute | solution.py:28
  44.7 2.2 %collective-permute-done.9 = f32[16,1024]{1,0:T(8,128)S(1)} collective-permute-done((f32[16,1024]{1,0:T(8,128)S(1)}, f32[16,1024]{1,0:T(8,128)S(1)}, u32[]{:S(2)}, u32[]{:S(2)}) %collective-permute-start.9) | collective-permute-done | bytes 65568 | tf_op jit(solution)/shard_map/ppermute | solution.py:28
  46.9 0.0 collective-permute-done.8
  46.9 2.8 %collective-permute-start.16 = (f32[64,1024]{1,0:T(8,128)S(1)}, f32[64,1024]{1,0:T(8,128)S(1)}, u32[]{:S(2)}, u32[]{:S(2)}) collective-permute-start(f32[64,1024]{1,0:T(8,128)S(1)} %pad_maximum_fusion.refs_5_.refs_0_), channel_id=1, source_target_pairs={{0,3},{1,2},{2,1},{3,0},{4,7},{5,6},{6,5},{7,4},{8,11},{9,10},{10,... | collective-permute-start | bytes 786440 | tf_op jit(solution)/shard_map/ppermute | solution.py:36
  49.7 0.0 collective-permute-start.15
  49.7 0.0 all-to-all-done.refs_0_
  49.7 3.1 %mid.1 = (f32[1024,128]{1,0:T(8,128)S(1)}, f32[1024,128]{1,0:T(8,128)S(1)}, f32[1024,128]{1,0:T(8,128)S(1)}, f32[1024,128]{1,0:T(8,128)S(1)}, f32[8,128]{1,0:T(8,128)S(1)}) custom-call(s32[5]{0:T(128)S(1)} %stack.19.info, f32[4,1024,128]{2,1,0:T(8,128)S(1)} %all-to-all-done.refs_0_, f32[40,1024]{1,0:T(8,128)} %copy-done, f32[40,1024]{1,0:T(8,128)} %copy-done.1, ...), custom_call_target="tpu_custom_call" | custom-call | flops 10000000000 | bytes 1048576 | tf_op jit(solution)/shard_map/mid/pallas_call | solution.py:67
  52.9 0.6 collective-permute-done.16.refs_1_
  53.5 4.5 %collective-permute-start.19 = (f32[64,1024]{1,0:T(8,128)S(1)}, f32[64,1024]{1,0:T(8,128)S(1)}, u32[]{:S(2)}, u32[]{:S(2)}) collective-permute-start(f32[64,1024]{1,0:T(8,128)S(1)} %collective-permute-done.16.refs_1_), channel_id=1, source_target_pairs={{0,4},{4,0},{8,12},{12,8},{16,20},{20,16},{24,28},{28,24},{32,36},... | collective-permute-start | bytes 786440 | tf_op jit(solution)/shard_map/ppermute | solution.py:47
  57.9 0.0 collective-permute-done.15.refs_0_
  57.9 1.8 %collective-permute-start.18 = (f32[64,1024]{1,0:T(8,128)S(1)}, f32[64,1024]{1,0:T(8,128)S(1)}, u32[]{:S(2)}, u32[]{:S(2)}) collective-permute-start(f32[64,1024]{1,0:T(8,128)S(1)} %collective-permute-done.15.refs_0_), channel_id=1, source_target_pairs={{0,4},{4,0},{8,12},{12,8},{16,20},{20,16},{24,28},{28,24},{32,36},... | collective-permute-start | bytes 786440 | tf_op jit(solution)/shard_map/ppermute | solution.py:47
  59.7 0.3 collective-permute-start.17
  60.1 0.2 collective-permute-start.11
  60.3 2.1 %collective-permute-start.12 = (f32[1024,128]{1,0:T(8,128)S(1)}, f32[1024,128]{1,0:T(8,128)S(1)}, u32[]{:S(2)}, u32[]{:S(2)}) collective-permute-start(f32[1024,128]{1,0:T(8,128)S(1)} %get-tuple-element.42), channel_id=1, source_target_pairs={{0,128},{4,132},{8,136},{12,140},{16,144},{20,148},{24,152},{28,15... | collective-permute-start | bytes 1572872 | tf_op jit(solution)/shard_map/ppermute | solution.py:28
  62.4 0.0 collective-permute-done.19.refs_3_
  62.4 1.5 %collective-permute-start.13 = (f32[1024,128]{1,0:T(8,128)S(1)}, f32[1024,128]{1,0:T(8,128)S(1)}, u32[]{:S(2)}, u32[]{:S(2)}) collective-permute-start(f32[1024,128]{1,0:T(8,128)S(1)} %get-tuple-element.43), channel_id=1, source_target_pairs={{0,192},{4,196},{8,200},{12,204},{16,208},{20,212},{24,216},{28,22... | collective-permute-start | bytes 1572872 | tf_op jit(solution)/shard_map/ppermute | solution.py:28
  64.0 0.0 collective-permute-done.18.refs_2_
  64.0 4.2 %update.3 = (f32[128,1024]{1,0:T(8,128)S(1)}, f32[128,1024]{1,0:T(8,128)S(1)}, f32[128,1024]{1,0:T(8,128)S(1)}) custom-call(s32[5]{0:T(128)S(1)} %stack.19.info, f32[64,1024]{1,0:T(8,128)S(1)} %collective-permute-done.15.refs_0_, f32[64,1024]{1,0:T(8,128)S(1)} %collective-permute-done.16.refs_1_, f32[64,1024]{1,0:T(8,128)S(1)} %collective-permute-done.18.refs_2_, ...), custom_call_target="tpu_custom_call" | custom-call | flops 1 | bytes 1048576 | tf_op jit(solution)/shard_map/update/pallas_call | solution.py:67
  68.1 1.1 %collective-permute-done.17.refs_0_ = f32[64,1024]{1,0:T(8,128)S(1)} collective-permute-done((f32[64,1024]{1,0:T(8,128)S(1)}, f32[64,1024]{1,0:T(8,128)S(1)}, u32[]{:S(2)}, u32[]{:S(2)}) %collective-permute-start.17) | collective-permute-done | bytes 262176 | tf_op jit(solution)/shard_map/ppermute | solution.py:36
  69.2 0.8 collective-permute-start.20
  70.0 1.1 %collective-permute-start.21 = (f32[128,1024]{1,0:T(8,128)S(1)}, f32[128,1024]{1,0:T(8,128)S(1)}, u32[]{:S(2)}, u32[]{:S(2)}) collective-permute-start(f32[128,1024]{1,0:T(8,128)S(1)} %get-tuple-element.56), channel_id=1, source_target_pairs={{0,1},{1,0},{2,3},{3,2},{4,5},{5,4},{6,7},{7,6},{8,9},{9,8},{10,11... | collective-permute-start | bytes 1572872 | tf_op jit(solution)/shard_map/ppermute | solution.py:36
  71.0 0.1 collective-permute-done.20.refs_1_
  71.1 1.3 %collective-permute-start.23 = (f32[128,1024]{1,0:T(8,128)S(1)}, f32[128,1024]{1,0:T(8,128)S(1)}, u32[]{:S(2)}, u32[]{:S(2)}) collective-permute-start(f32[128,1024]{1,0:T(8,128)S(1)} %get-tuple-element.58), channel_id=1, source_target_pairs={{0,3},{1,2},{2,1},{3,0},{4,7},{5,6},{6,5},{7,4},{8,11},{9,10},{10,... | collective-permute-start | bytes 1572872 | tf_op jit(solution)/shard_map/ppermute | solution.py:36
  72.4 3.4 %update.4 = (f32[128,1024]{1,0:T(8,128)S(1)}, f32[128,1024]{1,0:T(8,128)S(1)}) custom-call(s32[5]{0:T(128)S(1)} %stack.19.info, f32[64,1024]{1,0:T(8,128)S(1)} %collective-permute-done.17.refs_0_, f32[64,1024]{1,0:T(8,128)S(1)} %collective-permute-done.20.refs_1_, bf16[1024,1024]{1,0:T(8,128)(2,1)} %get-tuple-element.45.refs_4_.refs_2_, ...), custom_call_target="tpu_custom_call" | custom-call | flops 1 | bytes 1048576 | tf_op jit(solution)/shard_map/update/pallas_call | solution.py:67
  75.8 0.0 collective-permute-done.11.refs_1_
  75.8 1.6 %collective-permute-start.22 = (f32[128,1024]{1,0:T(8,128)S(1)}, f32[128,1024]{1,0:T(8,128)S(1)}, u32[]{:S(2)}, u32[]{:S(2)}) collective-permute-start(f32[128,1024]{1,0:T(8,128)S(1)} %get-tuple-element.57), channel_id=1, source_target_pairs={{0,2},{1,3},{2,0},{3,1},{4,6},{5,7},{6,4},{7,5},{8,10},{9,11},{10,... | collective-permute-start | bytes 1572872 | tf_op jit(solution)/shard_map/ppermute | solution.py:36
  77.5 7.9 %collective-permute-done.12.refs_2_ = f32[1024,128]{1,0:T(8,128)S(1)} collective-permute-done((f32[1024,128]{1,0:T(8,128)S(1)}, f32[1024,128]{1,0:T(8,128)S(1)}, u32[]{:S(2)}, u32[]{:S(2)}) %collective-permute-start.12) | collective-permute-done | bytes 524320 | tf_op jit(solution)/shard_map/ppermute | solution.py:28
  85.4 2.0 %collective-permute-done.13.refs_3_ = f32[1024,128]{1,0:T(8,128)S(1)} collective-permute-done((f32[1024,128]{1,0:T(8,128)S(1)}, f32[1024,128]{1,0:T(8,128)S(1)}, u32[]{:S(2)}, u32[]{:S(2)}) %collective-permute-start.13) | collective-permute-done | bytes 524320 | tf_op jit(solution)/shard_map/ppermute | solution.py:28
  87.4 1.8 %collective-permute-start.14 = (f32[64,1024]{1,0:T(8,128)S(1)}, f32[64,1024]{1,0:T(8,128)S(1)}, u32[]{:S(2)}, u32[]{:S(2)}) collective-permute-start(f32[64,1024]{1,0:T(8,128)S(1)} %pad_maximum_fusion.refs_5_.refs_0_), channel_id=1, source_target_pairs={{0,4},{4,0},{8,12},{12,8},{16,20},{20,16},{24,28},{28,24},{32,36},... | collective-permute-start | bytes 786440 | tf_op jit(solution)/shard_map/ppermute | solution.py:47
  89.2 1.2 %collective-permute-done.14.refs_1_ = f32[64,1024]{1,0:T(8,128)S(1)} collective-permute-done((f32[64,1024]{1,0:T(8,128)S(1)}, f32[64,1024]{1,0:T(8,128)S(1)}, u32[]{:S(2)}, u32[]{:S(2)}) %collective-permute-start.14) | collective-permute-done | bytes 262176 | tf_op jit(solution)/shard_map/ppermute | solution.py:47
  90.4 3.4 %update.5 = (f32[128,1024]{1,0:T(8,128)S(1)}, f32[128,1024]{1,0:T(8,128)S(1)}) custom-call(s32[5]{0:T(128)S(1)} %stack.19.info, f32[64,1024]{1,0:T(8,128)S(1)} %pad_maximum_fusion.refs_5_.refs_0_, f32[64,1024]{1,0:T(8,128)S(1)} %collective-permute-done.14.refs_1_, bf16[1024,1024]{1,0:T(8,128)(2,1)} %get-tuple-element.45.refs_4_.refs_2_, ...), custom_call_target="tpu_custom_call" | custom-call | flops 2000000000 | bytes 1048576 | tf_op jit(solution)/shard_map/update/pallas_call | solution.py:67
  93.8 0.0 collective-permute-done.21.refs_6_
  93.8 2.9 %collective-permute-done.23.refs_8_ = f32[128,1024]{1,0:T(8,128)S(1)} collective-permute-done((f32[128,1024]{1,0:T(8,128)S(1)}, f32[128,1024]{1,0:T(8,128)S(1)}, u32[]{:S(2)}, u32[]{:S(2)}) %collective-permute-start.23) | collective-permute-done | bytes 524320 | tf_op jit(solution)/shard_map/ppermute | solution.py:36
  96.7 0.0 collective-permute-done.22.refs_7_
  96.7 3.0 %last.1 = f32[4,1024,128]{2,1,0:T(8,128)} custom-call(s32[5]{0:T(128)S(1)} %stack.19.info, f32[1024,128]{1,0:T(8,128)S(1)} %get-tuple-element.40.refs_0_, f32[1024,128]{1,0:T(8,128)S(1)} %collective-permute-done.11.refs_1_, f32[1024,128]{1,0:T(8,128)S(1)} %collective-permute-done.12.refs_2_, f32[1024,128]{1,0:T(8,128)S(1)} %collective-permute-done.13.refs_3_, ...), custom_call_target="tpu_custom_call" | custom-call | tf_op jit(solution)/shard_map/last/pallas_call | solution.py:67
  (7 shorter events, 0.1 us)
Async XLA Ops:
  3.6 14.5 %copy-start = (f32[40,1024]{1,0:T(8,128)}, f32[40,1024]{1,0:T(8,128)S(1)}, u32[]{:S(2)}) copy-start(f32[40,1024]{1,0:T(8,128)S(1)} %get-tuple-element.32.token.refs_0_.refs_1_) | copy-start | bytes 491524
  3.6 12.8 %collective-permute-start = (f32[40,1024]{1,0:T(8,128)S(1)}, f32[40,1024]{1,0:T(8,128)S(1)}, u32[]{:S(2)}, u32[]{:S(2)}) collective-permute-start(f32[40,1024]{1,0:T(8,128)S(1)} %get-tuple-element.35), channel_id=1, source_target_pairs={{0,64},{4,68},{8,72},{12,76},{16,80},{20,84},{24,88},{28,92},{32,9... | collective-permute-start | bytes 491528 | tf_op jit(solution)/shard_map/ppermute | solution.py:28
  5.7 10.7 %collective-permute-start.1 = (f32[40,1024]{1,0:T(8,128)S(1)}, f32[40,1024]{1,0:T(8,128)S(1)}, u32[]{:S(2)}, u32[]{:S(2)}) collective-permute-start(f32[40,1024]{1,0:T(8,128)S(1)} %get-tuple-element.36), channel_id=1, source_target_pairs={{0,128},{4,132},{8,136},{12,140},{16,144},{20,148},{24,152},{28,15... | collective-permute-start | bytes 491528 | tf_op jit(solution)/shard_map/ppermute | solution.py:28
  8.2 9.9 %collective-permute-start.2 = (f32[40,1024]{1,0:T(8,128)S(1)}, f32[40,1024]{1,0:T(8,128)S(1)}, u32[]{:S(2)}, u32[]{:S(2)}) collective-permute-start(f32[40,1024]{1,0:T(8,128)S(1)} %get-tuple-element.37), channel_id=1, source_target_pairs={{0,192},{4,196},{8,200},{12,204},{16,208},{20,212},{24,216},{28,22... | collective-permute-start | bytes 491528 | tf_op jit(solution)/shard_map/ppermute | solution.py:28
  12.5 37.3 %all-to-all-start = ((f32[4,1024,128]{2,1,0:T(8,128)}), f32[4,1024,128]{2,1,0:T(8,128)S(1)}, u32[]{:S(2)}, u32[]{:S(2)}) async-start(f32[4,1024,128]{2,1,0:T(8,128)} %slab.1), calls=%async_computation | async-start | bytes 4194304 | tf_op jit(solution)/shard_map/all_to_all | solution.py:43
  16.4 4.6 %copy-start.1 = (f32[40,1024]{1,0:T(8,128)}, f32[40,1024]{1,0:T(8,128)S(1)}, u32[]{:S(2)}) copy-start(f32[40,1024]{1,0:T(8,128)S(1)} %collective-permute-done.refs_1_.refs_2_) | copy-start | bytes 491524
  16.4 4.6 %copy-start.2 = (f32[40,1024]{1,0:T(8,128)}, f32[40,1024]{1,0:T(8,128)S(1)}, u32[]{:S(2)}) copy-start(f32[40,1024]{1,0:T(8,128)S(1)} %collective-permute-done.1.refs_2_.refs_3_) | copy-start | bytes 491524
  18.0 3.0 %copy-start.3 = (f32[40,1024]{1,0:T(8,128)}, f32[40,1024]{1,0:T(8,128)S(1)}, u32[]{:S(2)}) copy-start(f32[40,1024]{1,0:T(8,128)S(1)} %collective-permute-done.2.refs_3_.refs_4_) | copy-start | bytes 491524
  21.0 2.5 %collective-permute-start.3 = (f32[16,1024]{1,0:T(8,128)S(1)}, f32[16,1024]{1,0:T(8,128)S(1)}, u32[]{:S(2)}, u32[]{:S(2)}) collective-permute-start(f32[16,1024]{1,0:T(8,128)S(1)} %get-tuple-element.39), channel_id=1, source_target_pairs={{0,4},{4,0},{8,12},{12,8},{16,20},{20,16},{24,28},{28,24},{32,36},... | collective-permute-start | bytes 196616 | tf_op jit(solution)/shard_map/ppermute | solution.py:47
  23.6 4.5 %collective-permute-start.6 = (f32[16,1024]{1,0:T(8,128)S(1)}, f32[16,1024]{1,0:T(8,128)S(1)}, u32[]{:S(2)}, u32[]{:S(2)}) collective-permute-start(f32[16,1024]{1,0:T(8,128)S(1)} %broadcast_select_fusion), channel_id=1, source_target_pairs={{0,8},{4,12},{8,0},{12,4},{16,24},{20,28},{24,16},{28,20},{32,40},... | collective-permute-start | bytes 196616 | tf_op jit(solution)/shard_map/ppermute | solution.py:32
  25.1 5.2 %collective-permute-start.5 = (f32[16,1024]{1,0:T(8,128)S(1)}, f32[16,1024]{1,0:T(8,128)S(1)}, u32[]{:S(2)}, u32[]{:S(2)}) collective-permute-start(f32[16,1024]{1,0:T(8,128)S(1)} %broadcast_select_fusion), channel_id=1, source_target_pairs={{0,16},{4,20},{8,24},{12,28},{16,0},{20,4},{24,8},{28,12},{32,48},... | collective-permute-start | bytes 196616 | tf_op jit(solution)/shard_map/ppermute | solution.py:32
  28.1 5.0 %collective-permute-start.4 = (f32[16,1024]{1,0:T(8,128)S(1)}, f32[16,1024]{1,0:T(8,128)S(1)}, u32[]{:S(2)}, u32[]{:S(2)}) collective-permute-start(f32[16,1024]{1,0:T(8,128)S(1)} %broadcast_select_fusion), channel_id=1, source_target_pairs={{0,24},{4,28},{8,16},{12,20},{16,8},{20,12},{24,0},{28,4},{32,56},... | collective-permute-start | bytes 196616 | tf_op jit(solution)/shard_map/ppermute | solution.py:32
  33.1 7.2 %collective-permute-start.7 = (f32[16,1024]{1,0:T(8,128)S(1)}, f32[16,1024]{1,0:T(8,128)S(1)}, u32[]{:S(2)}, u32[]{:S(2)}) collective-permute-start(f32[16,1024]{1,0:T(8,128)S(1)} %select_select_fusion), channel_id=1, source_target_pairs={{0,48},{4,52},{8,56},{12,60},{16,32},{20,36},{24,40},{28,44},{32,1... | collective-permute-start | bytes 196616 | tf_op jit(solution)/shard_map/ppermute | solution.py:32
  40.3 4.4 %collective-permute-start.10 = (f32[16,1024]{1,0:T(8,128)S(1)}, f32[16,1024]{1,0:T(8,128)S(1)}, u32[]{:S(2)}, u32[]{:S(2)}) collective-permute-start(f32[16,1024]{1,0:T(8,128)S(1)} %broadcast_select_fusion.1), channel_id=1, source_target_pairs={{0,192},{4,196},{8,200},{12,204},{16,208},{20,212},{24,216},{28,22... | collective-permute-start | bytes 196616 | tf_op jit(solution)/shard_map/ppermute | solution.py:28
  42.2 4.7 %collective-permute-start.9 = (f32[16,1024]{1,0:T(8,128)S(1)}, f32[16,1024]{1,0:T(8,128)S(1)}, u32[]{:S(2)}, u32[]{:S(2)}) collective-permute-start(f32[16,1024]{1,0:T(8,128)S(1)} %broadcast_select_fusion.1), channel_id=1, source_target_pairs={{0,128},{4,132},{8,136},{12,140},{16,144},{20,148},{24,152},{28,15... | collective-permute-start | bytes 196616 | tf_op jit(solution)/shard_map/ppermute | solution.py:28
  42.5 4.4 %collective-permute-start.8 = (f32[16,1024]{1,0:T(8,128)S(1)}, f32[16,1024]{1,0:T(8,128)S(1)}, u32[]{:S(2)}, u32[]{:S(2)}) collective-permute-start(f32[16,1024]{1,0:T(8,128)S(1)} %broadcast_select_fusion.1), channel_id=1, source_target_pairs={{0,64},{4,68},{8,72},{12,76},{16,80},{20,84},{24,88},{28,92},{32,9... | collective-permute-start | bytes 196616 | tf_op jit(solution)/shard_map/ppermute | solution.py:28
  46.9 6.6 %collective-permute-start.16 = (f32[64,1024]{1,0:T(8,128)S(1)}, f32[64,1024]{1,0:T(8,128)S(1)}, u32[]{:S(2)}, u32[]{:S(2)}) collective-permute-start(f32[64,1024]{1,0:T(8,128)S(1)} %pad_maximum_fusion.refs_5_.refs_0_), channel_id=1, source_target_pairs={{0,3},{1,2},{2,1},{3,0},{4,7},{5,6},{6,5},{7,4},{8,11},{9,10},{10,... | collective-permute-start | bytes 786440 | tf_op jit(solution)/shard_map/ppermute | solution.py:36
  49.7 8.2 %collective-permute-start.15 = (f32[64,1024]{1,0:T(8,128)S(1)}, f32[64,1024]{1,0:T(8,128)S(1)}, u32[]{:S(2)}, u32[]{:S(2)}) collective-permute-start(f32[64,1024]{1,0:T(8,128)S(1)} %pad_maximum_fusion.refs_5_.refs_0_), channel_id=1, source_target_pairs={{0,1},{1,0},{2,3},{3,2},{4,5},{5,4},{6,7},{7,6},{8,9},{9,8},{10,11... | collective-permute-start | bytes 786440 | tf_op jit(solution)/shard_map/ppermute | solution.py:36
  53.5 8.9 %collective-permute-start.19 = (f32[64,1024]{1,0:T(8,128)S(1)}, f32[64,1024]{1,0:T(8,128)S(1)}, u32[]{:S(2)}, u32[]{:S(2)}) collective-permute-start(f32[64,1024]{1,0:T(8,128)S(1)} %collective-permute-done.16.refs_1_), channel_id=1, source_target_pairs={{0,4},{4,0},{8,12},{12,8},{16,20},{20,16},{24,28},{28,24},{32,36},... | collective-permute-start | bytes 786440 | tf_op jit(solution)/shard_map/ppermute | solution.py:47
  57.9 6.0 %collective-permute-start.18 = (f32[64,1024]{1,0:T(8,128)S(1)}, f32[64,1024]{1,0:T(8,128)S(1)}, u32[]{:S(2)}, u32[]{:S(2)}) collective-permute-start(f32[64,1024]{1,0:T(8,128)S(1)} %collective-permute-done.15.refs_0_), channel_id=1, source_target_pairs={{0,4},{4,0},{8,12},{12,8},{16,20},{20,16},{24,28},{28,24},{32,36},... | collective-permute-start | bytes 786440 | tf_op jit(solution)/shard_map/ppermute | solution.py:47
  59.7 9.4 %collective-permute-start.17 = (f32[64,1024]{1,0:T(8,128)S(1)}, f32[64,1024]{1,0:T(8,128)S(1)}, u32[]{:S(2)}, u32[]{:S(2)}) collective-permute-start(f32[64,1024]{1,0:T(8,128)S(1)} %pad_maximum_fusion.refs_5_.refs_0_), channel_id=1, source_target_pairs={{0,2},{1,3},{2,0},{3,1},{4,6},{5,7},{6,4},{7,5},{8,10},{9,11},{10,... | collective-permute-start | bytes 786440 | tf_op jit(solution)/shard_map/ppermute | solution.py:36
  60.1 15.7 %collective-permute-start.11 = (f32[1024,128]{1,0:T(8,128)S(1)}, f32[1024,128]{1,0:T(8,128)S(1)}, u32[]{:S(2)}, u32[]{:S(2)}) collective-permute-start(f32[1024,128]{1,0:T(8,128)S(1)} %get-tuple-element.41), channel_id=1, source_target_pairs={{0,64},{4,68},{8,72},{12,76},{16,80},{20,84},{24,88},{28,92},{32,9... | collective-permute-start | bytes 1572872 | tf_op jit(solution)/shard_map/ppermute | solution.py:28
  60.3 25.1 %collective-permute-start.12 = (f32[1024,128]{1,0:T(8,128)S(1)}, f32[1024,128]{1,0:T(8,128)S(1)}, u32[]{:S(2)}, u32[]{:S(2)}) collective-permute-start(f32[1024,128]{1,0:T(8,128)S(1)} %get-tuple-element.42), channel_id=1, source_target_pairs={{0,128},{4,132},{8,136},{12,140},{16,144},{20,148},{24,152},{28,15... | collective-permute-start | bytes 1572872 | tf_op jit(solution)/shard_map/ppermute | solution.py:28
  62.4 25.0 %collective-permute-start.13 = (f32[1024,128]{1,0:T(8,128)S(1)}, f32[1024,128]{1,0:T(8,128)S(1)}, u32[]{:S(2)}, u32[]{:S(2)}) collective-permute-start(f32[1024,128]{1,0:T(8,128)S(1)} %get-tuple-element.43), channel_id=1, source_target_pairs={{0,192},{4,196},{8,200},{12,204},{16,208},{20,212},{24,216},{28,22... | collective-permute-start | bytes 1572872 | tf_op jit(solution)/shard_map/ppermute | solution.py:28
  69.2 1.9 %collective-permute-start.20 = (f32[64,1024]{1,0:T(8,128)S(1)}, f32[64,1024]{1,0:T(8,128)S(1)}, u32[]{:S(2)}, u32[]{:S(2)}) collective-permute-start(f32[64,1024]{1,0:T(8,128)S(1)} %collective-permute-done.17.refs_0_), channel_id=1, source_target_pairs={{0,4},{4,0},{8,12},{12,8},{16,20},{20,16},{24,28},{28,24},{32,36},... | collective-permute-start | bytes 786440 | tf_op jit(solution)/shard_map/ppermute | solution.py:47
  70.0 23.8 %collective-permute-start.21 = (f32[128,1024]{1,0:T(8,128)S(1)}, f32[128,1024]{1,0:T(8,128)S(1)}, u32[]{:S(2)}, u32[]{:S(2)}) collective-permute-start(f32[128,1024]{1,0:T(8,128)S(1)} %get-tuple-element.56), channel_id=1, source_target_pairs={{0,1},{1,0},{2,3},{3,2},{4,5},{5,4},{6,7},{7,6},{8,9},{9,8},{10,11... | collective-permute-start | bytes 1572872 | tf_op jit(solution)/shard_map/ppermute | solution.py:36
  71.1 25.6 %collective-permute-start.23 = (f32[128,1024]{1,0:T(8,128)S(1)}, f32[128,1024]{1,0:T(8,128)S(1)}, u32[]{:S(2)}, u32[]{:S(2)}) collective-permute-start(f32[128,1024]{1,0:T(8,128)S(1)} %get-tuple-element.58), channel_id=1, source_target_pairs={{0,3},{1,2},{2,1},{3,0},{4,7},{5,6},{6,5},{7,4},{8,11},{9,10},{10,... | collective-permute-start | bytes 1572872 | tf_op jit(solution)/shard_map/ppermute | solution.py:36
  75.8 20.9 %collective-permute-start.22 = (f32[128,1024]{1,0:T(8,128)S(1)}, f32[128,1024]{1,0:T(8,128)S(1)}, u32[]{:S(2)}, u32[]{:S(2)}) collective-permute-start(f32[128,1024]{1,0:T(8,128)S(1)} %get-tuple-element.57), channel_id=1, source_target_pairs={{0,2},{1,3},{2,0},{3,1},{4,6},{5,7},{6,4},{7,5},{8,10},{9,11},{10,... | collective-permute-start | bytes 1572872 | tf_op jit(solution)/shard_map/ppermute | solution.py:36
  87.4 3.0 %collective-permute-start.14 = (f32[64,1024]{1,0:T(8,128)S(1)}, f32[64,1024]{1,0:T(8,128)S(1)}, u32[]{:S(2)}, u32[]{:S(2)}) collective-permute-start(f32[64,1024]{1,0:T(8,128)S(1)} %pad_maximum_fusion.refs_5_.refs_0_), channel_id=1, source_target_pairs={{0,4},{4,0},{8,12},{12,8},{16,20},{20,16},{24,28},{28,24},{32,36},... | collective-permute-start | bytes 786440 | tf_op jit(solution)/shard_map/ppermute | solution.py:47

commit v4 on v3

--- a/solution.py
+++ b/solution.py
@@ -9,7 +9,8 @@
 NX, NZ, NC, NY = 4, 8, 2, 4
 NB = 1024
 HALF = 16
-OWN_HINT = 2 * 10**9
+OWN_HINT = 3 * 10**9
+MARK_HINT = 2 * 10**9
 F32 = jnp.float32
 BF16 = jnp.bfloat16
 
@@ -81,34 +82,51 @@
     )(info, *args)
 
 
-def prep_kernel(info, slab, diag, *refs):
-    outs, flipped = refs[:NX], refs[NX]
-    cycle, x = info[0] // (NX * NZ * NC), info[1]
-    flipped[...] = slab[0].T
+def prep_kernel(start, slabs, diags, *refs):
+    outs, (slab, diag, came) = refs[:NX], refs[NX:]
+    cycle, x = start[0] // (NX * NZ * NC), lax.axis_index("rows") // (NZ * NC)
+    copies = [pltpu.make_async_copy(diags, diag, came.at[4])]
+    for i in range(4):
+        part = pl.ds(256 * i, 256)
+        copies.append(pltpu.make_async_copy(slabs.at[cycle, part], slab.at[part], came.at[i]))
+    for copy in copies:
+        copy.start()
+    copies[0].wait()
     for s in range(NX):
         to = x ^ s
-        outs[s][:32, :] = flipped[pl.ds(pl.multiple_of(32 * to, 32), 32), :]
         for level in range(2):
             outs[s][32 + level : 33 + level, :] = diag[level, pl.ds(cycle, 1), :]
             outs[s][34 + level : 35 + level, :] = diag[level, pl.ds(to, 1), :]
-        outs[s][36:40, :] = jnp.zeros((4, 256), F32)
-
-
-def prep(info, right_sides, diag):
+        outs[s][36:40, :] = jnp.zeros((4, NB), F32)
+    for i in range(4):
+        copies[i + 1].wait()
+        at = slice(256 * i, 256 * i + 256)
+        flipped = slab[at, :].T
+        for to in range(NX):
+            rows = flipped[32 * to : 32 * to + 32]
+            for s in range(NX):
+
+                @pl.when(to ^ s == x)
+                def _():
+                    outs[s][:32, at] = rows
+
+
+def prep(start, right_sides, diag):
     return call(
         prep_kernel,
         "prep",
-        4,
-        info,
+        1,
+        start,
         far(right_sides, diag),
-        [
-            pl.BlockSpec((1, 256, 128), lambda i, s: (s[0] // (NX * NZ * NC), i, 0)),
-            pl.BlockSpec((2, 4, 256), lambda i, s: (0, 0, i)),
-        ],
-        [pl.BlockSpec((40, 256), lambda i, s: (0, i))] * NX,
+        [ANY] * 2,
+        [whole(40, NB)] * NX,
         [jax.ShapeDtypeStruct((40, NB), F32)] * NX,
         12,
-        [pltpu.VMEM((128, 256), F32)],
+        [
+            pltpu.VMEM((NB, 128), F32),
+            pltpu.VMEM((2, 4, NB), F32),
+            pltpu.SemaphoreType.DMA((5,)),
+        ],
     )
 
 
@@ -317,45 +335,59 @@
     )
 
 
+def mark_kernel(info, *refs):
+    refs[-1][...] = jnp.zeros((8, 128), F32)
+
+
+def mark_after(info, values, hint):
+    return call(
+        mark_kernel, "mark", 1, info, values, [ANY] * len(values), whole(8, 128), TOKEN, 4, hint=hint
+    )
+
+
 def block_index(info, step):
     return ((info[1] ^ step) * NX + info[1]) * (NZ * NC) + info[2] * NC + info[3]
 
 
 def last_kernel(info, *refs):
-    moved, mine, parts, out = refs[:4], refs[4], refs[5:9], refs[9]
-    step = pl.program_id(0)
-    start, index = info[0], block_index(info, step)
-
+    moved, mine, parts, out, block, went = refs[:4], refs[4], refs[5:9], *refs[10:]
+    start, copies = info[0], []
     for s in range(NX):
-
-        @pl.when((step == s) & (index < start))
+        index = block_index(info, s)
+
+        @pl.when(index < start)
         def _():
-            out[0] = moved[s][...]
-
-        @pl.when((step == s) & (index > start))
+            block[s] = moved[s][...]
+
+        @pl.when(index > start)
         def _():
+            column = pl.ds(pl.multiple_of(256 * (info[1] ^ s), 256), 256)
             for q in range(NY):
                 at = pl.ds(pl.multiple_of(256 * (info[4] ^ q), 256), 256)
-                out[0, at, :] = moved[s][at, :] - parts[q][...].T
-
-    @pl.when(index == start)
-    def _():
-        out[0] = mine[...].T
-
-
-def last(info, moved, mine, parts):
+                block[s, at, :] = moved[s][at, :] - parts[q][:, column].T
+
+        @pl.when(index == start)
+        def _():
+            block[s] = mine[...].T
+
+        copies.append(pltpu.make_async_copy(block.at[s], out.at[info[1] ^ s], went.at[s]))
+        copies[s].start()
+    for copy in copies:
+        copy.wait()
+
+
+def last(info, moved, mine, parts, token):
     return call(
         last_kernel,
         "last",
-        NX,
+        1,
         info,
-        (*moved, mine, *parts),
-        [whole(NB, 128)] * NX
-        + [whole(128, NB)]
-        + [pl.BlockSpec((128, 256), lambda i, s: (0, s[1] ^ i))] * NY,
-        pl.BlockSpec((1, NB, 128), lambda i, s: (s[1] ^ i, 0, 0)),
-        jax.ShapeDtypeStruct((4, NB, 128), F32),
+        (*moved, mine, *parts, token),
+        [whole(NB, 128)] * NX + [whole(128, NB)] * (NY + 1) + [ANY],
+        ANY,
+        pltpu.HBM((4, NB, 128), F32),
         12,
+        [pltpu.VMEM((4, NB, 128), F32), pltpu.SemaphoreType.DMA((4,))],
     )
 
 
@@ -372,7 +404,7 @@
     z0 = start % (NX * NZ * NC) // NC % NZ
     core0 = start % NC
 
-    message = prep(info, right_sides, butterfly_diagonals)
+    message = prep(band_block, right_sides, butterfly_diagonals)
     pieces = [flip_x(message[s], s) for s in range(NX)]
     top, low, ready = split_band(info, band_rows, message[0])
     mixed = exchange_x(after(right_sides, ready))
@@ -386,20 +418,23 @@
         half = jnp.where(away == m, got[m - 1], half)
     half = jnp.where(away >= 4, flip_z(half, 6), half)
 
-    line = jnp.concatenate([half] + [flip_x(half, t) for t in range(1, NX)], axis=0)
-    *blocks, mixed_done = mid(info, mixed, pieces, line)
+    *blocks, mixed_done = mid(info, mixed, pieces, half)
+    line = [half] + [after(flip_x(half, t), mixed_done) for t in range(1, NX)]
+    line = jnp.concatenate(line, axis=0)
+
+    one, three = flip_y(line, 1), flip_y(line, 3)
+    cross = [other_core(v) for v in (one, three)]
+    two = flip_y(after(line, (one, three)), 2)
+    one, three, token = update(info, [one, three], cross, top, low, mixed_done, 1)
+    blocks[2] = after(blocks[2], token)
     moved = [flip_x(v, s) for s, v in enumerate(blocks)]
-
-    one, three = flip_y(line, 1), flip_y(line, 3)
-    two = flip_y(after(line, (one, three, mixed_done)), 2)
-    cross = [other_core(after(v, mixed_done)) for v in (one, three)]
-    one, three, token = update(info, [one, three], cross, top, low, mixed_done, 1)
     two = after(two, token)
+    token = mark_after(info, [moved[1], moved[3], token], MARK_HINT)
     two, token = update(info, [two], [other_core(two)], top, low, token, 1)
-    line = after(line, moved)
-    zero, mine = update(info, [line], [other_core(line)], top, low, token, OWN_HINT)
-    parts = [zero, flip_y(one, 1), flip_y(two, 2), flip_y(three, 3)]
-    return last(info, moved, mine, parts)
+    zero, mine = update(info, [line], [other_core(line)], top, low, token, 1)
+    one, three = flip_y(one, 1), flip_y(three, 3)
+    token = mark_after(info, [one, three, zero], OWN_HINT)
+    return last(info, moved, mine, [zero, one, flip_y(two, 2), three], token)
 
 
 def solution(mesh):

time: 99.9 us -> 92.3 us (0.924)
  waiting for transfers between devices: 28.6 us -> 25 us
  starting transfers between devices: 43.1 us -> 40 us
  Pallas kernels: 27.1 us -> 25.8 us
    ppermute x9, waiting for transfers between devices: 14.8 us -> 6.46 us  [flip_x(): lax.ppermute(v, 'rows', row_perm(lambda x, z, c: (x ^ m, z, c)))]
    ppermute x6, waiting for transfers between devices: 4.62 us -> 9.86 us  [flip_y(): return lax.ppermute(v, 'rhs', [(i, i ^ m) for i in range(NY)]) if m else v]
    ppermute x6, starting transfers between devices: 7.14 us -> 5.53 us  [flip_y(): return lax.ppermute(v, 'rhs', [(i, i ^ m) for i in range(NY)]) if m else v]
    ppermute x5, starting transfers between devices: 10.5 us -> 9.13 us  [other_core(): return lax.ppermute(v, 'rows', row_perm(lambda x, z, c: (x, z, 1 - c)))]
    pallas_call x8 -> x10, Pallas kernels: 27.1 us -> 25.8 us  [call(): pl.pallas_call(body, grid_spec=pltpu.PrefetchScalarGridSpec(num_scalar_pr...]
  transfers between devices with their start and end apart: 25 -> 25, of which waited for: 14 -> 11; matrix products, arithmetic and copies ran while one was open for 0% -> 0% of each run, Pallas kernels for 21% -> 24%
where the time goes in v4:
time: 92.3 us; the launch traced here: 92 us
  starting transfers between devices  40 us (43%)
  Pallas kernels  25.8 us (28%)
  waiting for transfers between devices  25 us (27%)
  between operations  1 us (1%)
    pallas_call x10, Pallas kernels, call(): pl.pallas_call(body, grid_spec=pltpu.PrefetchScalarGridSpec(num_scalar_pr...  25.8 us
    ppermute x9, starting transfers between devices, flip_x(): lax.ppermute(v, 'rows', row_perm(lambda x, z, c: (x ^ m, z, c)))  11.8 us
    ppermute x6, waiting for transfers between devices, flip_y(): return lax.ppermute(v, 'rhs', [(i, i ^ m) for i in range(NY)]) if m else v  9.86 us
    ppermute x4, starting transfers between devices, flip_z(): return lax.ppermute(v, 'rows', row_perm(lambda x, z, c: (x, z ^ m, c)))  9.63 us
    ppermute x5, starting transfers between devices, other_core(): return lax.ppermute(v, 'rows', row_perm(lambda x, z, c: (x, z, 1 - c)))  9.13 us
    ppermute x4, waiting for transfers between devices, flip_z(): return lax.ppermute(v, 'rows', row_perm(lambda x, z, c: (x, z ^ m, c)))  6.97 us
    ppermute x9, waiting for transfers between devices, flip_x(): lax.ppermute(v, 'rows', row_perm(lambda x, z, c: (x ^ m, z, c)))  6.46 us
    ppermute x6, starting transfers between devices, flip_y(): return lax.ppermute(v, 'rhs', [(i, i ^ m) for i in range(NY)]) if m else v  5.53 us
  transfers between devices with their start and end apart: 25, of which 11 were waited for; matrix products, arithmetic and copies ran while one was open for 0% of the time, Pallas kernels for 24%

profile of v4, /device:TPU:1, one launch (start us, length us, event | category | flops | bytes accessed | tf_op | source)
XLA Modules:
  0.0 92.0 jit_solution(8536738412863962972)
XLA Ops:
  0.7 1.5 %prep.1 = (f32[40,1024]{1,0:T(8,128)S(1)}, f32[40,1024]{1,0:T(8,128)S(1)}, f32[40,1024]{1,0:T(8,128)S(1)}, f32[40,1024]{1,0:T(8,128)S(1)}) custom-call(s32[1]{0:T(128)} %copy.7.start, f32[4,1024,128]{2,1,0:T(8,128)} %slabs.1, f32[2,4,1024]{2,1,0:T(4,128)} %diags.1), custom_call_target="tpu_custom_call" | custom-call | tf_op jit(solution)/shard_map/prep/pallas_call | solution.py:68
  2.2 0.0 copy-start
  2.2 2.1 %collective-permute-start = (f32[40,1024]{1,0:T(8,128)S(1)}, f32[40,1024]{1,0:T(8,128)S(1)}, u32[]{:S(2)}, u32[]{:S(2)}) collective-permute-start(f32[40,1024]{1,0:T(8,128)S(1)} %get-tuple-element.36), channel_id=1, source_target_pairs={{0,64},{4,68},{8,72},{12,76},{16,80},{20,84},{24,88},{28,92},{32,9... | collective-permute-start | bytes 491528 | tf_op jit(solution)/shard_map/ppermute | solution.py:29
  4.3 2.4 %collective-permute-start.1 = (f32[40,1024]{1,0:T(8,128)S(1)}, f32[40,1024]{1,0:T(8,128)S(1)}, u32[]{:S(2)}, u32[]{:S(2)}) collective-permute-start(f32[40,1024]{1,0:T(8,128)S(1)} %get-tuple-element.37), channel_id=1, source_target_pairs={{0,128},{4,132},{8,136},{12,140},{16,144},{20,148},{24,152},{28,15... | collective-permute-start | bytes 491528 | tf_op jit(solution)/shard_map/ppermute | solution.py:29
  6.8 0.1 collective-permute-start.2
  6.8 0.1 stack.19.info
  6.9 4.2 %split_band.1 = (bf16[1024,1024]{1,0:T(8,128)(2,1)}, bf16[1024,1024]{1,0:T(8,128)(2,1)}, f32[8,128]{1,0:T(8,128)S(1)}) custom-call(s32[5]{0:T(128)S(1)} %stack.19.info, f32[8192,128]{1,0:T(8,128)} %bitcast.13, f32[40,1024]{1,0:T(8,128)S(1)} %get-tuple-element.33.token.refs_0_.refs_1_), custom_call_target="tpu_custom_call" | custom-call | tf_op jit(solution)/shard_map/split_band/pallas_call | solution.py:68
  11.1 3.9 %all-to-all-start = ((f32[4,1024,128]{2,1,0:T(8,128)}), f32[4,1024,128]{2,1,0:T(8,128)S(1)}, u32[]{:S(2)}, u32[]{:S(2)}) async-start(f32[4,1024,128]{2,1,0:T(8,128)} %slabs.1), calls=%async_computation | async-start | bytes 4194304 | tf_op jit(solution)/shard_map/all_to_all | solution.py:44
  15.1 0.0 collective-permute-done.refs_1_.refs_2_
  15.1 0.0 collective-permute-done.1.refs_2_.refs_3_
  15.1 0.0 copy-start.2
  15.1 1.6 %collective-permute-done.2.refs_3_.refs_4_ = f32[40,1024]{1,0:T(8,128)S(1)} collective-permute-done((f32[40,1024]{1,0:T(8,128)S(1)}, f32[40,1024]{1,0:T(8,128)S(1)}, u32[]{:S(2)}, u32[]{:S(2)}) %collective-permute-start.2) | collective-permute-done | bytes 163872 | tf_op jit(solution)/shard_map/ppermute | solution.py:29
  16.6 0.0 copy-done
  16.6 3.0 %solve.1 = (f32[16,1024]{1,0:T(8,128)S(1)}, f32[16,1024]{1,0:T(8,128)S(1)}) custom-call(s32[5]{0:T(128)S(1)} %stack.19.info, f32[40,1024]{1,0:T(8,128)S(1)} %get-tuple-element.33.token.refs_0_.refs_1_, f32[40,1024]{1,0:T(8,128)S(1)} %collective-permute-done.refs_1_.refs_2_, f32[40,1024]{1,0:T(8,128)S(1)} %collective-permute-done.1.refs_2_.refs_3_, ...), custom_call_target="tpu_custom_call" | custom-call | flops 70000001024 | bytes 1048576 | tf_op jit(solution)/shard_map/solve/pallas_call | solution.py:68
  19.6 1.7 %collective-permute-start.3 = (f32[16,1024]{1,0:T(8,128)S(1)}, f32[16,1024]{1,0:T(8,128)S(1)}, u32[]{:S(2)}, u32[]{:S(2)}) collective-permute-start(f32[16,1024]{1,0:T(8,128)S(1)} %get-tuple-element.40), channel_id=1, source_target_pairs={{0,4},{4,0},{8,12},{12,8},{16,20},{20,16},{24,28},{28,24},{32,36},... | collective-permute-start | bytes 196616 | tf_op jit(solution)/shard_map/ppermute | solution.py:48
  21.3 0.9 collective-permute-done.3
  22.2 1.4 %collective-permute-start.6 = (f32[16,1024]{1,0:T(8,128)S(1)}, f32[16,1024]{1,0:T(8,128)S(1)}, u32[]{:S(2)}, u32[]{:S(2)}) collective-permute-start(f32[16,1024]{1,0:T(8,128)S(1)} %broadcast_select_fusion), channel_id=1, source_target_pairs={{0,8},{4,12},{8,0},{12,4},{16,24},{20,28},{24,16},{28,20},{32,40},... | collective-permute-start | bytes 196616 | tf_op jit(solution)/shard_map/ppermute | solution.py:33
  23.7 3.0 %collective-permute-start.5 = (f32[16,1024]{1,0:T(8,128)S(1)}, f32[16,1024]{1,0:T(8,128)S(1)}, u32[]{:S(2)}, u32[]{:S(2)}) collective-permute-start(f32[16,1024]{1,0:T(8,128)S(1)} %broadcast_select_fusion), channel_id=1, source_target_pairs={{0,16},{4,20},{8,24},{12,28},{16,0},{20,4},{24,8},{28,12},{32,48},... | collective-permute-start | bytes 196616 | tf_op jit(solution)/shard_map/ppermute | solution.py:33
  26.7 0.0 collective-permute-start.4
  26.7 0.0 collective-permute-done.6
  26.7 2.2 %collective-permute-done.5 = f32[16,1024]{1,0:T(8,128)S(1)} collective-permute-done((f32[16,1024]{1,0:T(8,128)S(1)}, f32[16,1024]{1,0:T(8,128)S(1)}, u32[]{:S(2)}, u32[]{:S(2)}) %collective-permute-start.5) | collective-permute-done | bytes 65568 | tf_op jit(solution)/shard_map/ppermute | solution.py:33
  28.9 2.8 %collective-permute-done.4 = f32[16,1024]{1,0:T(8,128)S(1)} collective-permute-done((f32[16,1024]{1,0:T(8,128)S(1)}, f32[16,1024]{1,0:T(8,128)S(1)}, u32[]{:S(2)}, u32[]{:S(2)}) %collective-permute-start.4) | collective-permute-done | bytes 65568 | tf_op jit(solution)/shard_map/ppermute | solution.py:33
  31.7 5.2 %collective-permute-start.7 = (f32[16,1024]{1,0:T(8,128)S(1)}, f32[16,1024]{1,0:T(8,128)S(1)}, u32[]{:S(2)}, u32[]{:S(2)}) collective-permute-start(f32[16,1024]{1,0:T(8,128)S(1)} %select_select_fusion), channel_id=1, source_target_pairs={{0,48},{4,52},{8,56},{12,60},{16,32},{20,36},{24,40},{28,44},{32,1... | collective-permute-start | bytes 196616 | tf_op jit(solution)/shard_map/ppermute | solution.py:33
  36.9 2.0 %collective-permute-done.7 = f32[16,1024]{1,0:T(8,128)S(1)} collective-permute-done((f32[16,1024]{1,0:T(8,128)S(1)}, f32[16,1024]{1,0:T(8,128)S(1)}, u32[]{:S(2)}, u32[]{:S(2)}) %collective-permute-start.7) | collective-permute-done | bytes 65568 | tf_op jit(solution)/shard_map/ppermute | solution.py:33
  38.9 2.0 %collective-permute-start.11 = (f32[16,1024]{1,0:T(8,128)S(1)}, f32[16,1024]{1,0:T(8,128)S(1)}, u32[]{:S(2)}, u32[]{:S(2)}) collective-permute-start(f32[16,1024]{1,0:T(8,128)S(1)} %broadcast_select_fusion.1.refs_5_), channel_id=1, source_target_pairs={{0,192},{4,196},{8,200},{12,204},{16,208},{20,212},{24,216},{28,22... | collective-permute-start | bytes 196616 | tf_op jit(solution)/shard_map/ppermute | solution.py:29
  40.9 0.3 collective-permute-start.10
  41.2 1.1 %collective-permute-start.9 = (f32[16,1024]{1,0:T(8,128)S(1)}, f32[16,1024]{1,0:T(8,128)S(1)}, u32[]{:S(2)}, u32[]{:S(2)}) collective-permute-start(f32[16,1024]{1,0:T(8,128)S(1)} %broadcast_select_fusion.1.refs_5_), channel_id=1, source_target_pairs={{0,64},{4,68},{8,72},{12,76},{16,80},{20,84},{24,88},{28,92},{32,9... | collective-permute-start | bytes 196616 | tf_op jit(solution)/shard_map/ppermute | solution.py:29
  42.2 0.0 all-to-all-done.refs_0_
  42.2 3.1 %mid.1 = (f32[1024,128]{1,0:T(8,128)S(1)}, f32[1024,128]{1,0:T(8,128)S(1)}, f32[1024,128]{1,0:T(8,128)S(1)}, f32[1024,128]{1,0:T(8,128)S(1)}, f32[8,128]{1,0:T(8,128)S(1)}) custom-call(s32[5]{0:T(128)S(1)} %stack.19.info, f32[4,1024,128]{2,1,0:T(8,128)S(1)} %all-to-all-done.refs_0_, f32[40,1024]{1,0:T(8,128)} %copy-done, f32[40,1024]{1,0:T(8,128)} %copy-done.1, ...), custom_call_target="tpu_custom_call" | custom-call | flops 10000000000 | bytes 1048576 | tf_op jit(solution)/shard_map/mid/pallas_call | solution.py:68
  45.4 0.0 collective-permute-done.11
  45.4 0.2 collective-permute-done.10
  45.6 0.0 collective-permute-done.9
  45.6 2.8 %collective-permute-start.13 = (f32[64,1024]{1,0:T(8,128)S(1)}, f32[64,1024]{1,0:T(8,128)S(1)}, u32[]{:S(2)}, u32[]{:S(2)}) collective-permute-start(f32[64,1024]{1,0:T(8,128)S(1)} %pad_maximum_fusion.refs_0_), channel_id=1, source_target_pairs={{0,3},{1,2},{2,1},{3,0},{4,7},{5,6},{6,5},{7,4},{8,11},{9,10},{10,... | collective-permute-start | bytes 786440 | tf_op jit(solution)/shard_map/ppermute | solution.py:37
  48.4 0.0 collective-permute-start.12
  48.4 0.3 collective-permute-start.8
  48.7 1.8 %collective-permute-start.17 = (f32[1024,128]{1,0:T(8,128)S(1)}, f32[1024,128]{1,0:T(8,128)S(1)}, u32[]{:S(2)}, u32[]{:S(2)}) collective-permute-start(f32[1024,128]{1,0:T(8,128)S(1)} %get-tuple-element.52), channel_id=1, source_target_pairs={{0,192},{4,196},{8,200},{12,204},{16,208},{20,212},{24,216},{28,22... | collective-permute-start | bytes 1572872 | tf_op jit(solution)/shard_map/ppermute | solution.py:29
  50.5 1.7 %collective-permute-done.13.refs_1_ = f32[64,1024]{1,0:T(8,128)S(1)} collective-permute-done((f32[64,1024]{1,0:T(8,128)S(1)}, f32[64,1024]{1,0:T(8,128)S(1)}, u32[]{:S(2)}, u32[]{:S(2)}) %collective-permute-start.13) | collective-permute-done | bytes 262176 | tf_op jit(solution)/shard_map/ppermute | solution.py:37
  52.2 4.5 %collective-permute-start.15 = (f32[64,1024]{1,0:T(8,128)S(1)}, f32[64,1024]{1,0:T(8,128)S(1)}, u32[]{:S(2)}, u32[]{:S(2)}) collective-permute-start(f32[64,1024]{1,0:T(8,128)S(1)} %collective-permute-done.13.refs_1_), channel_id=1, source_target_pairs={{0,4},{4,0},{8,12},{12,8},{16,20},{20,16},{24,28},{28,24},{32,36},... | collective-permute-start | bytes 786440 | tf_op jit(solution)/shard_map/ppermute | solution.py:48
  56.6 0.0 collective-permute-done.12.refs_0_
  56.6 1.8 %collective-permute-start.14 = (f32[64,1024]{1,0:T(8,128)S(1)}, f32[64,1024]{1,0:T(8,128)S(1)}, u32[]{:S(2)}, u32[]{:S(2)}) collective-permute-start(f32[64,1024]{1,0:T(8,128)S(1)} %collective-permute-done.12.refs_0_), channel_id=1, source_target_pairs={{0,4},{4,0},{8,12},{12,8},{16,20},{20,16},{24,28},{28,24},{32,36},... | collective-permute-start | bytes 786440 | tf_op jit(solution)/shard_map/ppermute | solution.py:48
  58.4 0.3 collective-permute-start.19
  58.8 0.0 collective-permute-done.15.refs_3_
  58.8 0.8 collective-permute-done.14.refs_2_
  59.6 4.2 %update.3 = (f32[128,1024]{1,0:T(8,128)S(1)}, f32[128,1024]{1,0:T(8,128)S(1)}, f32[128,1024]{1,0:T(8,128)S(1)}) custom-call(s32[5]{0:T(128)S(1)} %stack.19.info, f32[64,1024]{1,0:T(8,128)S(1)} %collective-permute-done.12.refs_0_, f32[64,1024]{1,0:T(8,128)S(1)} %collective-permute-done.13.refs_1_, f32[64,1024]{1,0:T(8,128)S(1)} %collective-permute-done.14.refs_2_, ...), custom_call_target="tpu_custom_call" | custom-call | flops 1 | bytes 1048576 | tf_op jit(solution)/shard_map/update/pallas_call | solution.py:68
  63.7 0.5 collective-permute-start.21
  64.2 1.7 %collective-permute-start.23 = (f32[128,1024]{1,0:T(8,128)S(1)}, f32[128,1024]{1,0:T(8,128)S(1)}, u32[]{:S(2)}, u32[]{:S(2)}) collective-permute-start(f32[128,1024]{1,0:T(8,128)S(1)} %get-tuple-element.60), channel_id=1, source_target_pairs={{0,3},{1,2},{2,1},{3,0},{4,7},{5,6},{6,5},{7,4},{8,11},{9,10},{10,... | collective-permute-start | bytes 1572872 | tf_op jit(solution)/shard_map/ppermute | solution.py:37
  65.9 1.9 %collective-permute-done.19.refs_0_ = f32[64,1024]{1,0:T(8,128)S(1)} collective-permute-done((f32[64,1024]{1,0:T(8,128)S(1)}, f32[64,1024]{1,0:T(8,128)S(1)}, u32[]{:S(2)}, u32[]{:S(2)}) %collective-permute-start.19) | collective-permute-done | bytes 262176 | tf_op jit(solution)/shard_map/ppermute | solution.py:37
  67.9 1.2 %collective-permute-start.20 = (f32[64,1024]{1,0:T(8,128)S(1)}, f32[64,1024]{1,0:T(8,128)S(1)}, u32[]{:S(2)}, u32[]{:S(2)}) collective-permute-start(f32[64,1024]{1,0:T(8,128)S(1)} %collective-permute-done.19.refs_0_), channel_id=1, source_target_pairs={{0,4},{4,0},{8,12},{12,8},{16,20},{20,16},{24,28},{28,24},{32,36},... | collective-permute-start | bytes 786440 | tf_op jit(solution)/shard_map/ppermute | solution.py:48
  69.0 0.0 collective-permute-done.8.refs_0_.refs_1_
  69.0 0.0 collective-permute-start.18
  69.0 0.0 collective-permute-done.17.refs_1_.refs_3_
  69.0 1.8 %collective-permute-start.16 = (f32[1024,128]{1,0:T(8,128)S(1)}, f32[1024,128]{1,0:T(8,128)S(1)}, u32[]{:S(2)}, u32[]{:S(2)}) collective-permute-start(f32[1024,128]{1,0:T(8,128)S(1)} %get-tuple-element.51), channel_id=1, source_target_pairs={{0,128},{4,132},{8,136},{12,140},{16,144},{20,148},{24,152},{28,15... | collective-permute-start | bytes 1572872 | tf_op jit(solution)/shard_map/ppermute | solution.py:29
  70.9 0.5 mark.2.refs_4_
  71.4 0.0 collective-permute-done.20.refs_1_
  71.4 3.4 %update.4 = (f32[128,1024]{1,0:T(8,128)S(1)}, f32[128,1024]{1,0:T(8,128)S(1)}) custom-call(s32[5]{0:T(128)S(1)} %stack.19.info, f32[64,1024]{1,0:T(8,128)S(1)} %collective-permute-done.19.refs_0_, f32[64,1024]{1,0:T(8,128)S(1)} %collective-permute-done.20.refs_1_, bf16[1024,1024]{1,0:T(8,128)(2,1)} %get-tuple-element.48.refs_4_.refs_2_, ...), custom_call_target="tpu_custom_call" | custom-call | flops 1 | bytes 1048576 | tf_op jit(solution)/shard_map/update/pallas_call | solution.py:68
  74.8 0.2 collective-permute-start.22
  75.0 0.0 collective-permute-done.18.refs_1_
  75.0 3.4 %update.5 = (f32[128,1024]{1,0:T(8,128)S(1)}, f32[128,1024]{1,0:T(8,128)S(1)}) custom-call(s32[5]{0:T(128)S(1)} %stack.19.info, f32[64,1024]{1,0:T(8,128)S(1)} %pad_maximum_fusion.refs_0_, f32[64,1024]{1,0:T(8,128)S(1)} %collective-permute-done.18.refs_1_, bf16[1024,1024]{1,0:T(8,128)(2,1)} %get-tuple-element.48.refs_4_.refs_2_, ...), custom_call_target="tpu_custom_call" | custom-call | flops 1 | bytes 1048576 | tf_op jit(solution)/shard_map/update/pallas_call | solution.py:68
  78.4 0.0 collective-permute-done.21.refs_0_.refs_6_
  78.4 0.0 collective-permute-done.23.refs_1_.refs_8_
  78.5 0.5 mark.3.refs_9_
  79.0 4.7 %collective-permute-done.16.refs_2_ = f32[1024,128]{1,0:T(8,128)S(1)} collective-permute-done((f32[1024,128]{1,0:T(8,128)S(1)}, f32[1024,128]{1,0:T(8,128)S(1)}, u32[]{:S(2)}, u32[]{:S(2)}) %collective-permute-start.16) | collective-permute-done | bytes 524320 | tf_op jit(solution)/shard_map/ppermute | solution.py:29
  83.7 6.2 %collective-permute-done.22.refs_7_ = f32[128,1024]{1,0:T(8,128)S(1)} collective-permute-done((f32[128,1024]{1,0:T(8,128)S(1)}, f32[128,1024]{1,0:T(8,128)S(1)}, u32[]{:S(2)}, u32[]{:S(2)}) %collective-permute-start.22) | collective-permute-done | bytes 524320 | tf_op jit(solution)/shard_map/ppermute | solution.py:37
  89.9 1.9 %last.1 = f32[4,1024,128]{2,1,0:T(8,128)} custom-call(s32[5]{0:T(128)S(1)} %stack.19.info, f32[1024,128]{1,0:T(8,128)S(1)} %get-tuple-element.41.refs_0_, f32[1024,128]{1,0:T(8,128)S(1)} %collective-permute-done.8.refs_0_.refs_1_, f32[1024,128]{1,0:T(8,128)S(1)} %collective-permute-done.16.refs_2_, f32[1024,128]{1,0:T(8,128)S(1)} %collective-permute-done.17.refs_1_.refs_3_, ...), custom_call_target="tpu_custom_call" | custom-call | tf_op jit(solution)/shard_map/last/pallas_call | solution.py:68
  (9 shorter events, 0.1 us)
Async XLA Ops:
  2.2 14.5 %copy-start = (f32[40,1024]{1,0:T(8,128)}, f32[40,1024]{1,0:T(8,128)S(1)}, u32[]{:S(2)}) copy-start(f32[40,1024]{1,0:T(8,128)S(1)} %get-tuple-element.33.token.refs_0_.refs_1_) | copy-start | bytes 491524
  2.2 12.9 %collective-permute-start = (f32[40,1024]{1,0:T(8,128)S(1)}, f32[40,1024]{1,0:T(8,128)S(1)}, u32[]{:S(2)}, u32[]{:S(2)}) collective-permute-start(f32[40,1024]{1,0:T(8,128)S(1)} %get-tuple-element.36), channel_id=1, source_target_pairs={{0,64},{4,68},{8,72},{12,76},{16,80},{20,84},{24,88},{28,92},{32,9... | collective-permute-start | bytes 491528 | tf_op jit(solution)/shard_map/ppermute | solution.py:29
  4.3 10.7 %collective-permute-start.1 = (f32[40,1024]{1,0:T(8,128)S(1)}, f32[40,1024]{1,0:T(8,128)S(1)}, u32[]{:S(2)}, u32[]{:S(2)}) collective-permute-start(f32[40,1024]{1,0:T(8,128)S(1)} %get-tuple-element.37), channel_id=1, source_target_pairs={{0,128},{4,132},{8,136},{12,140},{16,144},{20,148},{24,152},{28,15... | collective-permute-start | bytes 491528 | tf_op jit(solution)/shard_map/ppermute | solution.py:29
  6.8 9.9 %collective-permute-start.2 = (f32[40,1024]{1,0:T(8,128)S(1)}, f32[40,1024]{1,0:T(8,128)S(1)}, u32[]{:S(2)}, u32[]{:S(2)}) collective-permute-start(f32[40,1024]{1,0:T(8,128)S(1)} %get-tuple-element.38), channel_id=1, source_target_pairs={{0,192},{4,196},{8,200},{12,204},{16,208},{20,212},{24,216},{28,22... | collective-permute-start | bytes 491528 | tf_op jit(solution)/shard_map/ppermute | solution.py:29
  11.1 31.1 %all-to-all-start = ((f32[4,1024,128]{2,1,0:T(8,128)}), f32[4,1024,128]{2,1,0:T(8,128)S(1)}, u32[]{:S(2)}, u32[]{:S(2)}) async-start(f32[4,1024,128]{2,1,0:T(8,128)} %slabs.1), calls=%async_computation | async-start | bytes 4194304 | tf_op jit(solution)/shard_map/all_to_all | solution.py:44
  15.1 4.5 %copy-start.1 = (f32[40,1024]{1,0:T(8,128)}, f32[40,1024]{1,0:T(8,128)S(1)}, u32[]{:S(2)}) copy-start(f32[40,1024]{1,0:T(8,128)S(1)} %collective-permute-done.refs_1_.refs_2_) | copy-start | bytes 491524
  15.1 4.5 %copy-start.2 = (f32[40,1024]{1,0:T(8,128)}, f32[40,1024]{1,0:T(8,128)S(1)}, u32[]{:S(2)}) copy-start(f32[40,1024]{1,0:T(8,128)S(1)} %collective-permute-done.1.refs_2_.refs_3_) | copy-start | bytes 491524
  16.6 3.0 %copy-start.3 = (f32[40,1024]{1,0:T(8,128)}, f32[40,1024]{1,0:T(8,128)S(1)}, u32[]{:S(2)}) copy-start(f32[40,1024]{1,0:T(8,128)S(1)} %collective-permute-done.2.refs_3_.refs_4_) | copy-start | bytes 491524
  19.6 2.6 %collective-permute-start.3 = (f32[16,1024]{1,0:T(8,128)S(1)}, f32[16,1024]{1,0:T(8,128)S(1)}, u32[]{:S(2)}, u32[]{:S(2)}) collective-permute-start(f32[16,1024]{1,0:T(8,128)S(1)} %get-tuple-element.40), channel_id=1, source_target_pairs={{0,4},{4,0},{8,12},{12,8},{16,20},{20,16},{24,28},{28,24},{32,36},... | collective-permute-start | bytes 196616 | tf_op jit(solution)/shard_map/ppermute | solution.py:48
  22.2 4.4 %collective-permute-start.6 = (f32[16,1024]{1,0:T(8,128)S(1)}, f32[16,1024]{1,0:T(8,128)S(1)}, u32[]{:S(2)}, u32[]{:S(2)}) collective-permute-start(f32[16,1024]{1,0:T(8,128)S(1)} %broadcast_select_fusion), channel_id=1, source_target_pairs={{0,8},{4,12},{8,0},{12,4},{16,24},{20,28},{24,16},{28,20},{32,40},... | collective-permute-start | bytes 196616 | tf_op jit(solution)/shard_map/ppermute | solution.py:33
  23.7 5.2 %collective-permute-start.5 = (f32[16,1024]{1,0:T(8,128)S(1)}, f32[16,1024]{1,0:T(8,128)S(1)}, u32[]{:S(2)}, u32[]{:S(2)}) collective-permute-start(f32[16,1024]{1,0:T(8,128)S(1)} %broadcast_select_fusion), channel_id=1, source_target_pairs={{0,16},{4,20},{8,24},{12,28},{16,0},{20,4},{24,8},{28,12},{32,48},... | collective-permute-start | bytes 196616 | tf_op jit(solution)/shard_map/ppermute | solution.py:33
  26.7 5.0 %collective-permute-start.4 = (f32[16,1024]{1,0:T(8,128)S(1)}, f32[16,1024]{1,0:T(8,128)S(1)}, u32[]{:S(2)}, u32[]{:S(2)}) collective-permute-start(f32[16,1024]{1,0:T(8,128)S(1)} %broadcast_select_fusion), channel_id=1, source_target_pairs={{0,24},{4,28},{8,16},{12,20},{16,8},{20,12},{24,0},{28,4},{32,56},... | collective-permute-start | bytes 196616 | tf_op jit(solution)/shard_map/ppermute | solution.py:33
  31.7 7.2 %collective-permute-start.7 = (f32[16,1024]{1,0:T(8,128)S(1)}, f32[16,1024]{1,0:T(8,128)S(1)}, u32[]{:S(2)}, u32[]{:S(2)}) collective-permute-start(f32[16,1024]{1,0:T(8,128)S(1)} %select_select_fusion), channel_id=1, source_target_pairs={{0,48},{4,52},{8,56},{12,60},{16,32},{20,36},{24,40},{28,44},{32,1... | collective-permute-start | bytes 196616 | tf_op jit(solution)/shard_map/ppermute | solution.py:33
  38.9 6.5 %collective-permute-start.11 = (f32[16,1024]{1,0:T(8,128)S(1)}, f32[16,1024]{1,0:T(8,128)S(1)}, u32[]{:S(2)}, u32[]{:S(2)}) collective-permute-start(f32[16,1024]{1,0:T(8,128)S(1)} %broadcast_select_fusion.1.refs_5_), channel_id=1, source_target_pairs={{0,192},{4,196},{8,200},{12,204},{16,208},{20,212},{24,216},{28,22... | collective-permute-start | bytes 196616 | tf_op jit(solution)/shard_map/ppermute | solution.py:29
  40.9 4.7 %collective-permute-start.10 = (f32[16,1024]{1,0:T(8,128)S(1)}, f32[16,1024]{1,0:T(8,128)S(1)}, u32[]{:S(2)}, u32[]{:S(2)}) collective-permute-start(f32[16,1024]{1,0:T(8,128)S(1)} %broadcast_select_fusion.1.refs_5_), channel_id=1, source_target_pairs={{0,128},{4,132},{8,136},{12,140},{16,144},{20,148},{24,152},{28,15... | collective-permute-start | bytes 196616 | tf_op jit(solution)/shard_map/ppermute | solution.py:29
  41.2 4.4 %collective-permute-start.9 = (f32[16,1024]{1,0:T(8,128)S(1)}, f32[16,1024]{1,0:T(8,128)S(1)}, u32[]{:S(2)}, u32[]{:S(2)}) collective-permute-start(f32[16,1024]{1,0:T(8,128)S(1)} %broadcast_select_fusion.1.refs_5_), channel_id=1, source_target_pairs={{0,64},{4,68},{8,72},{12,76},{16,80},{20,84},{24,88},{28,92},{32,9... | collective-permute-start | bytes 196616 | tf_op jit(solution)/shard_map/ppermute | solution.py:29
  45.6 6.6 %collective-permute-start.13 = (f32[64,1024]{1,0:T(8,128)S(1)}, f32[64,1024]{1,0:T(8,128)S(1)}, u32[]{:S(2)}, u32[]{:S(2)}) collective-permute-start(f32[64,1024]{1,0:T(8,128)S(1)} %pad_maximum_fusion.refs_0_), channel_id=1, source_target_pairs={{0,3},{1,2},{2,1},{3,0},{4,7},{5,6},{6,5},{7,4},{8,11},{9,10},{10,... | collective-permute-start | bytes 786440 | tf_op jit(solution)/shard_map/ppermute | solution.py:37
  48.4 8.2 %collective-permute-start.12 = (f32[64,1024]{1,0:T(8,128)S(1)}, f32[64,1024]{1,0:T(8,128)S(1)}, u32[]{:S(2)}, u32[]{:S(2)}) collective-permute-start(f32[64,1024]{1,0:T(8,128)S(1)} %pad_maximum_fusion.refs_0_), channel_id=1, source_target_pairs={{0,1},{1,0},{2,3},{3,2},{4,5},{5,4},{6,7},{7,6},{8,9},{9,8},{10,11... | collective-permute-start | bytes 786440 | tf_op jit(solution)/shard_map/ppermute | solution.py:37
  48.4 20.6 %collective-permute-start.8 = (f32[1024,128]{1,0:T(8,128)S(1)}, f32[1024,128]{1,0:T(8,128)S(1)}, u32[]{:S(2)}, u32[]{:S(2)}) collective-permute-start(f32[1024,128]{1,0:T(8,128)S(1)} %get-tuple-element.42), channel_id=1, source_target_pairs={{0,64},{4,68},{8,72},{12,76},{16,80},{20,84},{24,88},{28,92},{32,9... | collective-permute-start | bytes 1572872 | tf_op jit(solution)/shard_map/ppermute | solution.py:29
  48.7 20.4 %collective-permute-start.17 = (f32[1024,128]{1,0:T(8,128)S(1)}, f32[1024,128]{1,0:T(8,128)S(1)}, u32[]{:S(2)}, u32[]{:S(2)}) collective-permute-start(f32[1024,128]{1,0:T(8,128)S(1)} %get-tuple-element.52), channel_id=1, source_target_pairs={{0,192},{4,196},{8,200},{12,204},{16,208},{20,212},{24,216},{28,22... | collective-permute-start | bytes 1572872 | tf_op jit(solution)/shard_map/ppermute | solution.py:29
  52.2 6.6 %collective-permute-start.15 = (f32[64,1024]{1,0:T(8,128)S(1)}, f32[64,1024]{1,0:T(8,128)S(1)}, u32[]{:S(2)}, u32[]{:S(2)}) collective-permute-start(f32[64,1024]{1,0:T(8,128)S(1)} %collective-permute-done.13.refs_1_), channel_id=1, source_target_pairs={{0,4},{4,0},{8,12},{12,8},{16,20},{20,16},{24,28},{28,24},{32,36},... | collective-permute-start | bytes 786440 | tf_op jit(solution)/shard_map/ppermute | solution.py:48
  56.6 3.0 %collective-permute-start.14 = (f32[64,1024]{1,0:T(8,128)S(1)}, f32[64,1024]{1,0:T(8,128)S(1)}, u32[]{:S(2)}, u32[]{:S(2)}) collective-permute-start(f32[64,1024]{1,0:T(8,128)S(1)} %collective-permute-done.12.refs_0_), channel_id=1, source_target_pairs={{0,4},{4,0},{8,12},{12,8},{16,20},{20,16},{24,28},{28,24},{32,36},... | collective-permute-start | bytes 786440 | tf_op jit(solution)/shard_map/ppermute | solution.py:48
  58.4 9.4 %collective-permute-start.19 = (f32[64,1024]{1,0:T(8,128)S(1)}, f32[64,1024]{1,0:T(8,128)S(1)}, u32[]{:S(2)}, u32[]{:S(2)}) collective-permute-start(f32[64,1024]{1,0:T(8,128)S(1)} %pad_maximum_fusion.refs_0_), channel_id=1, source_target_pairs={{0,2},{1,3},{2,0},{3,1},{4,6},{5,7},{6,4},{7,5},{8,10},{9,11},{10,... | collective-permute-start | bytes 786440 | tf_op jit(solution)/shard_map/ppermute | solution.py:37
  63.7 14.7 %collective-permute-start.21 = (f32[128,1024]{1,0:T(8,128)S(1)}, f32[128,1024]{1,0:T(8,128)S(1)}, u32[]{:S(2)}, u32[]{:S(2)}) collective-permute-start(f32[128,1024]{1,0:T(8,128)S(1)} %get-tuple-element.58), channel_id=1, source_target_pairs={{0,1},{1,0},{2,3},{3,2},{4,5},{5,4},{6,7},{7,6},{8,9},{9,8},{10,11... | collective-permute-start | bytes 1572872 | tf_op jit(solution)/shard_map/ppermute | solution.py:37
  64.2 14.2 %collective-permute-start.23 = (f32[128,1024]{1,0:T(8,128)S(1)}, f32[128,1024]{1,0:T(8,128)S(1)}, u32[]{:S(2)}, u32[]{:S(2)}) collective-permute-start(f32[128,1024]{1,0:T(8,128)S(1)} %get-tuple-element.60), channel_id=1, source_target_pairs={{0,3},{1,2},{2,1},{3,0},{4,7},{5,6},{6,5},{7,4},{8,11},{9,10},{10,... | collective-permute-start | bytes 1572872 | tf_op jit(solution)/shard_map/ppermute | solution.py:37
  67.9 3.6 %collective-permute-start.20 = (f32[64,1024]{1,0:T(8,128)S(1)}, f32[64,1024]{1,0:T(8,128)S(1)}, u32[]{:S(2)}, u32[]{:S(2)}) collective-permute-start(f32[64,1024]{1,0:T(8,128)S(1)} %collective-permute-done.19.refs_0_), channel_id=1, source_target_pairs={{0,4},{4,0},{8,12},{12,8},{16,20},{20,16},{24,28},{28,24},{32,36},... | collective-permute-start | bytes 786440 | tf_op jit(solution)/shard_map/ppermute | solution.py:48
  69.0 6.0 %collective-permute-start.18 = (f32[64,1024]{1,0:T(8,128)S(1)}, f32[64,1024]{1,0:T(8,128)S(1)}, u32[]{:S(2)}, u32[]{:S(2)}) collective-permute-start(f32[64,1024]{1,0:T(8,128)S(1)} %pad_maximum_fusion.refs_0_), channel_id=1, source_target_pairs={{0,4},{4,0},{8,12},{12,8},{16,20},{20,16},{24,28},{28,24},{32,36},... | collective-permute-start | bytes 786440 | tf_op jit(solution)/shard_map/ppermute | solution.py:48
  69.0 14.7 %collective-permute-start.16 = (f32[1024,128]{1,0:T(8,128)S(1)}, f32[1024,128]{1,0:T(8,128)S(1)}, u32[]{:S(2)}, u32[]{:S(2)}) collective-permute-start(f32[1024,128]{1,0:T(8,128)S(1)} %get-tuple-element.51), channel_id=1, source_target_pairs={{0,128},{4,132},{8,136},{12,140},{16,144},{20,148},{24,152},{28,15... | collective-permute-start | bytes 1572872 | tf_op jit(solution)/shard_map/ppermute | solution.py:29
  74.8 15.1 %collective-permute-start.22 = (f32[128,1024]{1,0:T(8,128)S(1)}, f32[128,1024]{1,0:T(8,128)S(1)}, u32[]{:S(2)}, u32[]{:S(2)}) collective-permute-start(f32[128,1024]{1,0:T(8,128)S(1)} %get-tuple-element.59), channel_id=1, source_target_pairs={{0,2},{1,3},{2,0},{3,1},{4,6},{5,7},{6,4},{7,5},{8,10},{9,11},{10,... | collective-permute-start | bytes 1572872 | tf_op jit(solution)/shard_map/ppermute | solution.py:37

commit v5 on v4

--- a/solution.py
+++ b/solution.py
@@ -82,9 +82,8 @@
     )(info, *args)
 
 
-def prep_kernel(start, slabs, diags, *refs):
-    outs, (slab, diag, came) = refs[:NX], refs[NX:]
-    cycle, x = start[0] // (NX * NZ * NC), lax.axis_index("rows") // (NZ * NC)
+def prep_kernel(start, slabs, diags, keep, send, slab, diag, came):
+    cycle, core = start[0] // (NX * NZ * NC), lax.axis_index("rows") % NC
     copies = [pltpu.make_async_copy(diags, diag, came.at[4])]
     for i in range(4):
         part = pl.ds(256 * i, 256)
@@ -92,23 +91,19 @@
     for copy in copies:
         copy.start()
     copies[0].wait()
-    for s in range(NX):
-        to = x ^ s
+    for out in (keep, send):
         for level in range(2):
-            outs[s][32 + level : 33 + level, :] = diag[level, pl.ds(cycle, 1), :]
-            outs[s][34 + level : 35 + level, :] = diag[level, pl.ds(to, 1), :]
-        outs[s][36:40, :] = jnp.zeros((4, NB), F32)
+            out[64 + level : 65 + level, :] = diag[level, pl.ds(cycle, 1), :]
+        out[66:72, :] = jnp.zeros((6, NB), F32)
     for i in range(4):
         copies[i + 1].wait()
         at = slice(256 * i, 256 * i + 256)
         flipped = slab[at, :].T
         for to in range(NX):
-            rows = flipped[32 * to : 32 * to + 32]
-            for s in range(NX):
-
-                @pl.when(to ^ s == x)
-                def _():
-                    outs[s][:32, at] = rows
+            first, second = [flipped[HALF * j : HALF * j + HALF] for j in (2 * to, 2 * to + 1)]
+            rows = slice(HALF * to, HALF * to + HALF)
+            keep[rows, at] = jnp.where(core == 0, first, second)
+            send[rows, at] = jnp.where(core == 0, second, first)
 
 
 def prep(start, right_sides, diag):
@@ -119,8 +114,8 @@
         start,
         far(right_sides, diag),
         [ANY] * 2,
-        [whole(40, NB)] * NX,
-        [jax.ShapeDtypeStruct((40, NB), F32)] * NX,
+        [whole(72, NB)] * 2,
+        [jax.ShapeDtypeStruct((72, NB), F32)] * 2,
         12,
         [
             pltpu.VMEM((NB, 128), F32),
@@ -130,6 +125,37 @@
     )
 
 
+def pack_kernel(info, keep, came, diag, *outs):
+    x = info[1]
+    for source, mine in ((keep, True), (came, False)):
+
+        @pl.when((info[3] == info[0] % NC) == mine)
+        def _():
+            for s in range(NX):
+                at = pl.ds(pl.multiple_of(HALF * (x ^ s), HALF), HALF)
+                outs[s][:16, :] = source[at, :]
+                outs[s][16:18, :] = source[64:66, :]
+
+    for s in range(NX):
+        for level in range(2):
+            outs[s][18 + level : 19 + level, :] = diag[level, pl.ds(x ^ s, 1), :]
+        outs[s][20:24, :] = jnp.zeros((4, NB), F32)
+
+
+def pack(info, keep, came, diag):
+    return call(
+        pack_kernel,
+        "pack",
+        1,
+        info,
+        (keep, came, diag),
+        [whole(72, NB)] * 2 + [whole(2, 4, NB)],
+        [whole(24, NB)] * NX,
+        [jax.ShapeDtypeStruct((24, NB), F32)] * NX,
+        8,
+    )
+
+
 def split(v):
     top = v.astype(BF16)
     return top, (v - top.astype(F32)).astype(BF16)
@@ -138,29 +164,13 @@
 TOKEN = jax.ShapeDtypeStruct((8, 128), F32)
 
 
-def split_band_kernel(info, rows, token, top, low, mark, near, near_top, near_low, came, went):
-    mark[...] = jnp.zeros((8, 128), F32)
-    copies = []
-    for i in range(4):
-        part = pl.ds(2048 * i, 2048)
-        copies.append(pltpu.make_async_copy(rows.at[part], near.at[part], came.at[i]))
-        copies[i].start()
-    sent = []
-    for i in range(4):
-        copies[i].wait()
-        part = slice(256 * i, 256 * i + 256)
-        for c in range(4):
-            for half in range(2):
-                a, b = split(near[pl.ds(2048 * i + 4 * half + c, 256, stride=8), :])
-                at = slice(256 * c + 128 * half, 256 * c + 128 * half + 128)
-                near_top[part, at] = a
-                near_low[part, at] = b
-        part = pl.ds(256 * i, 256)
-        for j, (here, there) in enumerate(((near_top, top), (near_low, low))):
-            sent.append(pltpu.make_async_copy(here.at[part], there.at[part], went.at[j, i]))
-            sent[-1].start()
-    for copy in sent:
-        copy.wait()
+def split_band_kernel(info, rows, token, top, low):
+    for c in range(4):
+        for half in range(2):
+            a, b = split(rows[pl.ds(4 * half + c, NB, stride=8), :])
+            at = slice(256 * c + 128 * half, 256 * c + 128 * half + 128)
+            top[:, at] = a
+            low[:, at] = b
 
 
 def split_band(info, band_rows, token):
@@ -170,18 +180,12 @@
         "split_band",
         1,
         info,
-        (*far(view), token),
-        [ANY] * 2,
-        [ANY] * 2 + [whole(8, 128)],
-        [pltpu.HBM((NB, NB), BF16)] * 2 + [TOKEN],
+        (view, token),
+        [whole(8 * NB, 128), ANY],
+        [whole(NB, NB)] * 2,
+        [jax.ShapeDtypeStruct((NB, NB), BF16)] * 2,
         12,
-        [
-            pltpu.VMEM((8 * NB, 128), F32),
-            pltpu.VMEM((NB, NB), BF16),
-            pltpu.VMEM((NB, NB), BF16),
-            pltpu.SemaphoreType.DMA((4,)),
-            pltpu.SemaphoreType.DMA((2, 4)),
-        ],
+        hint=10**9,
     )
 
 
@@ -191,13 +195,13 @@
 
 def solve_kernel(info, *refs):
     pieces, inverse = refs[:4], refs[4]
-    keep, send, got, near, full, done = refs[6:]
+    out, got, near, done = refs[5:]
     copies = []
     for i in range(4):
         part = (pl.ds(0, 256 * (i + 1)), pl.ds(256 * i, 256))
         copies.append(pltpu.make_async_copy(inverse.at[part], near.at[part], done.at[i]))
         copies[i].start()
-    x, core = info[1], info[3]
+    x = info[1]
     for s in range(NX):
         got[x ^ s] = pieces[s][...]
     x0 = info[0] % (NX * NZ * NC) // (NZ * NC)
@@ -205,36 +209,33 @@
     sign_high = jnp.where(high == 0, 1.0, -1.0).astype(F32)
     sign_low = jnp.where((x0 & 1) == 0, 1.0, -1.0).astype(F32)
     level = [
-        got[high | p, 32:33, :] * (got[p, :32, :] + sign_high * got[p + 2, :32, :])
+        got[high | p, 16:17, :] * (got[p, :16, :] + sign_high * got[p + 2, :16, :])
         for p in range(2)
     ]
-    top, low = split(got[x0, 33:34, :] * (0.5 * (level[0] + sign_low * level[1])))
+    top, low = split(got[x0, 17:18, :] * (0.5 * (level[0] + sign_low * level[1])))
     for i in range(4):
         depth, at = 256 * (i + 1), slice(256 * i, 256 * i + 256)
         copies[i].wait()
         a, b = split(near[:depth, at])
-        full[:, at] = (
+        out[:, at] = (
             product(top[:, :depth], b) + product(low[:, :depth], a) + product(top[:, :depth], a)
         )
-    keep[...] = full[pl.ds(pl.multiple_of(HALF * core, HALF), HALF), :]
-    send[...] = full[pl.ds(pl.multiple_of(HALF * (1 - core), HALF), HALF), :]
-
-
-def solve(info, pieces, inverse, token):
+
+
+def solve(info, pieces, inverse):
     return call(
         solve_kernel,
         "solve",
         1,
         info,
-        (*pieces, *far(inverse), token),
-        [whole(40, NB)] * NX + [ANY] * 2,
-        [whole(HALF, NB)] * 2,
-        [jax.ShapeDtypeStruct((HALF, NB), F32)] * 2,
+        (*pieces, *far(inverse)),
+        [whole(24, NB)] * NX + [ANY],
+        whole(HALF, NB),
+        jax.ShapeDtypeStruct((HALF, NB), F32),
         12,
         [
-            pltpu.VMEM((NX, 40, NB), F32),
+            pltpu.VMEM((NX, 24, NB), F32),
             pltpu.VMEM((NB, NB), F32),
-            pltpu.VMEM((32, NB), F32),
             pltpu.SemaphoreType.DMA((4,)),
         ],
         70 * 10**9,
@@ -243,20 +244,9 @@
 
 def update_kernel(n, info, *refs):
     own, other = refs[:n], refs[n : 2 * n]
-    far_top, far_low = refs[2 * n : 2 * n + 2]
+    top, low = refs[2 * n : 2 * n + 2]
     outs, mine = refs[2 * n + 3 : 3 * n + 3], refs[3 * n + 3]
-    left_top, left_low, top, low, done = refs[3 * n + 4 :]
-    copies = []
-    for c in range(2):
-        at = (slice(None), pl.ds(512 * c, 512))
-        copies.append(
-            [
-                pltpu.make_async_copy(far_top.at[at], top.at[at], done.at[0, c]),
-                pltpu.make_async_copy(far_low.at[at], low.at[at], done.at[1, c]),
-            ]
-        )
-        for copy in copies[c]:
-            copy.start()
+    left_top, left_low = refs[3 * n + 4 :]
     x, core = info[1], info[3]
     for t in range(NX):
         for h in range(NC):
@@ -268,8 +258,6 @@
                 if s == 0:
                     mine[pl.ds(pl.multiple_of(base, HALF), HALF), :] = piece
     for c in range(2):
-        for copy in copies[c]:
-            copy.wait()
         at = slice(512 * c, 512 * c + 512)
         result = (
             product(left_top[...], low[:, at])
@@ -287,18 +275,12 @@
         "update",
         1,
         info,
-        (*own, *other, *far(top, low), token),
-        [whole(64, NB)] * (2 * n) + [ANY] * 3,
+        (*own, *other, top, low, token),
+        [whole(64, NB)] * (2 * n) + [whole(NB, NB)] * 2 + [ANY],
         [whole(128, NB)] * (n + 1),
         [jax.ShapeDtypeStruct((128, NB), F32)] * (n + 1),
-        20,
-        [
-            pltpu.VMEM((128 * n, NB), BF16),
-            pltpu.VMEM((128 * n, NB), BF16),
-            pltpu.VMEM((NB, NB), BF16),
-            pltpu.VMEM((NB, NB), BF16),
-            pltpu.SemaphoreType.DMA((2, 2)),
-        ],
+        16,
+        [pltpu.VMEM((128 * n, NB), BF16)] * 2,
         hint,
     )
 
@@ -326,7 +308,7 @@
         info,
         (got, *far(*pieces), token),
         [whole(NX, NB, 128)]
-        + [pl.BlockSpec((8, NB), lambda i, s: (4, 0))] * NX
+        + [pl.BlockSpec((8, NB), lambda i, s: (2, 0))] * NX
         + [ANY],
         [whole(NB, 128)] * NX + [whole(8, 128)],
         [jax.ShapeDtypeStruct((NB, 128), F32)] * NX + [TOKEN],
@@ -402,15 +384,12 @@
     start = band_block[0]
     info = jnp.stack([start, x, z, core, y]).astype(jnp.int32)
     z0 = start % (NX * NZ * NC) // NC % NZ
-    core0 = start % NC
-
-    message = prep(band_block, right_sides, butterfly_diagonals)
+
+    keep, send = prep(band_block, right_sides, butterfly_diagonals)
+    message = pack(info, keep, other_core(send), butterfly_diagonals)
     pieces = [flip_x(message[s], s) for s in range(NX)]
-    top, low, ready = split_band(info, band_rows, message[0])
-    mixed = exchange_x(after(right_sides, ready))
-
-    half, other_half = solve(info, pieces, diag_inverse, ready)
-    half = jnp.where(core == core0, half, other_core(other_half))
+    mixed = exchange_x(after(right_sides, message[0]))
+    half = solve(info, pieces, diag_inverse)
 
     away = z ^ z0
     got = [flip_z(half, m) for m in (1, 2, 3)]
@@ -421,9 +400,10 @@
     *blocks, mixed_done = mid(info, mixed, pieces, half)
     line = [half] + [after(flip_x(half, t), mixed_done) for t in range(1, NX)]
     line = jnp.concatenate(line, axis=0)
+    top, low = split_band(info, band_rows, line)
 
     one, three = flip_y(line, 1), flip_y(line, 3)
-    cross = [other_core(v) for v in (one, three)]
+    cross = [other_core(after(v, top)) for v in (one, three)]
     two = flip_y(after(line, (one, three)), 2)
     one, three, token = update(info, [one, three], cross, top, low, mixed_done, 1)
     blocks[2] = after(blocks[2], token)

time: 92.3 us -> 89.2 us (0.966)
  Pallas kernels: 25.8 us -> 19.4 us
  waiting for transfers between devices: 25 us -> 30.5 us
  starting transfers between devices: 40 us -> 37.8 us
    pallas_call x10 -> x11, Pallas kernels: 25.8 us -> 19.4 us  [call(): pl.pallas_call(body, grid_spec=pltpu.PrefetchScalarGridSpec(num_scalar_pr...]
    ppermute x6, waiting for transfers between devices: 9.86 us -> 15.1 us  [flip_y(): return lax.ppermute(v, 'rhs', [(i, i ^ m) for i in range(NY)]) if m else v]
    ppermute x9, starting transfers between devices: 11.8 us -> 8.94 us  [flip_x(): lax.ppermute(v, 'rows', row_perm(lambda x, z, c: (x ^ m, z, c)))]
  transfers between devices with their start and end apart: 25 -> 25, of which waited for: 11 -> 15; matrix products, arithmetic and copies ran while one was open for 0% -> 0% of each run, Pallas kernels for 24% -> 17%
where the time goes in v5:
time: 89.2 us; the launch traced here: 88.9 us
  starting transfers between devices  37.8 us (42%)
  waiting for transfers between devices  30.5 us (34%)
  Pallas kernels  19.4 us (22%)
  between operations  1.07 us (1%)
    pallas_call x11, Pallas kernels, call(): pl.pallas_call(body, grid_spec=pltpu.PrefetchScalarGridSpec(num_scalar_pr...  19.4 us
    ppermute x6, waiting for transfers between devices, flip_y(): return lax.ppermute(v, 'rhs', [(i, i ^ m) for i in range(NY)]) if m else v  15.1 us
    ppermute x5, starting transfers between devices, other_core(): return lax.ppermute(v, 'rows', row_perm(lambda x, z, c: (x, z, 1 - c)))  9.82 us
    ppermute x4, starting transfers between devices, flip_z(): return lax.ppermute(v, 'rows', row_perm(lambda x, z, c: (x, z ^ m, c)))  9.74 us
    ppermute x9, starting transfers between devices, flip_x(): lax.ppermute(v, 'rows', row_perm(lambda x, z, c: (x ^ m, z, c)))  8.94 us
    ppermute x4, waiting for transfers between devices, flip_z(): return lax.ppermute(v, 'rows', row_perm(lambda x, z, c: (x, z ^ m, c)))  6.96 us
    ppermute x9, waiting for transfers between devices, flip_x(): lax.ppermute(v, 'rows', row_perm(lambda x, z, c: (x ^ m, z, c)))  5.78 us
    ppermute x6, starting transfers between devices, flip_y(): return lax.ppermute(v, 'rhs', [(i, i ^ m) for i in range(NY)]) if m else v  5.67 us
  transfers between devices with their start and end apart: 25, of which 15 were waited for; matrix products, arithmetic and copies ran while one was open for 0% of the time, Pallas kernels for 17%

profile of v5, /device:TPU:1, one launch (start us, length us, event | category | flops | bytes accessed | tf_op | source)
XLA Modules:
  0.0 88.9 jit_solution(636969499996324993)
XLA Ops:
  0.7 1.4 %prep.1 = (f32[72,1024]{1,0:T(8,128)S(1)}, f32[72,1024]{1,0:T(8,128)S(1)}) custom-call(s32[1]{0:T(128)} %copy.7.start, f32[4,1024,128]{2,1,0:T(8,128)} %slabs.1, f32[2,4,1024]{2,1,0:T(4,128)} %diag.1), custom_call_target="tpu_custom_call" | custom-call | tf_op jit(solution)/shard_map/prep/pallas_call | solution.py:68
  2.0 3.3 %collective-permute-start = (f32[72,1024]{1,0:T(8,128)S(1)}, f32[72,1024]{1,0:T(8,128)S(1)}, u32[]{:S(2)}, u32[]{:S(2)}) collective-permute-start(f32[72,1024]{1,0:T(8,128)S(1)} %get-tuple-element.35), channel_id=1, source_target_pairs={{0,4},{4,0},{8,12},{12,8},{16,20},{20,16},{24,28},{28,24},{32,36},... | collective-permute-start | bytes 884744 | tf_op jit(solution)/shard_map/ppermute | solution.py:48
  5.4 0.1 stack.19.info
  5.5 1.1 %collective-permute-done.came = f32[72,1024]{1,0:T(8,128)S(1)} collective-permute-done((f32[72,1024]{1,0:T(8,128)S(1)}, f32[72,1024]{1,0:T(8,128)S(1)}, u32[]{:S(2)}, u32[]{:S(2)}) %collective-permute-start) | collective-permute-done | bytes 294944 | tf_op jit(solution)/shard_map/ppermute | solution.py:48
  6.6 0.0 copy-done.1
  6.6 0.6 pack.1
  7.2 0.0 copy-start.2
  7.2 0.1 collective-permute-start.1
  7.3 1.9 %collective-permute-start.2 = (f32[24,1024]{1,0:T(8,128)S(1)}, f32[24,1024]{1,0:T(8,128)S(1)}, u32[]{:S(2)}, u32[]{:S(2)}) collective-permute-start(f32[24,1024]{1,0:T(8,128)S(1)} %get-tuple-element.39), channel_id=1, source_target_pairs={{0,128},{4,132},{8,136},{12,140},{16,144},{20,148},{24,152},{28,15... | collective-permute-start | bytes 294920 | tf_op jit(solution)/shard_map/ppermute | solution.py:29
  9.2 1.9 %collective-permute-start.3 = (f32[24,1024]{1,0:T(8,128)S(1)}, f32[24,1024]{1,0:T(8,128)S(1)}, u32[]{:S(2)}, u32[]{:S(2)}) collective-permute-start(f32[24,1024]{1,0:T(8,128)S(1)} %get-tuple-element.40), channel_id=1, source_target_pairs={{0,192},{4,196},{8,200},{12,204},{16,208},{20,212},{24,216},{28,22... | collective-permute-start | bytes 294920 | tf_op jit(solution)/shard_map/ppermute | solution.py:29
  11.2 3.6 %all-to-all-start = ((f32[4,1024,128]{2,1,0:T(8,128)}), f32[4,1024,128]{2,1,0:T(8,128)S(1)}, u32[]{:S(2)}, u32[]{:S(2)}) async-start(f32[4,1024,128]{2,1,0:T(8,128)} %slabs.1), calls=%async_computation | async-start | bytes 4194304 | tf_op jit(solution)/shard_map/all_to_all | solution.py:44
  14.8 0.0 collective-permute-done.1.refs_1_.refs_2_
  14.8 0.0 collective-permute-done.2.refs_2_.refs_3_
  14.8 1.6 %collective-permute-done.3.refs_3_.refs_4_ = f32[24,1024]{1,0:T(8,128)S(1)} collective-permute-done((f32[24,1024]{1,0:T(8,128)S(1)}, f32[24,1024]{1,0:T(8,128)S(1)}, u32[]{:S(2)}, u32[]{:S(2)}) %collective-permute-start.3) | collective-permute-done | bytes 98336 | tf_op jit(solution)/shard_map/ppermute | solution.py:29
  16.5 2.9 %solve.1 = f32[16,1024]{1,0:T(8,128)S(1)} custom-call(s32[5]{0:T(128)S(1)} %stack.19.info, f32[24,1024]{1,0:T(8,128)S(1)} %get-tuple-element.36.refs_0_.refs_1_, f32[24,1024]{1,0:T(8,128)S(1)} %collective-permute-done.1.refs_1_.refs_2_, f32[24,1024]{1,0:T(8,128)S(1)} %collective-permute-done.2.refs_2_.refs_3_, ...), custom_call_target="tpu_custom_call" | custom-call | flops 70000001024 | bytes 1048576 | tf_op jit(solution)/shard_map/solve/pallas_call | solution.py:68
  19.4 1.7 %collective-permute-start.6 = (f32[16,1024]{1,0:T(8,128)S(1)}, f32[16,1024]{1,0:T(8,128)S(1)}, u32[]{:S(2)}, u32[]{:S(2)}) collective-permute-start(f32[16,1024]{1,0:T(8,128)S(1)} %solve.1), channel_id=1, source_target_pairs={{0,8},{4,12},{8,0},{12,4},{16,24},{20,28},{24,16},{28,20},{32,40},... | collective-permute-start | bytes 196616 | tf_op jit(solution)/shard_map/ppermute | solution.py:33
  21.1 3.0 %collective-permute-start.5 = (f32[16,1024]{1,0:T(8,128)S(1)}, f32[16,1024]{1,0:T(8,128)S(1)}, u32[]{:S(2)}, u32[]{:S(2)}) collective-permute-start(f32[16,1024]{1,0:T(8,128)S(1)} %solve.1), channel_id=1, source_target_pairs={{0,16},{4,20},{8,24},{12,28},{16,0},{20,4},{24,8},{28,12},{32,48},... | collective-permute-start | bytes 196616 | tf_op jit(solution)/shard_map/ppermute | solution.py:33
  24.1 0.0 collective-permute-start.4
  24.1 0.0 collective-permute-done.6
  24.1 2.5 %collective-permute-done.5 = f32[16,1024]{1,0:T(8,128)S(1)} collective-permute-done((f32[16,1024]{1,0:T(8,128)S(1)}, f32[16,1024]{1,0:T(8,128)S(1)}, u32[]{:S(2)}, u32[]{:S(2)}) %collective-permute-start.5) | collective-permute-done | bytes 65568 | tf_op jit(solution)/shard_map/ppermute | solution.py:33
  26.6 2.5 %collective-permute-done.4 = f32[16,1024]{1,0:T(8,128)S(1)} collective-permute-done((f32[16,1024]{1,0:T(8,128)S(1)}, f32[16,1024]{1,0:T(8,128)S(1)}, u32[]{:S(2)}, u32[]{:S(2)}) %collective-permute-start.4) | collective-permute-done | bytes 65568 | tf_op jit(solution)/shard_map/ppermute | solution.py:33
  29.2 5.0 %collective-permute-start.7 = (f32[16,1024]{1,0:T(8,128)S(1)}, f32[16,1024]{1,0:T(8,128)S(1)}, u32[]{:S(2)}, u32[]{:S(2)}) collective-permute-start(f32[16,1024]{1,0:T(8,128)S(1)} %select_select_fusion), channel_id=1, source_target_pairs={{0,48},{4,52},{8,56},{12,60},{16,32},{20,36},{24,40},{28,44},{32,1... | collective-permute-start | bytes 196616 | tf_op jit(solution)/shard_map/ppermute | solution.py:33
  34.2 2.0 %collective-permute-done.7 = f32[16,1024]{1,0:T(8,128)S(1)} collective-permute-done((f32[16,1024]{1,0:T(8,128)S(1)}, f32[16,1024]{1,0:T(8,128)S(1)}, u32[]{:S(2)}, u32[]{:S(2)}) %collective-permute-start.7) | collective-permute-done | bytes 65568 | tf_op jit(solution)/shard_map/ppermute | solution.py:33
  36.2 0.1 collective-permute-start.11
  36.3 0.1 collective-permute-start.10
  36.4 3.1 %collective-permute-start.9 = (f32[16,1024]{1,0:T(8,128)S(1)}, f32[16,1024]{1,0:T(8,128)S(1)}, u32[]{:S(2)}, u32[]{:S(2)}) collective-permute-start(f32[16,1024]{1,0:T(8,128)S(1)} %broadcast_select_fusion.refs_5_), channel_id=1, source_target_pairs={{0,64},{4,68},{8,72},{12,76},{16,80},{20,84},{24,88},{28,92},{32,9... | collective-permute-start | bytes 196616 | tf_op jit(solution)/shard_map/ppermute | solution.py:29
  39.5 0.4 all-to-all-done.refs_0_
  39.9 3.4 %mid.1 = (f32[1024,128]{1,0:T(8,128)S(1)}, f32[1024,128]{1,0:T(8,128)S(1)}, f32[1024,128]{1,0:T(8,128)S(1)}, f32[1024,128]{1,0:T(8,128)S(1)}, f32[8,128]{1,0:T(8,128)S(1)}) custom-call(s32[5]{0:T(128)S(1)} %stack.19.info, f32[4,1024,128]{2,1,0:T(8,128)S(1)} %all-to-all-done.refs_0_, f32[24,1024]{1,0:T(8,128)} %copy-done.2, f32[24,1024]{1,0:T(8,128)} %copy-done.3, ...), custom_call_target="tpu_custom_call" | custom-call | flops 10000000000 | bytes 1048576 | tf_op jit(solution)/shard_map/mid/pallas_call | solution.py:68
  43.3 0.0 collective-permute-done.11
  43.3 0.0 collective-permute-done.10
  43.3 0.0 collective-permute-done.9
  43.3 2.4 %collective-permute-start.13 = (f32[64,1024]{1,0:T(8,128)S(1)}, f32[64,1024]{1,0:T(8,128)S(1)}, u32[]{:S(2)}, u32[]{:S(2)}) collective-permute-start(f32[64,1024]{1,0:T(8,128)S(1)} %pad_maximum_fusion.token.refs_0_), channel_id=1, source_target_pairs={{0,3},{1,2},{2,1},{3,0},{4,7},{5,6},{6,5},{7,4},{8,11},{9,10},{10,... | collective-permute-start | bytes 786440 | tf_op jit(solution)/shard_map/ppermute | solution.py:37
  45.8 0.0 collective-permute-start.12
  45.8 0.1 collective-permute-start.8
  45.9 0.8 collective-permute-start.17
  46.7 2.2 %split_band.1 = (bf16[1024,1024]{1,0:T(8,128)(2,1)S(1)}, bf16[1024,1024]{1,0:T(8,128)(2,1)S(1)}) custom-call(s32[5]{0:T(128)S(1)} %stack.19.info, f32[8192,128]{1,0:T(8,128)S(1)} %bitcast.13, f32[64,1024]{1,0:T(8,128)S(1)} %pad_maximum_fusion.token.refs_0_), custom_call_target="tpu_custom_call" | custom-call | flops 1000000000 | bytes 1048576 | tf_op jit(solution)/shard_map/split_band/pallas_call | solution.py:68
  48.9 1.0 %collective-permute-done.13.refs_1_ = f32[64,1024]{1,0:T(8,128)S(1)} collective-permute-done((f32[64,1024]{1,0:T(8,128)S(1)}, f32[64,1024]{1,0:T(8,128)S(1)}, u32[]{:S(2)}, u32[]{:S(2)}) %collective-permute-start.13) | collective-permute-done | bytes 262176 | tf_op jit(solution)/shard_map/ppermute | solution.py:37
  49.9 1.4 %collective-permute-done.12.refs_0_ = f32[64,1024]{1,0:T(8,128)S(1)} collective-permute-done((f32[64,1024]{1,0:T(8,128)S(1)}, f32[64,1024]{1,0:T(8,128)S(1)}, u32[]{:S(2)}, u32[]{:S(2)}) %collective-permute-start.12) | collective-permute-done | bytes 262176 | tf_op jit(solution)/shard_map/ppermute | solution.py:37
  51.3 4.2 %collective-permute-start.14 = (f32[64,1024]{1,0:T(8,128)S(1)}, f32[64,1024]{1,0:T(8,128)S(1)}, u32[]{:S(2)}, u32[]{:S(2)}) collective-permute-start(f32[64,1024]{1,0:T(8,128)S(1)} %collective-permute-done.12.refs_0_), channel_id=1, source_target_pairs={{0,4},{4,0},{8,12},{12,8},{16,20},{20,16},{24,28},{28,24},{32,36},... | collective-permute-start | bytes 786440 | tf_op jit(solution)/shard_map/ppermute | solution.py:48
  55.5 0.0 collective-permute-start.15
  55.5 0.3 collective-permute-start.19
  55.8 0.8 collective-permute-done.14.refs_2_
  56.6 0.4 collective-permute-done.15.refs_3_
  57.0 2.5 %update.3 = (f32[128,1024]{1,0:T(8,128)S(1)}, f32[128,1024]{1,0:T(8,128)S(1)}, f32[128,1024]{1,0:T(8,128)S(1)}) custom-call(s32[5]{0:T(128)S(1)} %stack.19.info, f32[64,1024]{1,0:T(8,128)S(1)} %collective-permute-done.12.refs_0_, f32[64,1024]{1,0:T(8,128)S(1)} %collective-permute-done.13.refs_1_, f32[64,1024]{1,0:T(8,128)S(1)} %collective-permute-done.14.refs_2_, ...), custom_call_target="tpu_custom_call" | custom-call | flops 1 | bytes 1048576 | tf_op jit(solution)/shard_map/update/pallas_call | solution.py:68
  59.5 0.1 collective-permute-start.21
  59.6 1.7 %collective-permute-start.23 = (f32[128,1024]{1,0:T(8,128)S(1)}, f32[128,1024]{1,0:T(8,128)S(1)}, u32[]{:S(2)}, u32[]{:S(2)}) collective-permute-start(f32[128,1024]{1,0:T(8,128)S(1)} %get-tuple-element.62), channel_id=1, source_target_pairs={{0,3},{1,2},{2,1},{3,0},{4,7},{5,6},{6,5},{7,4},{8,11},{9,10},{10,... | collective-permute-start | bytes 1572872 | tf_op jit(solution)/shard_map/ppermute | solution.py:37
  61.3 3.0 %collective-permute-done.19.refs_0_ = f32[64,1024]{1,0:T(8,128)S(1)} collective-permute-done((f32[64,1024]{1,0:T(8,128)S(1)}, f32[64,1024]{1,0:T(8,128)S(1)}, u32[]{:S(2)}, u32[]{:S(2)}) %collective-permute-start.19) | collective-permute-done | bytes 262176 | tf_op jit(solution)/shard_map/ppermute | solution.py:37
  64.3 2.3 %collective-permute-start.20 = (f32[64,1024]{1,0:T(8,128)S(1)}, f32[64,1024]{1,0:T(8,128)S(1)}, u32[]{:S(2)}, u32[]{:S(2)}) collective-permute-start(f32[64,1024]{1,0:T(8,128)S(1)} %collective-permute-done.19.refs_0_), channel_id=1, source_target_pairs={{0,4},{4,0},{8,12},{12,8},{16,20},{20,16},{24,28},{28,24},{32,36},... | collective-permute-start | bytes 786440 | tf_op jit(solution)/shard_map/ppermute | solution.py:48
  66.7 0.0 collective-permute-done.8.refs_0_.refs_1_
  66.7 0.0 collective-permute-start.18
  66.7 0.0 collective-permute-done.17.refs_1_.refs_3_
  66.7 0.8 collective-permute-start.16
  67.5 0.5 mark.2.refs_4_
  68.0 0.0 collective-permute-done.20.refs_1_
  68.0 1.7 %update.4 = (f32[128,1024]{1,0:T(8,128)S(1)}, f32[128,1024]{1,0:T(8,128)S(1)}) custom-call(s32[5]{0:T(128)S(1)} %stack.19.info, f32[64,1024]{1,0:T(8,128)S(1)} %collective-permute-done.19.refs_0_, f32[64,1024]{1,0:T(8,128)S(1)} %collective-permute-done.20.refs_1_, bf16[1024,1024]{1,0:T(8,128)(2,1)S(1)} %get-tuple-element.48.refs_4_.refs_2_, ...), custom_call_target="tpu_custom_call" | custom-call | flops 1 | bytes 1048576 | tf_op jit(solution)/shard_map/update/pallas_call | solution.py:68
  69.7 1.1 %collective-permute-start.22 = (f32[128,1024]{1,0:T(8,128)S(1)}, f32[128,1024]{1,0:T(8,128)S(1)}, u32[]{:S(2)}, u32[]{:S(2)}) collective-permute-start(f32[128,1024]{1,0:T(8,128)S(1)} %get-tuple-element.61), channel_id=1, source_target_pairs={{0,2},{1,3},{2,0},{3,1},{4,6},{5,7},{6,4},{7,5},{8,10},{9,11},{10,... | collective-permute-start | bytes 1572872 | tf_op jit(solution)/shard_map/ppermute | solution.py:37
  70.8 0.0 collective-permute-done.18.refs_1_
  70.8 1.7 %update.5 = (f32[128,1024]{1,0:T(8,128)S(1)}, f32[128,1024]{1,0:T(8,128)S(1)}) custom-call(s32[5]{0:T(128)S(1)} %stack.19.info, f32[64,1024]{1,0:T(8,128)S(1)} %pad_maximum_fusion.token.refs_0_, f32[64,1024]{1,0:T(8,128)S(1)} %collective-permute-done.18.refs_1_, bf16[1024,1024]{1,0:T(8,128)(2,1)S(1)} %get-tuple-element.48.refs_4_.refs_2_, ...), custom_call_target="tpu_custom_call" | custom-call | flops 1 | bytes 1048576 | tf_op jit(solution)/shard_map/update/pallas_call | solution.py:68
  72.5 1.7 %collective-permute-done.21.refs_0_.refs_6_ = f32[128,1024]{1,0:T(8,128)S(1)} collective-permute-done((f32[128,1024]{1,0:T(8,128)S(1)}, f32[128,1024]{1,0:T(8,128)S(1)}, u32[]{:S(2)}, u32[]{:S(2)}) %collective-permute-start.21) | collective-permute-done | bytes 524320 | tf_op jit(solution)/shard_map/ppermute | solution.py:37
  74.1 2.6 %collective-permute-done.23.refs_1_.refs_8_ = f32[128,1024]{1,0:T(8,128)S(1)} collective-permute-done((f32[128,1024]{1,0:T(8,128)S(1)}, f32[128,1024]{1,0:T(8,128)S(1)}, u32[]{:S(2)}, u32[]{:S(2)}) %collective-permute-start.23) | collective-permute-done | bytes 524320 | tf_op jit(solution)/shard_map/ppermute | solution.py:37
  76.7 0.5 mark.3.refs_9_
  77.2 4.1 %collective-permute-done.16.refs_2_ = f32[1024,128]{1,0:T(8,128)S(1)} collective-permute-done((f32[1024,128]{1,0:T(8,128)S(1)}, f32[1024,128]{1,0:T(8,128)S(1)}, u32[]{:S(2)}, u32[]{:S(2)}) %collective-permute-start.16) | collective-permute-done | bytes 524320 | tf_op jit(solution)/shard_map/ppermute | solution.py:29
  81.3 5.5 %collective-permute-done.22.refs_7_ = f32[128,1024]{1,0:T(8,128)S(1)} collective-permute-done((f32[128,1024]{1,0:T(8,128)S(1)}, f32[128,1024]{1,0:T(8,128)S(1)}, u32[]{:S(2)}, u32[]{:S(2)}) %collective-permute-start.22) | collective-permute-done | bytes 524320 | tf_op jit(solution)/shard_map/ppermute | solution.py:37
  86.8 1.9 %last.1 = f32[4,1024,128]{2,1,0:T(8,128)} custom-call(s32[5]{0:T(128)S(1)} %stack.19.info, f32[1024,128]{1,0:T(8,128)S(1)} %get-tuple-element.41.refs_0_, f32[1024,128]{1,0:T(8,128)S(1)} %collective-permute-done.8.refs_0_.refs_1_, f32[1024,128]{1,0:T(8,128)S(1)} %collective-permute-done.16.refs_2_, f32[1024,128]{1,0:T(8,128)S(1)} %collective-permute-done.17.refs_1_.refs_3_, ...), custom_call_target="tpu_custom_call" | custom-call | tf_op jit(solution)/shard_map/last/pallas_call | solution.py:68
  (13 shorter events, 0.1 us)
Async XLA Ops:
  0.0 6.6 %copy-start.1 = (f32[2,4,1024]{2,1,0:T(4,128)S(1)}, f32[2,4,1024]{2,1,0:T(4,128)}, u32[]{:S(2)}) copy-start(f32[2,4,1024]{2,1,0:T(4,128)} %diag.1) | copy-start | bytes 98308
  2.0 4.5 %collective-permute-start = (f32[72,1024]{1,0:T(8,128)S(1)}, f32[72,1024]{1,0:T(8,128)S(1)}, u32[]{:S(2)}, u32[]{:S(2)}) collective-permute-start(f32[72,1024]{1,0:T(8,128)S(1)} %get-tuple-element.35), channel_id=1, source_target_pairs={{0,4},{4,0},{8,12},{12,8},{16,20},{20,16},{24,28},{28,24},{32,36},... | collective-permute-start | bytes 884744 | tf_op jit(solution)/shard_map/ppermute | solution.py:48
  7.2 9.3 %copy-start.2 = (f32[24,1024]{1,0:T(8,128)}, f32[24,1024]{1,0:T(8,128)S(1)}, u32[]{:S(2)}) copy-start(f32[24,1024]{1,0:T(8,128)S(1)} %get-tuple-element.36.refs_0_.refs_1_) | copy-start | bytes 294916
  7.2 7.6 %collective-permute-start.1 = (f32[24,1024]{1,0:T(8,128)S(1)}, f32[24,1024]{1,0:T(8,128)S(1)}, u32[]{:S(2)}, u32[]{:S(2)}) collective-permute-start(f32[24,1024]{1,0:T(8,128)S(1)} %get-tuple-element.38), channel_id=1, source_target_pairs={{0,64},{4,68},{8,72},{12,76},{16,80},{20,84},{24,88},{28,92},{32,9... | collective-permute-start | bytes 294920 | tf_op jit(solution)/shard_map/ppermute | solution.py:29
  7.3 7.5 %collective-permute-start.2 = (f32[24,1024]{1,0:T(8,128)S(1)}, f32[24,1024]{1,0:T(8,128)S(1)}, u32[]{:S(2)}, u32[]{:S(2)}) collective-permute-start(f32[24,1024]{1,0:T(8,128)S(1)} %get-tuple-element.39), channel_id=1, source_target_pairs={{0,128},{4,132},{8,136},{12,140},{16,144},{20,148},{24,152},{28,15... | collective-permute-start | bytes 294920 | tf_op jit(solution)/shard_map/ppermute | solution.py:29
  9.2 7.2 %collective-permute-start.3 = (f32[24,1024]{1,0:T(8,128)S(1)}, f32[24,1024]{1,0:T(8,128)S(1)}, u32[]{:S(2)}, u32[]{:S(2)}) collective-permute-start(f32[24,1024]{1,0:T(8,128)S(1)} %get-tuple-element.40), channel_id=1, source_target_pairs={{0,192},{4,196},{8,200},{12,204},{16,208},{20,212},{24,216},{28,22... | collective-permute-start | bytes 294920 | tf_op jit(solution)/shard_map/ppermute | solution.py:29
  11.2 28.7 %all-to-all-start = ((f32[4,1024,128]{2,1,0:T(8,128)}), f32[4,1024,128]{2,1,0:T(8,128)S(1)}, u32[]{:S(2)}, u32[]{:S(2)}) async-start(f32[4,1024,128]{2,1,0:T(8,128)} %slabs.1), calls=%async_computation | async-start | bytes 4194304 | tf_op jit(solution)/shard_map/all_to_all | solution.py:44
  14.8 4.6 %copy-start.3 = (f32[24,1024]{1,0:T(8,128)}, f32[24,1024]{1,0:T(8,128)S(1)}, u32[]{:S(2)}) copy-start(f32[24,1024]{1,0:T(8,128)S(1)} %collective-permute-done.1.refs_1_.refs_2_) | copy-start | bytes 294916
  14.8 4.6 %copy-start.4 = (f32[24,1024]{1,0:T(8,128)}, f32[24,1024]{1,0:T(8,128)S(1)}, u32[]{:S(2)}) copy-start(f32[24,1024]{1,0:T(8,128)S(1)} %collective-permute-done.2.refs_2_.refs_3_) | copy-start | bytes 294916
  16.5 2.9 %copy-start.5 = (f32[24,1024]{1,0:T(8,128)}, f32[24,1024]{1,0:T(8,128)S(1)}, u32[]{:S(2)}) copy-start(f32[24,1024]{1,0:T(8,128)S(1)} %collective-permute-done.3.refs_3_.refs_4_) | copy-start | bytes 294916
  19.4 4.7 %collective-permute-start.6 = (f32[16,1024]{1,0:T(8,128)S(1)}, f32[16,1024]{1,0:T(8,128)S(1)}, u32[]{:S(2)}, u32[]{:S(2)}) collective-permute-start(f32[16,1024]{1,0:T(8,128)S(1)} %solve.1), channel_id=1, source_target_pairs={{0,8},{4,12},{8,0},{12,4},{16,24},{20,28},{24,16},{28,20},{32,40},... | collective-permute-start | bytes 196616 | tf_op jit(solution)/shard_map/ppermute | solution.py:33
  21.1 5.5 %collective-permute-start.5 = (f32[16,1024]{1,0:T(8,128)S(1)}, f32[16,1024]{1,0:T(8,128)S(1)}, u32[]{:S(2)}, u32[]{:S(2)}) collective-permute-start(f32[16,1024]{1,0:T(8,128)S(1)} %solve.1), channel_id=1, source_target_pairs={{0,16},{4,20},{8,24},{12,28},{16,0},{20,4},{24,8},{28,12},{32,48},... | collective-permute-start | bytes 196616 | tf_op jit(solution)/shard_map/ppermute | solution.py:33
  24.1 5.0 %collective-permute-start.4 = (f32[16,1024]{1,0:T(8,128)S(1)}, f32[16,1024]{1,0:T(8,128)S(1)}, u32[]{:S(2)}, u32[]{:S(2)}) collective-permute-start(f32[16,1024]{1,0:T(8,128)S(1)} %solve.1), channel_id=1, source_target_pairs={{0,24},{4,28},{8,16},{12,20},{16,8},{20,12},{24,0},{28,4},{32,56},... | collective-permute-start | bytes 196616 | tf_op jit(solution)/shard_map/ppermute | solution.py:33
  29.2 7.0 %collective-permute-start.7 = (f32[16,1024]{1,0:T(8,128)S(1)}, f32[16,1024]{1,0:T(8,128)S(1)}, u32[]{:S(2)}, u32[]{:S(2)}) collective-permute-start(f32[16,1024]{1,0:T(8,128)S(1)} %select_select_fusion), channel_id=1, source_target_pairs={{0,48},{4,52},{8,56},{12,60},{16,32},{20,36},{24,40},{28,44},{32,1... | collective-permute-start | bytes 196616 | tf_op jit(solution)/shard_map/ppermute | solution.py:33
  36.2 7.1 %collective-permute-start.11 = (f32[16,1024]{1,0:T(8,128)S(1)}, f32[16,1024]{1,0:T(8,128)S(1)}, u32[]{:S(2)}, u32[]{:S(2)}) collective-permute-start(f32[16,1024]{1,0:T(8,128)S(1)} %broadcast_select_fusion.refs_5_), channel_id=1, source_target_pairs={{0,192},{4,196},{8,200},{12,204},{16,208},{20,212},{24,216},{28,22... | collective-permute-start | bytes 196616 | tf_op jit(solution)/shard_map/ppermute | solution.py:29
  36.3 7.0 %collective-permute-start.10 = (f32[16,1024]{1,0:T(8,128)S(1)}, f32[16,1024]{1,0:T(8,128)S(1)}, u32[]{:S(2)}, u32[]{:S(2)}) collective-permute-start(f32[16,1024]{1,0:T(8,128)S(1)} %broadcast_select_fusion.refs_5_), channel_id=1, source_target_pairs={{0,128},{4,132},{8,136},{12,140},{16,144},{20,148},{24,152},{28,15... | collective-permute-start | bytes 196616 | tf_op jit(solution)/shard_map/ppermute | solution.py:29
  36.4 7.0 %collective-permute-start.9 = (f32[16,1024]{1,0:T(8,128)S(1)}, f32[16,1024]{1,0:T(8,128)S(1)}, u32[]{:S(2)}, u32[]{:S(2)}) collective-permute-start(f32[16,1024]{1,0:T(8,128)S(1)} %broadcast_select_fusion.refs_5_), channel_id=1, source_target_pairs={{0,64},{4,68},{8,72},{12,76},{16,80},{20,84},{24,88},{28,92},{32,9... | collective-permute-start | bytes 196616 | tf_op jit(solution)/shard_map/ppermute | solution.py:29
  39.9 6.8 %copy-start = (f32[1024,4,256]{2,1,0:T(4,128)S(1)}, f32[1024,4,256]{2,1,0:T(4,128)}, u32[]{:S(2)}) copy-start(f32[1024,4,256]{2,1,0:T(4,128)} %param.7) | copy-start | bytes 12582916
  43.3 6.5 %collective-permute-start.13 = (f32[64,1024]{1,0:T(8,128)S(1)}, f32[64,1024]{1,0:T(8,128)S(1)}, u32[]{:S(2)}, u32[]{:S(2)}) collective-permute-start(f32[64,1024]{1,0:T(8,128)S(1)} %pad_maximum_fusion.token.refs_0_), channel_id=1, source_target_pairs={{0,3},{1,2},{2,1},{3,0},{4,7},{5,6},{6,5},{7,4},{8,11},{9,10},{10,... | collective-permute-start | bytes 786440 | tf_op jit(solution)/shard_map/ppermute | solution.py:37
  45.8 5.5 %collective-permute-start.12 = (f32[64,1024]{1,0:T(8,128)S(1)}, f32[64,1024]{1,0:T(8,128)S(1)}, u32[]{:S(2)}, u32[]{:S(2)}) collective-permute-start(f32[64,1024]{1,0:T(8,128)S(1)} %pad_maximum_fusion.token.refs_0_), channel_id=1, source_target_pairs={{0,1},{1,0},{2,3},{3,2},{4,5},{5,4},{6,7},{7,6},{8,9},{9,8},{10,11... | collective-permute-start | bytes 786440 | tf_op jit(solution)/shard_map/ppermute | solution.py:37
  45.8 20.9 %collective-permute-start.8 = (f32[1024,128]{1,0:T(8,128)S(1)}, f32[1024,128]{1,0:T(8,128)S(1)}, u32[]{:S(2)}, u32[]{:S(2)}) collective-permute-start(f32[1024,128]{1,0:T(8,128)S(1)} %get-tuple-element.42), channel_id=1, source_target_pairs={{0,64},{4,68},{8,72},{12,76},{16,80},{20,84},{24,88},{28,92},{32,9... | collective-permute-start | bytes 1572872 | tf_op jit(solution)/shard_map/ppermute | solution.py:29
  45.9 20.8 %collective-permute-start.17 = (f32[1024,128]{1,0:T(8,128)S(1)}, f32[1024,128]{1,0:T(8,128)S(1)}, u32[]{:S(2)}, u32[]{:S(2)}) collective-permute-start(f32[1024,128]{1,0:T(8,128)S(1)} %get-tuple-element.54), channel_id=1, source_target_pairs={{0,192},{4,196},{8,200},{12,204},{16,208},{20,212},{24,216},{28,22... | collective-permute-start | bytes 1572872 | tf_op jit(solution)/shard_map/ppermute | solution.py:29
  51.3 5.3 %collective-permute-start.14 = (f32[64,1024]{1,0:T(8,128)S(1)}, f32[64,1024]{1,0:T(8,128)S(1)}, u32[]{:S(2)}, u32[]{:S(2)}) collective-permute-start(f32[64,1024]{1,0:T(8,128)S(1)} %collective-permute-done.12.refs_0_), channel_id=1, source_target_pairs={{0,4},{4,0},{8,12},{12,8},{16,20},{20,16},{24,28},{28,24},{32,36},... | collective-permute-start | bytes 786440 | tf_op jit(solution)/shard_map/ppermute | solution.py:48
  55.5 1.5 %collective-permute-start.15 = (f32[64,1024]{1,0:T(8,128)S(1)}, f32[64,1024]{1,0:T(8,128)S(1)}, u32[]{:S(2)}, u32[]{:S(2)}) collective-permute-start(f32[64,1024]{1,0:T(8,128)S(1)} %collective-permute-done.13.refs_1_), channel_id=1, source_target_pairs={{0,4},{4,0},{8,12},{12,8},{16,20},{20,16},{24,28},{28,24},{32,36},... | collective-permute-start | bytes 786440 | tf_op jit(solution)/shard_map/ppermute | solution.py:48
  55.5 8.9 %collective-permute-start.19 = (f32[64,1024]{1,0:T(8,128)S(1)}, f32[64,1024]{1,0:T(8,128)S(1)}, u32[]{:S(2)}, u32[]{:S(2)}) collective-permute-start(f32[64,1024]{1,0:T(8,128)S(1)} %pad_maximum_fusion.token.refs_0_), channel_id=1, source_target_pairs={{0,2},{1,3},{2,0},{3,1},{4,6},{5,7},{6,4},{7,5},{8,10},{9,11},{10,... | collective-permute-start | bytes 786440 | tf_op jit(solution)/shard_map/ppermute | solution.py:37
  59.5 14.6 %collective-permute-start.21 = (f32[128,1024]{1,0:T(8,128)S(1)}, f32[128,1024]{1,0:T(8,128)S(1)}, u32[]{:S(2)}, u32[]{:S(2)}) collective-permute-start(f32[128,1024]{1,0:T(8,128)S(1)} %get-tuple-element.60), channel_id=1, source_target_pairs={{0,1},{1,0},{2,3},{3,2},{4,5},{5,4},{6,7},{7,6},{8,9},{9,8},{10,11... | collective-permute-start | bytes 1572872 | tf_op jit(solution)/shard_map/ppermute | solution.py:37
  59.6 17.0 %collective-permute-start.23 = (f32[128,1024]{1,0:T(8,128)S(1)}, f32[128,1024]{1,0:T(8,128)S(1)}, u32[]{:S(2)}, u32[]{:S(2)}) collective-permute-start(f32[128,1024]{1,0:T(8,128)S(1)} %get-tuple-element.62), channel_id=1, source_target_pairs={{0,3},{1,2},{2,1},{3,0},{4,7},{5,6},{6,5},{7,4},{8,11},{9,10},{10,... | collective-permute-start | bytes 1572872 | tf_op jit(solution)/shard_map/ppermute | solution.py:37
  64.3 3.7 %collective-permute-start.20 = (f32[64,1024]{1,0:T(8,128)S(1)}, f32[64,1024]{1,0:T(8,128)S(1)}, u32[]{:S(2)}, u32[]{:S(2)}) collective-permute-start(f32[64,1024]{1,0:T(8,128)S(1)} %collective-permute-done.19.refs_0_), channel_id=1, source_target_pairs={{0,4},{4,0},{8,12},{12,8},{16,20},{20,16},{24,28},{28,24},{32,36},... | collective-permute-start | bytes 786440 | tf_op jit(solution)/shard_map/ppermute | solution.py:48
  66.7 4.1 %collective-permute-start.18 = (f32[64,1024]{1,0:T(8,128)S(1)}, f32[64,1024]{1,0:T(8,128)S(1)}, u32[]{:S(2)}, u32[]{:S(2)}) collective-permute-start(f32[64,1024]{1,0:T(8,128)S(1)} %pad_maximum_fusion.token.refs_0_), channel_id=1, source_target_pairs={{0,4},{4,0},{8,12},{12,8},{16,20},{20,16},{24,28},{28,24},{32,36},... | collective-permute-start | bytes 786440 | tf_op jit(solution)/shard_map/ppermute | solution.py:48
  66.7 14.7 %collective-permute-start.16 = (f32[1024,128]{1,0:T(8,128)S(1)}, f32[1024,128]{1,0:T(8,128)S(1)}, u32[]{:S(2)}, u32[]{:S(2)}) collective-permute-start(f32[1024,128]{1,0:T(8,128)S(1)} %get-tuple-element.53), channel_id=1, source_target_pairs={{0,128},{4,132},{8,136},{12,140},{16,144},{20,148},{24,152},{28,15... | collective-permute-start | bytes 1572872 | tf_op jit(solution)/shard_map/ppermute | solution.py:29
  69.7 17.1 %collective-permute-start.22 = (f32[128,1024]{1,0:T(8,128)S(1)}, f32[128,1024]{1,0:T(8,128)S(1)}, u32[]{:S(2)}, u32[]{:S(2)}) collective-permute-start(f32[128,1024]{1,0:T(8,128)S(1)} %get-tuple-element.61), channel_id=1, source_target_pairs={{0,2},{1,3},{2,0},{3,1},{4,6},{5,7},{6,4},{7,5},{8,10},{9,11},{10,... | collective-permute-start | bytes 1572872 | tf_op jit(solution)/shard_map/ppermute | solution.py:37

commit v6 on v5

--- a/solution.py
+++ b/solution.py
@@ -331,45 +331,104 @@
     return ((info[1] ^ step) * NX + info[1]) * (NZ * NC) + info[2] * NC + info[3]
 
 
-def last_kernel(info, *refs):
-    moved, mine, parts, out, block, went = refs[:4], refs[4], refs[5:9], *refs[10:]
+def quarter(info, q):
+    return pl.ds(pl.multiple_of(256 * (info[4] ^ q), 256), 256)
+
+
+def columns(info, s):
+    return pl.ds(pl.multiple_of(256 * (info[1] ^ s), 256), 256)
+
+
+NEAR = (0, 1, 3)
+
+
+def send(copies, source, out, done):
+    copies.append(pltpu.make_async_copy(source, out, done))
+    copies[-1].start()
+
+
+def subtract_kernel(info, *refs):
+    moved, mine, parts, (out, block, went) = refs[:3], refs[3], refs[4:7], refs[7:]
     start, copies = info[0], []
-    for s in range(NX):
+    for j, s in enumerate(NEAR):
         index = block_index(info, s)
 
         @pl.when(index < start)
         def _():
-            block[s] = moved[s][...]
+            block[j] = moved[j][...]
 
         @pl.when(index > start)
         def _():
-            column = pl.ds(pl.multiple_of(256 * (info[1] ^ s), 256), 256)
-            for q in range(NY):
-                at = pl.ds(pl.multiple_of(256 * (info[4] ^ q), 256), 256)
-                block[s, at, :] = moved[s][at, :] - parts[q][:, column].T
+            for part, q in zip(parts, NEAR):
+                at = quarter(info, q)
+                block[j, at, :] = moved[j][at, :] - part[:, columns(info, s)].T
 
         @pl.when(index == start)
         def _():
-            block[s] = mine[...].T
-
-        copies.append(pltpu.make_async_copy(block.at[s], out.at[info[1] ^ s], went.at[s]))
-        copies[s].start()
+            block[j] = mine[...].T
+
+        for i, q in enumerate(NEAR):
+            at = quarter(info, q)
+            send(copies, block.at[j, at], out.at[info[1] ^ s, at], went.at[j, i])
     for copy in copies:
         copy.wait()
 
 
-def last(info, moved, mine, parts, token):
+def subtract(info, moved, mine, parts):
+    return call(
+        subtract_kernel,
+        "subtract",
+        1,
+        info,
+        (*moved, mine, *parts),
+        [whole(NB, 128)] * 3 + [whole(128, NB)] * 4,
+        ANY,
+        pltpu.HBM((4, NB, 128), F32),
+        12,
+        [pltpu.VMEM((3, NB, 128), F32), pltpu.SemaphoreType.DMA((3, 3))],
+        OWN_HINT,
+    )
+
+
+def last_kernel(info, before, *refs):
+    moved, mine, parts, (out, block, went) = refs[:4], refs[4], refs[5:9], refs[9:]
+    start, copies = info[0], []
+    for s in (2, 0, 1, 3):
+        index = block_index(info, s)
+        quarters = range(NY) if s == 2 else (2,)
+        for q in quarters:
+            at = quarter(info, q)
+
+            @pl.when(index < start)
+            def _():
+                block[s, at, :] = moved[s][at, :]
+
+            @pl.when(index > start)
+            def _():
+                block[s, at, :] = moved[s][at, :] - parts[q][:, columns(info, s)].T
+
+            @pl.when(index == start)
+            def _():
+                block[s, at, :] = mine[:, at].T
+
+            send(copies, block.at[s, at], out.at[info[1] ^ s, at], went.at[s, q])
+    for copy in copies:
+        copy.wait()
+
+
+def last(info, before, moved, mine, parts):
     return call(
         last_kernel,
         "last",
         1,
         info,
-        (*moved, mine, *parts, token),
-        [whole(NB, 128)] * NX + [whole(128, NB)] * (NY + 1) + [ANY],
+        (before, *moved, mine, *parts),
+        [ANY] + [whole(NB, 128)] * 4 + [whole(128, NB)] * (NY + 1),
         ANY,
         pltpu.HBM((4, NB, 128), F32),
         12,
-        [pltpu.VMEM((4, NB, 128), F32), pltpu.SemaphoreType.DMA((4,))],
+        [pltpu.VMEM((4, NB, 128), F32), pltpu.SemaphoreType.DMA((4, 4))],
+        aliases={1: 0},
     )
 
 
@@ -413,8 +472,8 @@
     two, token = update(info, [two], [other_core(two)], top, low, token, 1)
     zero, mine = update(info, [line], [other_core(line)], top, low, token, 1)
     one, three = flip_y(one, 1), flip_y(three, 3)
-    token = mark_after(info, [one, three, zero], OWN_HINT)
-    return last(info, moved, mine, [zero, one, flip_y(two, 2), three], token)
+    before = subtract(info, [moved[i] for i in NEAR], mine, [zero, one, three])
+    return last(info, before, moved, mine, [zero, one, flip_y(two, 2), three])
 
 
 def solution(mesh):

time: 89.2 us -> 89.1 us (level)
  waiting for transfers between devices: 30.5 us -> 29.4 us
    ppermute x9, waiting for transfers between devices: 5.78 us -> 4.65 us  [flip_x(): lax.ppermute(v, 'rows', row_perm(lambda x, z, c: (x ^ m, z, c)))]
  transfers between devices with their start and end apart: 25 -> 25, of which waited for: 15 -> 15; matrix products, arithmetic and copies ran while one was open for 0% -> 0% of each run, Pallas kernels for 17% -> 19%
where the time goes in v6:
time: 89.1 us; the launch traced here: 88.6 us
  starting transfers between devices  37.8 us (42%)
  waiting for transfers between devices  29.4 us (33%)
  Pallas kernels  20.2 us (23%)
  between operations  1.07 us (1%)
    pallas_call x11, Pallas kernels, call(): pl.pallas_call(body, grid_spec=pltpu.PrefetchScalarGridSpec(num_scalar_pr...  20.2 us
    ppermute x6, waiting for transfers between devices, flip_y(): return lax.ppermute(v, 'rhs', [(i, i ^ m) for i in range(NY)]) if m else v  15.1 us
    ppermute x5, starting transfers between devices, other_core(): return lax.ppermute(v, 'rows', row_perm(lambda x, z, c: (x, z, 1 - c)))  9.82 us
    ppermute x4, starting transfers between devices, flip_z(): return lax.ppermute(v, 'rows', row_perm(lambda x, z, c: (x, z ^ m, c)))  9.74 us
    ppermute x9, starting transfers between devices, flip_x(): lax.ppermute(v, 'rows', row_perm(lambda x, z, c: (x ^ m, z, c)))  8.94 us
    ppermute x4, waiting for transfers between devices, flip_z(): return lax.ppermute(v, 'rows', row_perm(lambda x, z, c: (x, z ^ m, c)))  6.96 us
    ppermute x6, starting transfers between devices, flip_y(): return lax.ppermute(v, 'rhs', [(i, i ^ m) for i in range(NY)]) if m else v  5.67 us
    ppermute x9, waiting for transfers between devices, flip_x(): lax.ppermute(v, 'rows', row_perm(lambda x, z, c: (x ^ m, z, c)))  4.65 us
  transfers between devices with their start and end apart: 25, of which 15 were waited for; matrix products, arithmetic and copies ran while one was open for 0% of the time, Pallas kernels for 19%

profile of v6, /device:TPU:1, one launch (start us, length us, event | category | flops | bytes accessed | tf_op | source)
XLA Modules:
  0.0 88.6 jit_solution(15969679950895509099)
XLA Ops:
  0.7 1.4 %prep.1 = (f32[72,1024]{1,0:T(8,128)S(1)}, f32[72,1024]{1,0:T(8,128)S(1)}) custom-call(s32[1]{0:T(128)} %copy.9.start, f32[4,1024,128]{2,1,0:T(8,128)} %slabs.1, f32[2,4,1024]{2,1,0:T(4,128)} %diag.1), custom_call_target="tpu_custom_call" | custom-call | tf_op jit(solution)/shard_map/prep/pallas_call | solution.py:68
  2.0 3.3 %collective-permute-start = (f32[72,1024]{1,0:T(8,128)S(1)}, f32[72,1024]{1,0:T(8,128)S(1)}, u32[]{:S(2)}, u32[]{:S(2)}) collective-permute-start(f32[72,1024]{1,0:T(8,128)S(1)} %get-tuple-element.35), channel_id=1, source_target_pairs={{0,4},{4,0},{8,12},{12,8},{16,20},{20,16},{24,28},{28,24},{32,36},... | collective-permute-start | bytes 884744 | tf_op jit(solution)/shard_map/ppermute | solution.py:48
  5.4 0.1 stack.19.info
  5.5 1.1 %collective-permute-done.came = f32[72,1024]{1,0:T(8,128)S(1)} collective-permute-done((f32[72,1024]{1,0:T(8,128)S(1)}, f32[72,1024]{1,0:T(8,128)S(1)}, u32[]{:S(2)}, u32[]{:S(2)}) %collective-permute-start) | collective-permute-done | bytes 294944 | tf_op jit(solution)/shard_map/ppermute | solution.py:48
  6.6 0.0 copy-done.1
  6.6 0.6 pack.1
  7.2 0.0 copy-start.2
  7.2 0.1 collective-permute-start.1
  7.3 1.9 %collective-permute-start.2 = (f32[24,1024]{1,0:T(8,128)S(1)}, f32[24,1024]{1,0:T(8,128)S(1)}, u32[]{:S(2)}, u32[]{:S(2)}) collective-permute-start(f32[24,1024]{1,0:T(8,128)S(1)} %get-tuple-element.39), channel_id=1, source_target_pairs={{0,128},{4,132},{8,136},{12,140},{16,144},{20,148},{24,152},{28,15... | collective-permute-start | bytes 294920 | tf_op jit(solution)/shard_map/ppermute | solution.py:29
  9.2 1.9 %collective-permute-start.3 = (f32[24,1024]{1,0:T(8,128)S(1)}, f32[24,1024]{1,0:T(8,128)S(1)}, u32[]{:S(2)}, u32[]{:S(2)}) collective-permute-start(f32[24,1024]{1,0:T(8,128)S(1)} %get-tuple-element.40), channel_id=1, source_target_pairs={{0,192},{4,196},{8,200},{12,204},{16,208},{20,212},{24,216},{28,22... | collective-permute-start | bytes 294920 | tf_op jit(solution)/shard_map/ppermute | solution.py:29
  11.2 3.6 %all-to-all-start = ((f32[4,1024,128]{2,1,0:T(8,128)}), f32[4,1024,128]{2,1,0:T(8,128)S(1)}, u32[]{:S(2)}, u32[]{:S(2)}) async-start(f32[4,1024,128]{2,1,0:T(8,128)} %slabs.1), calls=%async_computation | async-start | bytes 4194304 | tf_op jit(solution)/shard_map/all_to_all | solution.py:44
  14.8 0.0 collective-permute-done.1.refs_1_.refs_2_
  14.8 0.0 collective-permute-done.2.refs_2_.refs_3_
  14.8 1.6 %collective-permute-done.3.refs_3_.refs_4_ = f32[24,1024]{1,0:T(8,128)S(1)} collective-permute-done((f32[24,1024]{1,0:T(8,128)S(1)}, f32[24,1024]{1,0:T(8,128)S(1)}, u32[]{:S(2)}, u32[]{:S(2)}) %collective-permute-start.3) | collective-permute-done | bytes 98336 | tf_op jit(solution)/shard_map/ppermute | solution.py:29
  16.5 2.9 %solve.1 = f32[16,1024]{1,0:T(8,128)S(1)} custom-call(s32[5]{0:T(128)S(1)} %stack.19.info, f32[24,1024]{1,0:T(8,128)S(1)} %get-tuple-element.36.refs_0_.refs_1_, f32[24,1024]{1,0:T(8,128)S(1)} %collective-permute-done.1.refs_1_.refs_2_, f32[24,1024]{1,0:T(8,128)S(1)} %collective-permute-done.2.refs_2_.refs_3_, ...), custom_call_target="tpu_custom_call" | custom-call | flops 70000001024 | bytes 1048576 | tf_op jit(solution)/shard_map/solve/pallas_call | solution.py:68
  19.4 1.7 %collective-permute-start.6 = (f32[16,1024]{1,0:T(8,128)S(1)}, f32[16,1024]{1,0:T(8,128)S(1)}, u32[]{:S(2)}, u32[]{:S(2)}) collective-permute-start(f32[16,1024]{1,0:T(8,128)S(1)} %solve.1), channel_id=1, source_target_pairs={{0,8},{4,12},{8,0},{12,4},{16,24},{20,28},{24,16},{28,20},{32,40},... | collective-permute-start | bytes 196616 | tf_op jit(solution)/shard_map/ppermute | solution.py:33
  21.1 3.0 %collective-permute-start.5 = (f32[16,1024]{1,0:T(8,128)S(1)}, f32[16,1024]{1,0:T(8,128)S(1)}, u32[]{:S(2)}, u32[]{:S(2)}) collective-permute-start(f32[16,1024]{1,0:T(8,128)S(1)} %solve.1), channel_id=1, source_target_pairs={{0,16},{4,20},{8,24},{12,28},{16,0},{20,4},{24,8},{28,12},{32,48},... | collective-permute-start | bytes 196616 | tf_op jit(solution)/shard_map/ppermute | solution.py:33
  24.1 0.0 collective-permute-start.4
  24.1 0.0 collective-permute-done.6
  24.1 2.5 %collective-permute-done.5 = f32[16,1024]{1,0:T(8,128)S(1)} collective-permute-done((f32[16,1024]{1,0:T(8,128)S(1)}, f32[16,1024]{1,0:T(8,128)S(1)}, u32[]{:S(2)}, u32[]{:S(2)}) %collective-permute-start.5) | collective-permute-done | bytes 65568 | tf_op jit(solution)/shard_map/ppermute | solution.py:33
  26.6 2.5 %collective-permute-done.4 = f32[16,1024]{1,0:T(8,128)S(1)} collective-permute-done((f32[16,1024]{1,0:T(8,128)S(1)}, f32[16,1024]{1,0:T(8,128)S(1)}, u32[]{:S(2)}, u32[]{:S(2)}) %collective-permute-start.4) | collective-permute-done | bytes 65568 | tf_op jit(solution)/shard_map/ppermute | solution.py:33
  29.2 5.0 %collective-permute-start.7 = (f32[16,1024]{1,0:T(8,128)S(1)}, f32[16,1024]{1,0:T(8,128)S(1)}, u32[]{:S(2)}, u32[]{:S(2)}) collective-permute-start(f32[16,1024]{1,0:T(8,128)S(1)} %select_select_fusion), channel_id=1, source_target_pairs={{0,48},{4,52},{8,56},{12,60},{16,32},{20,36},{24,40},{28,44},{32,1... | collective-permute-start | bytes 196616 | tf_op jit(solution)/shard_map/ppermute | solution.py:33
  34.2 2.0 %collective-permute-done.7 = f32[16,1024]{1,0:T(8,128)S(1)} collective-permute-done((f32[16,1024]{1,0:T(8,128)S(1)}, f32[16,1024]{1,0:T(8,128)S(1)}, u32[]{:S(2)}, u32[]{:S(2)}) %collective-permute-start.7) | collective-permute-done | bytes 65568 | tf_op jit(solution)/shard_map/ppermute | solution.py:33
  36.2 0.1 collective-permute-start.12
  36.3 0.1 collective-permute-start.11
  36.4 3.1 %collective-permute-start.10 = (f32[16,1024]{1,0:T(8,128)S(1)}, f32[16,1024]{1,0:T(8,128)S(1)}, u32[]{:S(2)}, u32[]{:S(2)}) collective-permute-start(f32[16,1024]{1,0:T(8,128)S(1)} %broadcast_select_fusion.refs_5_), channel_id=1, source_target_pairs={{0,64},{4,68},{8,72},{12,76},{16,80},{20,84},{24,88},{28,92},{32,9... | collective-permute-start | bytes 196616 | tf_op jit(solution)/shard_map/ppermute | solution.py:29
  39.5 0.4 all-to-all-done.refs_0_
  39.9 3.4 %mid.1 = (f32[1024,128]{1,0:T(8,128)S(1)}, f32[1024,128]{1,0:T(8,128)S(1)}, f32[1024,128]{1,0:T(8,128)S(1)}, f32[1024,128]{1,0:T(8,128)S(1)}, f32[8,128]{1,0:T(8,128)S(1)}) custom-call(s32[5]{0:T(128)S(1)} %stack.19.info, f32[4,1024,128]{2,1,0:T(8,128)S(1)} %all-to-all-done.refs_0_, f32[24,1024]{1,0:T(8,128)} %copy-done.2, f32[24,1024]{1,0:T(8,128)} %copy-done.3, ...), custom_call_target="tpu_custom_call" | custom-call | flops 10000000000 | bytes 1048576 | tf_op jit(solution)/shard_map/mid/pallas_call | solution.py:68
  43.3 0.0 collective-permute-done.12
  43.3 0.0 collective-permute-done.11
  43.3 0.0 collective-permute-done.10
  43.3 2.4 %collective-permute-start.15 = (f32[64,1024]{1,0:T(8,128)S(1)}, f32[64,1024]{1,0:T(8,128)S(1)}, u32[]{:S(2)}, u32[]{:S(2)}) collective-permute-start(f32[64,1024]{1,0:T(8,128)S(1)} %pad_maximum_fusion.token.refs_0_), channel_id=1, source_target_pairs={{0,3},{1,2},{2,1},{3,0},{4,7},{5,6},{6,5},{7,4},{8,11},{9,10},{10,... | collective-permute-start | bytes 786440 | tf_op jit(solution)/shard_map/ppermute | solution.py:37
  45.8 0.0 collective-permute-start.14
  45.8 0.1 collective-permute-start.8
  45.9 0.8 collective-permute-start.9
  46.7 2.2 %split_band.1 = (bf16[1024,1024]{1,0:T(8,128)(2,1)S(1)}, bf16[1024,1024]{1,0:T(8,128)(2,1)S(1)}) custom-call(s32[5]{0:T(128)S(1)} %stack.19.info, f32[8192,128]{1,0:T(8,128)S(1)} %bitcast.13, f32[64,1024]{1,0:T(8,128)S(1)} %pad_maximum_fusion.token.refs_0_), custom_call_target="tpu_custom_call" | custom-call | flops 1000000000 | bytes 1048576 | tf_op jit(solution)/shard_map/split_band/pallas_call | solution.py:68
  48.9 1.0 %collective-permute-done.15.refs_1_ = f32[64,1024]{1,0:T(8,128)S(1)} collective-permute-done((f32[64,1024]{1,0:T(8,128)S(1)}, f32[64,1024]{1,0:T(8,128)S(1)}, u32[]{:S(2)}, u32[]{:S(2)}) %collective-permute-start.15) | collective-permute-done | bytes 262176 | tf_op jit(solution)/shard_map/ppermute | solution.py:37
  49.9 1.4 %collective-permute-done.14.refs_0_ = f32[64,1024]{1,0:T(8,128)S(1)} collective-permute-done((f32[64,1024]{1,0:T(8,128)S(1)}, f32[64,1024]{1,0:T(8,128)S(1)}, u32[]{:S(2)}, u32[]{:S(2)}) %collective-permute-start.14) | collective-permute-done | bytes 262176 | tf_op jit(solution)/shard_map/ppermute | solution.py:37
  51.3 4.2 %collective-permute-start.17 = (f32[64,1024]{1,0:T(8,128)S(1)}, f32[64,1024]{1,0:T(8,128)S(1)}, u32[]{:S(2)}, u32[]{:S(2)}) collective-permute-start(f32[64,1024]{1,0:T(8,128)S(1)} %collective-permute-done.14.refs_0_), channel_id=1, source_target_pairs={{0,4},{4,0},{8,12},{12,8},{16,20},{20,16},{24,28},{28,24},{32,36},... | collective-permute-start | bytes 786440 | tf_op jit(solution)/shard_map/ppermute | solution.py:48
  55.5 0.0 collective-permute-start.18
  55.5 0.3 collective-permute-start.16
  55.8 0.8 collective-permute-done.17.refs_2_
  56.6 0.4 collective-permute-done.18.refs_3_
  57.0 2.5 %update.3 = (f32[128,1024]{1,0:T(8,128)S(1)}, f32[128,1024]{1,0:T(8,128)S(1)}, f32[128,1024]{1,0:T(8,128)S(1)}) custom-call(s32[5]{0:T(128)S(1)} %stack.19.info, f32[64,1024]{1,0:T(8,128)S(1)} %collective-permute-done.14.refs_0_, f32[64,1024]{1,0:T(8,128)S(1)} %collective-permute-done.15.refs_1_, f32[64,1024]{1,0:T(8,128)S(1)} %collective-permute-done.17.refs_2_, ...), custom_call_target="tpu_custom_call" | custom-call | flops 1 | bytes 1048576 | tf_op jit(solution)/shard_map/update/pallas_call | solution.py:68
  59.5 0.1 collective-permute-start.20
  59.6 1.7 %collective-permute-start.21 = (f32[128,1024]{1,0:T(8,128)S(1)}, f32[128,1024]{1,0:T(8,128)S(1)}, u32[]{:S(2)}, u32[]{:S(2)}) collective-permute-start(f32[128,1024]{1,0:T(8,128)S(1)} %get-tuple-element.59), channel_id=1, source_target_pairs={{0,3},{1,2},{2,1},{3,0},{4,7},{5,6},{6,5},{7,4},{8,11},{9,10},{10,... | collective-permute-start | bytes 1572872 | tf_op jit(solution)/shard_map/ppermute | solution.py:37
  61.3 3.0 %collective-permute-done.16.refs_0_ = f32[64,1024]{1,0:T(8,128)S(1)} collective-permute-done((f32[64,1024]{1,0:T(8,128)S(1)}, f32[64,1024]{1,0:T(8,128)S(1)}, u32[]{:S(2)}, u32[]{:S(2)}) %collective-permute-start.16) | collective-permute-done | bytes 262176 | tf_op jit(solution)/shard_map/ppermute | solution.py:37
  64.3 2.3 %collective-permute-start.19 = (f32[64,1024]{1,0:T(8,128)S(1)}, f32[64,1024]{1,0:T(8,128)S(1)}, u32[]{:S(2)}, u32[]{:S(2)}) collective-permute-start(f32[64,1024]{1,0:T(8,128)S(1)} %collective-permute-done.16.refs_0_), channel_id=1, source_target_pairs={{0,4},{4,0},{8,12},{12,8},{16,20},{20,16},{24,28},{28,24},{32,36},... | collective-permute-start | bytes 786440 | tf_op jit(solution)/shard_map/ppermute | solution.py:48
  66.7 0.0 collective-permute-done.8.refs_0_.refs_1_
  66.7 0.0 collective-permute-start.13
  66.7 0.0 collective-permute-done.9.refs_1_.refs_2_.refs_3_
  66.7 0.8 collective-permute-start.22
  67.5 0.5 mark.1.refs_4_
  68.0 0.0 collective-permute-done.19.refs_1_
  68.0 1.7 %update.4 = (f32[128,1024]{1,0:T(8,128)S(1)}, f32[128,1024]{1,0:T(8,128)S(1)}) custom-call(s32[5]{0:T(128)S(1)} %stack.19.info, f32[64,1024]{1,0:T(8,128)S(1)} %collective-permute-done.16.refs_0_, f32[64,1024]{1,0:T(8,128)S(1)} %collective-permute-done.19.refs_1_, bf16[1024,1024]{1,0:T(8,128)(2,1)S(1)} %get-tuple-element.48.refs_4_.refs_2_, ...), custom_call_target="tpu_custom_call" | custom-call | flops 1 | bytes 1048576 | tf_op jit(solution)/shard_map/update/pallas_call | solution.py:68
  69.7 1.1 %collective-permute-start.23 = (f32[128,1024]{1,0:T(8,128)S(1)}, f32[128,1024]{1,0:T(8,128)S(1)}, u32[]{:S(2)}, u32[]{:S(2)}) collective-permute-start(f32[128,1024]{1,0:T(8,128)S(1)} %get-tuple-element.62), channel_id=1, source_target_pairs={{0,2},{1,3},{2,0},{3,1},{4,6},{5,7},{6,4},{7,5},{8,10},{9,11},{10,... | collective-permute-start | bytes 1572872 | tf_op jit(solution)/shard_map/ppermute | solution.py:37
  70.8 0.0 collective-permute-done.13.refs_1_
  70.8 1.7 %update.5 = (f32[128,1024]{1,0:T(8,128)S(1)}, f32[128,1024]{1,0:T(8,128)S(1)}) custom-call(s32[5]{0:T(128)S(1)} %stack.19.info, f32[64,1024]{1,0:T(8,128)S(1)} %pad_maximum_fusion.token.refs_0_, f32[64,1024]{1,0:T(8,128)S(1)} %collective-permute-done.13.refs_1_, bf16[1024,1024]{1,0:T(8,128)(2,1)S(1)} %get-tuple-element.48.refs_4_.refs_2_, ...), custom_call_target="tpu_custom_call" | custom-call | flops 1 | bytes 1048576 | tf_op jit(solution)/shard_map/update/pallas_call | solution.py:68
  72.5 1.7 %collective-permute-done.20.refs_5_.refs_6_ = f32[128,1024]{1,0:T(8,128)S(1)} collective-permute-done((f32[128,1024]{1,0:T(8,128)S(1)}, f32[128,1024]{1,0:T(8,128)S(1)}, u32[]{:S(2)}, u32[]{:S(2)}) %collective-permute-start.20) | collective-permute-done | bytes 524320 | tf_op jit(solution)/shard_map/ppermute | solution.py:37
  74.1 2.6 %collective-permute-done.21.refs_6_.refs_8_ = f32[128,1024]{1,0:T(8,128)S(1)} collective-permute-done((f32[128,1024]{1,0:T(8,128)S(1)}, f32[128,1024]{1,0:T(8,128)S(1)}, u32[]{:S(2)}, u32[]{:S(2)}) %collective-permute-start.21) | collective-permute-done | bytes 524320 | tf_op jit(solution)/shard_map/ppermute | solution.py:37
  76.7 1.7 %subtract.1.before = f32[4,1024,128]{2,1,0:T(8,128)} custom-call(s32[5]{0:T(128)S(1)} %stack.19.info, f32[1024,128]{1,0:T(8,128)S(1)} %get-tuple-element.41.refs_0_, f32[1024,128]{1,0:T(8,128)S(1)} %collective-permute-done.8.refs_0_.refs_1_, f32[1024,128]{1,0:T(8,128)S(1)} %collective-permute-done.9.refs_1_.refs_2_.refs_3_, ...), custom_call_target="tpu_custom_call" | custom-call | flops 3000000000 | bytes 1048576 | tf_op jit(solution)/shard_map/subtract/pallas_call | solution.py:68
  78.4 3.0 %collective-permute-done.22.refs_2_ = f32[1024,128]{1,0:T(8,128)S(1)} collective-permute-done((f32[1024,128]{1,0:T(8,128)S(1)}, f32[1024,128]{1,0:T(8,128)S(1)}, u32[]{:S(2)}, u32[]{:S(2)}) %collective-permute-start.22) | collective-permute-done | bytes 524320 | tf_op jit(solution)/shard_map/ppermute | solution.py:29
  81.3 5.5 %collective-permute-done.23.refs_7_ = f32[128,1024]{1,0:T(8,128)S(1)} collective-permute-done((f32[128,1024]{1,0:T(8,128)S(1)}, f32[128,1024]{1,0:T(8,128)S(1)}, u32[]{:S(2)}, u32[]{:S(2)}) %collective-permute-start.23) | collective-permute-done | bytes 524320 | tf_op jit(solution)/shard_map/ppermute | solution.py:37
  86.8 1.6 %last.1 = f32[4,1024,128]{2,1,0:T(8,128)} custom-call(s32[5]{0:T(128)S(1)} %stack.19.info, f32[4,1024,128]{2,1,0:T(8,128)} %subtract.1.before, f32[1024,128]{1,0:T(8,128)S(1)} %get-tuple-element.41.refs_0_, f32[1024,128]{1,0:T(8,128)S(1)} %collective-permute-done.8.refs_0_.refs_1_, ...), custom_call_target="tpu_custom_call", output_to_operand_aliasing={{}: (1, {})} | custom-call | tf_op jit(solution)/shard_map/last/pallas_call | solution.py:68
  (13 shorter events, 0.1 us)
Async XLA Ops:
  0.0 6.6 %copy-start.1 = (f32[2,4,1024]{2,1,0:T(4,128)S(1)}, f32[2,4,1024]{2,1,0:T(4,128)}, u32[]{:S(2)}) copy-start(f32[2,4,1024]{2,1,0:T(4,128)} %diag.1) | copy-start | bytes 98308
  2.0 4.5 %collective-permute-start = (f32[72,1024]{1,0:T(8,128)S(1)}, f32[72,1024]{1,0:T(8,128)S(1)}, u32[]{:S(2)}, u32[]{:S(2)}) collective-permute-start(f32[72,1024]{1,0:T(8,128)S(1)} %get-tuple-element.35), channel_id=1, source_target_pairs={{0,4},{4,0},{8,12},{12,8},{16,20},{20,16},{24,28},{28,24},{32,36},... | collective-permute-start | bytes 884744 | tf_op jit(solution)/shard_map/ppermute | solution.py:48
  7.2 9.3 %copy-start.2 = (f32[24,1024]{1,0:T(8,128)}, f32[24,1024]{1,0:T(8,128)S(1)}, u32[]{:S(2)}) copy-start(f32[24,1024]{1,0:T(8,128)S(1)} %get-tuple-element.36.refs_0_.refs_1_) | copy-start | bytes 294916
  7.2 7.6 %collective-permute-start.1 = (f32[24,1024]{1,0:T(8,128)S(1)}, f32[24,1024]{1,0:T(8,128)S(1)}, u32[]{:S(2)}, u32[]{:S(2)}) collective-permute-start(f32[24,1024]{1,0:T(8,128)S(1)} %get-tuple-element.38), channel_id=1, source_target_pairs={{0,64},{4,68},{8,72},{12,76},{16,80},{20,84},{24,88},{28,92},{32,9... | collective-permute-start | bytes 294920 | tf_op jit(solution)/shard_map/ppermute | solution.py:29
  7.3 7.5 %collective-permute-start.2 = (f32[24,1024]{1,0:T(8,128)S(1)}, f32[24,1024]{1,0:T(8,128)S(1)}, u32[]{:S(2)}, u32[]{:S(2)}) collective-permute-start(f32[24,1024]{1,0:T(8,128)S(1)} %get-tuple-element.39), channel_id=1, source_target_pairs={{0,128},{4,132},{8,136},{12,140},{16,144},{20,148},{24,152},{28,15... | collective-permute-start | bytes 294920 | tf_op jit(solution)/shard_map/ppermute | solution.py:29
  9.2 7.2 %collective-permute-start.3 = (f32[24,1024]{1,0:T(8,128)S(1)}, f32[24,1024]{1,0:T(8,128)S(1)}, u32[]{:S(2)}, u32[]{:S(2)}) collective-permute-start(f32[24,1024]{1,0:T(8,128)S(1)} %get-tuple-element.40), channel_id=1, source_target_pairs={{0,192},{4,196},{8,200},{12,204},{16,208},{20,212},{24,216},{28,22... | collective-permute-start | bytes 294920 | tf_op jit(solution)/shard_map/ppermute | solution.py:29
  11.2 28.7 %all-to-all-start = ((f32[4,1024,128]{2,1,0:T(8,128)}), f32[4,1024,128]{2,1,0:T(8,128)S(1)}, u32[]{:S(2)}, u32[]{:S(2)}) async-start(f32[4,1024,128]{2,1,0:T(8,128)} %slabs.1), calls=%async_computation | async-start | bytes 4194304 | tf_op jit(solution)/shard_map/all_to_all | solution.py:44
  14.8 4.6 %copy-start.3 = (f32[24,1024]{1,0:T(8,128)}, f32[24,1024]{1,0:T(8,128)S(1)}, u32[]{:S(2)}) copy-start(f32[24,1024]{1,0:T(8,128)S(1)} %collective-permute-done.1.refs_1_.refs_2_) | copy-start | bytes 294916
  14.8 4.6 %copy-start.4 = (f32[24,1024]{1,0:T(8,128)}, f32[24,1024]{1,0:T(8,128)S(1)}, u32[]{:S(2)}) copy-start(f32[24,1024]{1,0:T(8,128)S(1)} %collective-permute-done.2.refs_2_.refs_3_) | copy-start | bytes 294916
  16.5 2.9 %copy-start.5 = (f32[24,1024]{1,0:T(8,128)}, f32[24,1024]{1,0:T(8,128)S(1)}, u32[]{:S(2)}) copy-start(f32[24,1024]{1,0:T(8,128)S(1)} %collective-permute-done.3.refs_3_.refs_4_) | copy-start | bytes 294916
  19.4 4.7 %collective-permute-start.6 = (f32[16,1024]{1,0:T(8,128)S(1)}, f32[16,1024]{1,0:T(8,128)S(1)}, u32[]{:S(2)}, u32[]{:S(2)}) collective-permute-start(f32[16,1024]{1,0:T(8,128)S(1)} %solve.1), channel_id=1, source_target_pairs={{0,8},{4,12},{8,0},{12,4},{16,24},{20,28},{24,16},{28,20},{32,40},... | collective-permute-start | bytes 196616 | tf_op jit(solution)/shard_map/ppermute | solution.py:33
  21.1 5.5 %collective-permute-start.5 = (f32[16,1024]{1,0:T(8,128)S(1)}, f32[16,1024]{1,0:T(8,128)S(1)}, u32[]{:S(2)}, u32[]{:S(2)}) collective-permute-start(f32[16,1024]{1,0:T(8,128)S(1)} %solve.1), channel_id=1, source_target_pairs={{0,16},{4,20},{8,24},{12,28},{16,0},{20,4},{24,8},{28,12},{32,48},... | collective-permute-start | bytes 196616 | tf_op jit(solution)/shard_map/ppermute | solution.py:33
  24.1 5.0 %collective-permute-start.4 = (f32[16,1024]{1,0:T(8,128)S(1)}, f32[16,1024]{1,0:T(8,128)S(1)}, u32[]{:S(2)}, u32[]{:S(2)}) collective-permute-start(f32[16,1024]{1,0:T(8,128)S(1)} %solve.1), channel_id=1, source_target_pairs={{0,24},{4,28},{8,16},{12,20},{16,8},{20,12},{24,0},{28,4},{32,56},... | collective-permute-start | bytes 196616 | tf_op jit(solution)/shard_map/ppermute | solution.py:33
  29.2 7.0 %collective-permute-start.7 = (f32[16,1024]{1,0:T(8,128)S(1)}, f32[16,1024]{1,0:T(8,128)S(1)}, u32[]{:S(2)}, u32[]{:S(2)}) collective-permute-start(f32[16,1024]{1,0:T(8,128)S(1)} %select_select_fusion), channel_id=1, source_target_pairs={{0,48},{4,52},{8,56},{12,60},{16,32},{20,36},{24,40},{28,44},{32,1... | collective-permute-start | bytes 196616 | tf_op jit(solution)/shard_map/ppermute | solution.py:33
  36.2 7.1 %collective-permute-start.12 = (f32[16,1024]{1,0:T(8,128)S(1)}, f32[16,1024]{1,0:T(8,128)S(1)}, u32[]{:S(2)}, u32[]{:S(2)}) collective-permute-start(f32[16,1024]{1,0:T(8,128)S(1)} %broadcast_select_fusion.refs_5_), channel_id=1, source_target_pairs={{0,192},{4,196},{8,200},{12,204},{16,208},{20,212},{24,216},{28,22... | collective-permute-start | bytes 196616 | tf_op jit(solution)/shard_map/ppermute | solution.py:29
  36.3 7.0 %collective-permute-start.11 = (f32[16,1024]{1,0:T(8,128)S(1)}, f32[16,1024]{1,0:T(8,128)S(1)}, u32[]{:S(2)}, u32[]{:S(2)}) collective-permute-start(f32[16,1024]{1,0:T(8,128)S(1)} %broadcast_select_fusion.refs_5_), channel_id=1, source_target_pairs={{0,128},{4,132},{8,136},{12,140},{16,144},{20,148},{24,152},{28,15... | collective-permute-start | bytes 196616 | tf_op jit(solution)/shard_map/ppermute | solution.py:29
  36.4 7.0 %collective-permute-start.10 = (f32[16,1024]{1,0:T(8,128)S(1)}, f32[16,1024]{1,0:T(8,128)S(1)}, u32[]{:S(2)}, u32[]{:S(2)}) collective-permute-start(f32[16,1024]{1,0:T(8,128)S(1)} %broadcast_select_fusion.refs_5_), channel_id=1, source_target_pairs={{0,64},{4,68},{8,72},{12,76},{16,80},{20,84},{24,88},{28,92},{32,9... | collective-permute-start | bytes 196616 | tf_op jit(solution)/shard_map/ppermute | solution.py:29
  39.9 6.8 %copy-start = (f32[1024,4,256]{2,1,0:T(4,128)S(1)}, f32[1024,4,256]{2,1,0:T(4,128)}, u32[]{:S(2)}) copy-start(f32[1024,4,256]{2,1,0:T(4,128)} %param.7) | copy-start | bytes 12582916
  43.3 6.5 %collective-permute-start.15 = (f32[64,1024]{1,0:T(8,128)S(1)}, f32[64,1024]{1,0:T(8,128)S(1)}, u32[]{:S(2)}, u32[]{:S(2)}) collective-permute-start(f32[64,1024]{1,0:T(8,128)S(1)} %pad_maximum_fusion.token.refs_0_), channel_id=1, source_target_pairs={{0,3},{1,2},{2,1},{3,0},{4,7},{5,6},{6,5},{7,4},{8,11},{9,10},{10,... | collective-permute-start | bytes 786440 | tf_op jit(solution)/shard_map/ppermute | solution.py:37
  45.8 5.5 %collective-permute-start.14 = (f32[64,1024]{1,0:T(8,128)S(1)}, f32[64,1024]{1,0:T(8,128)S(1)}, u32[]{:S(2)}, u32[]{:S(2)}) collective-permute-start(f32[64,1024]{1,0:T(8,128)S(1)} %pad_maximum_fusion.token.refs_0_), channel_id=1, source_target_pairs={{0,1},{1,0},{2,3},{3,2},{4,5},{5,4},{6,7},{7,6},{8,9},{9,8},{10,11... | collective-permute-start | bytes 786440 | tf_op jit(solution)/shard_map/ppermute | solution.py:37
  45.8 20.9 %collective-permute-start.8 = (f32[1024,128]{1,0:T(8,128)S(1)}, f32[1024,128]{1,0:T(8,128)S(1)}, u32[]{:S(2)}, u32[]{:S(2)}) collective-permute-start(f32[1024,128]{1,0:T(8,128)S(1)} %get-tuple-element.42), channel_id=1, source_target_pairs={{0,64},{4,68},{8,72},{12,76},{16,80},{20,84},{24,88},{28,92},{32,9... | collective-permute-start | bytes 1572872 | tf_op jit(solution)/shard_map/ppermute | solution.py:29
  45.9 20.8 %collective-permute-start.9 = (f32[1024,128]{1,0:T(8,128)S(1)}, f32[1024,128]{1,0:T(8,128)S(1)}, u32[]{:S(2)}, u32[]{:S(2)}) collective-permute-start(f32[1024,128]{1,0:T(8,128)S(1)} %get-tuple-element.43), channel_id=1, source_target_pairs={{0,192},{4,196},{8,200},{12,204},{16,208},{20,212},{24,216},{28,22... | collective-permute-start | bytes 1572872 | tf_op jit(solution)/shard_map/ppermute | solution.py:29
  51.3 5.3 %collective-permute-start.17 = (f32[64,1024]{1,0:T(8,128)S(1)}, f32[64,1024]{1,0:T(8,128)S(1)}, u32[]{:S(2)}, u32[]{:S(2)}) collective-permute-start(f32[64,1024]{1,0:T(8,128)S(1)} %collective-permute-done.14.refs_0_), channel_id=1, source_target_pairs={{0,4},{4,0},{8,12},{12,8},{16,20},{20,16},{24,28},{28,24},{32,36},... | collective-permute-start | bytes 786440 | tf_op jit(solution)/shard_map/ppermute | solution.py:48
  55.5 1.5 %collective-permute-start.18 = (f32[64,1024]{1,0:T(8,128)S(1)}, f32[64,1024]{1,0:T(8,128)S(1)}, u32[]{:S(2)}, u32[]{:S(2)}) collective-permute-start(f32[64,1024]{1,0:T(8,128)S(1)} %collective-permute-done.15.refs_1_), channel_id=1, source_target_pairs={{0,4},{4,0},{8,12},{12,8},{16,20},{20,16},{24,28},{28,24},{32,36},... | collective-permute-start | bytes 786440 | tf_op jit(solution)/shard_map/ppermute | solution.py:48
  55.5 8.9 %collective-permute-start.16 = (f32[64,1024]{1,0:T(8,128)S(1)}, f32[64,1024]{1,0:T(8,128)S(1)}, u32[]{:S(2)}, u32[]{:S(2)}) collective-permute-start(f32[64,1024]{1,0:T(8,128)S(1)} %pad_maximum_fusion.token.refs_0_), channel_id=1, source_target_pairs={{0,2},{1,3},{2,0},{3,1},{4,6},{5,7},{6,4},{7,5},{8,10},{9,11},{10,... | collective-permute-start | bytes 786440 | tf_op jit(solution)/shard_map/ppermute | solution.py:37
  59.5 14.6 %collective-permute-start.20 = (f32[128,1024]{1,0:T(8,128)S(1)}, f32[128,1024]{1,0:T(8,128)S(1)}, u32[]{:S(2)}, u32[]{:S(2)}) collective-permute-start(f32[128,1024]{1,0:T(8,128)S(1)} %get-tuple-element.58), channel_id=1, source_target_pairs={{0,1},{1,0},{2,3},{3,2},{4,5},{5,4},{6,7},{7,6},{8,9},{9,8},{10,11... | collective-permute-start | bytes 1572872 | tf_op jit(solution)/shard_map/ppermute | solution.py:37
  59.6 17.0 %collective-permute-start.21 = (f32[128,1024]{1,0:T(8,128)S(1)}, f32[128,1024]{1,0:T(8,128)S(1)}, u32[]{:S(2)}, u32[]{:S(2)}) collective-permute-start(f32[128,1024]{1,0:T(8,128)S(1)} %get-tuple-element.59), channel_id=1, source_target_pairs={{0,3},{1,2},{2,1},{3,0},{4,7},{5,6},{6,5},{7,4},{8,11},{9,10},{10,... | collective-permute-start | bytes 1572872 | tf_op jit(solution)/shard_map/ppermute | solution.py:37
  64.3 3.7 %collective-permute-start.19 = (f32[64,1024]{1,0:T(8,128)S(1)}, f32[64,1024]{1,0:T(8,128)S(1)}, u32[]{:S(2)}, u32[]{:S(2)}) collective-permute-start(f32[64,1024]{1,0:T(8,128)S(1)} %collective-permute-done.16.refs_0_), channel_id=1, source_target_pairs={{0,4},{4,0},{8,12},{12,8},{16,20},{20,16},{24,28},{28,24},{32,36},... | collective-permute-start | bytes 786440 | tf_op jit(solution)/shard_map/ppermute | solution.py:48
  66.7 4.1 %collective-permute-start.13 = (f32[64,1024]{1,0:T(8,128)S(1)}, f32[64,1024]{1,0:T(8,128)S(1)}, u32[]{:S(2)}, u32[]{:S(2)}) collective-permute-start(f32[64,1024]{1,0:T(8,128)S(1)} %pad_maximum_fusion.token.refs_0_), channel_id=1, source_target_pairs={{0,4},{4,0},{8,12},{12,8},{16,20},{20,16},{24,28},{28,24},{32,36},... | collective-permute-start | bytes 786440 | tf_op jit(solution)/shard_map/ppermute | solution.py:48
  66.7 14.7 %collective-permute-start.22 = (f32[1024,128]{1,0:T(8,128)S(1)}, f32[1024,128]{1,0:T(8,128)S(1)}, u32[]{:S(2)}, u32[]{:S(2)}) collective-permute-start(f32[1024,128]{1,0:T(8,128)S(1)} %get-tuple-element.61), channel_id=1, source_target_pairs={{0,128},{4,132},{8,136},{12,140},{16,144},{20,148},{24,152},{28,15... | collective-permute-start | bytes 1572872 | tf_op jit(solution)/shard_map/ppermute | solution.py:29
  69.7 17.1 %collective-permute-start.23 = (f32[128,1024]{1,0:T(8,128)S(1)}, f32[128,1024]{1,0:T(8,128)S(1)}, u32[]{:S(2)}, u32[]{:S(2)}) collective-permute-start(f32[128,1024]{1,0:T(8,128)S(1)} %get-tuple-element.62), channel_id=1, source_target_pairs={{0,2},{1,3},{2,0},{3,1},{4,6},{5,7},{6,4},{7,5},{8,10},{9,11},{10,... | collective-permute-start | bytes 1572872 | tf_op jit(solution)/shard_map/ppermute | solution.py:37

commit v7 on v6

--- a/solution.py
+++ b/solution.py
@@ -198,9 +198,13 @@
     out, got, near, done = refs[5:]
     copies = []
     for i in range(4):
-        part = (pl.ds(0, 256 * (i + 1)), pl.ds(256 * i, 256))
-        copies.append(pltpu.make_async_copy(inverse.at[part], near.at[part], done.at[i]))
-        copies[i].start()
+        copies.append([])
+        for j in range(i + 1):
+            part = (pl.ds(256 * j, 256), pl.ds(256 * i, 256))
+            copies[i].append(
+                pltpu.make_async_copy(inverse.at[part], near.at[part], done.at[i, j])
+            )
+            copies[i][j].start()
     x = info[1]
     for s in range(NX):
         got[x ^ s] = pieces[s][...]
@@ -215,7 +219,8 @@
     top, low = split(got[x0, 17:18, :] * (0.5 * (level[0] + sign_low * level[1])))
     for i in range(4):
         depth, at = 256 * (i + 1), slice(256 * i, 256 * i + 256)
-        copies[i].wait()
+        for copy in copies[i]:
+            copy.wait()
         a, b = split(near[:depth, at])
         out[:, at] = (
             product(top[:, :depth], b) + product(low[:, :depth], a) + product(top[:, :depth], a)
@@ -236,7 +241,7 @@
         [
             pltpu.VMEM((NX, 24, NB), F32),
             pltpu.VMEM((NB, NB), F32),
-            pltpu.SemaphoreType.DMA((4,)),
+            pltpu.SemaphoreType.DMA((4, 4)),
         ],
         70 * 10**9,
     )

time: 89.1 us -> 89 us (level)
  no operation moved by 1% of the time
where the time goes in v7:
time: 89 us; the launch traced here: 88.7 us
  starting transfers between devices  37.7 us (42%)
  waiting for transfers between devices  29.5 us (33%)
  Pallas kernels  20.3 us (23%)
  between operations  1.07 us (1%)
    pallas_call x11, Pallas kernels, call(): pl.pallas_call(body, grid_spec=pltpu.PrefetchScalarGridSpec(num_scalar_pr...  20.3 us
    ppermute x6, waiting for transfers between devices, flip_y(): return lax.ppermute(v, 'rhs', [(i, i ^ m) for i in range(NY)]) if m else v  15.3 us
    ppermute x5, starting transfers between devices, other_core(): return lax.ppermute(v, 'rows', row_perm(lambda x, z, c: (x, z, 1 - c)))  9.82 us
    ppermute x4, starting transfers between devices, flip_z(): return lax.ppermute(v, 'rows', row_perm(lambda x, z, c: (x, z ^ m, c)))  9.74 us
    ppermute x9, starting transfers between devices, flip_x(): lax.ppermute(v, 'rows', row_perm(lambda x, z, c: (x ^ m, z, c)))  8.94 us
    ppermute x4, waiting for transfers between devices, flip_z(): return lax.ppermute(v, 'rows', row_perm(lambda x, z, c: (x, z ^ m, c)))  6.96 us
    ppermute x6, starting transfers between devices, flip_y(): return lax.ppermute(v, 'rhs', [(i, i ^ m) for i in range(NY)]) if m else v  5.55 us
    ppermute x9, waiting for transfers between devices, flip_x(): lax.ppermute(v, 'rows', row_perm(lambda x, z, c: (x ^ m, z, c)))  4.65 us
  transfers between devices with their start and end apart: 25, of which 15 were waited for; matrix products, arithmetic and copies ran while one was open for 0% of the time, Pallas kernels for 19%

profile of v7, /device:TPU:1, one launch (start us, length us, event | category | flops | bytes accessed | tf_op | source)
XLA Modules:
  0.0 88.7 jit_solution(11425072246620678123)
XLA Ops:
  0.7 1.4 %prep.1 = (f32[72,1024]{1,0:T(8,128)S(1)}, f32[72,1024]{1,0:T(8,128)S(1)}) custom-call(s32[1]{0:T(128)} %copy.9.start, f32[4,1024,128]{2,1,0:T(8,128)} %slabs.1, f32[2,4,1024]{2,1,0:T(4,128)} %diag.1), custom_call_target="tpu_custom_call" | custom-call | tf_op jit(solution)/shard_map/prep/pallas_call | solution.py:68
  2.0 3.3 %collective-permute-start = (f32[72,1024]{1,0:T(8,128)S(1)}, f32[72,1024]{1,0:T(8,128)S(1)}, u32[]{:S(2)}, u32[]{:S(2)}) collective-permute-start(f32[72,1024]{1,0:T(8,128)S(1)} %get-tuple-element.35), channel_id=1, source_target_pairs={{0,4},{4,0},{8,12},{12,8},{16,20},{20,16},{24,28},{28,24},{32,36},... | collective-permute-start | bytes 884744 | tf_op jit(solution)/shard_map/ppermute | solution.py:48
  5.4 0.1 stack.19.info
  5.5 1.1 %collective-permute-done.came = f32[72,1024]{1,0:T(8,128)S(1)} collective-permute-done((f32[72,1024]{1,0:T(8,128)S(1)}, f32[72,1024]{1,0:T(8,128)S(1)}, u32[]{:S(2)}, u32[]{:S(2)}) %collective-permute-start) | collective-permute-done | bytes 294944 | tf_op jit(solution)/shard_map/ppermute | solution.py:48
  6.6 0.0 copy-done.1
  6.6 0.6 pack.1
  7.2 0.0 copy-start.2
  7.2 0.1 collective-permute-start.1
  7.3 1.9 %collective-permute-start.2 = (f32[24,1024]{1,0:T(8,128)S(1)}, f32[24,1024]{1,0:T(8,128)S(1)}, u32[]{:S(2)}, u32[]{:S(2)}) collective-permute-start(f32[24,1024]{1,0:T(8,128)S(1)} %get-tuple-element.39), channel_id=1, source_target_pairs={{0,128},{4,132},{8,136},{12,140},{16,144},{20,148},{24,152},{28,15... | collective-permute-start | bytes 294920 | tf_op jit(solution)/shard_map/ppermute | solution.py:29
  9.2 1.9 %collective-permute-start.3 = (f32[24,1024]{1,0:T(8,128)S(1)}, f32[24,1024]{1,0:T(8,128)S(1)}, u32[]{:S(2)}, u32[]{:S(2)}) collective-permute-start(f32[24,1024]{1,0:T(8,128)S(1)} %get-tuple-element.40), channel_id=1, source_target_pairs={{0,192},{4,196},{8,200},{12,204},{16,208},{20,212},{24,216},{28,22... | collective-permute-start | bytes 294920 | tf_op jit(solution)/shard_map/ppermute | solution.py:29
  11.2 3.6 %all-to-all-start = ((f32[4,1024,128]{2,1,0:T(8,128)}), f32[4,1024,128]{2,1,0:T(8,128)S(1)}, u32[]{:S(2)}, u32[]{:S(2)}) async-start(f32[4,1024,128]{2,1,0:T(8,128)} %slabs.1), calls=%async_computation | async-start | bytes 4194304 | tf_op jit(solution)/shard_map/all_to_all | solution.py:44
  14.8 0.0 collective-permute-done.1.refs_1_.refs_2_
  14.8 0.0 collective-permute-done.2.refs_2_.refs_3_
  14.8 1.6 %collective-permute-done.3.refs_3_.refs_4_ = f32[24,1024]{1,0:T(8,128)S(1)} collective-permute-done((f32[24,1024]{1,0:T(8,128)S(1)}, f32[24,1024]{1,0:T(8,128)S(1)}, u32[]{:S(2)}, u32[]{:S(2)}) %collective-permute-start.3) | collective-permute-done | bytes 98336 | tf_op jit(solution)/shard_map/ppermute | solution.py:29
  16.5 3.0 %solve.1 = f32[16,1024]{1,0:T(8,128)S(1)} custom-call(s32[5]{0:T(128)S(1)} %stack.19.info, f32[24,1024]{1,0:T(8,128)S(1)} %get-tuple-element.36.refs_0_.refs_1_, f32[24,1024]{1,0:T(8,128)S(1)} %collective-permute-done.1.refs_1_.refs_2_, f32[24,1024]{1,0:T(8,128)S(1)} %collective-permute-done.2.refs_2_.refs_3_, ...), custom_call_target="tpu_custom_call" | custom-call | flops 70000001024 | bytes 1048576 | tf_op jit(solution)/shard_map/solve/pallas_call | solution.py:68
  19.5 1.7 %collective-permute-start.6 = (f32[16,1024]{1,0:T(8,128)S(1)}, f32[16,1024]{1,0:T(8,128)S(1)}, u32[]{:S(2)}, u32[]{:S(2)}) collective-permute-start(f32[16,1024]{1,0:T(8,128)S(1)} %solve.1), channel_id=1, source_target_pairs={{0,8},{4,12},{8,0},{12,4},{16,24},{20,28},{24,16},{28,20},{32,40},... | collective-permute-start | bytes 196616 | tf_op jit(solution)/shard_map/ppermute | solution.py:33
  21.3 3.0 %collective-permute-start.5 = (f32[16,1024]{1,0:T(8,128)S(1)}, f32[16,1024]{1,0:T(8,128)S(1)}, u32[]{:S(2)}, u32[]{:S(2)}) collective-permute-start(f32[16,1024]{1,0:T(8,128)S(1)} %solve.1), channel_id=1, source_target_pairs={{0,16},{4,20},{8,24},{12,28},{16,0},{20,4},{24,8},{28,12},{32,48},... | collective-permute-start | bytes 196616 | tf_op jit(solution)/shard_map/ppermute | solution.py:33
  24.2 0.0 collective-permute-start.4
  24.2 0.0 collective-permute-done.6
  24.3 2.5 %collective-permute-done.5 = f32[16,1024]{1,0:T(8,128)S(1)} collective-permute-done((f32[16,1024]{1,0:T(8,128)S(1)}, f32[16,1024]{1,0:T(8,128)S(1)}, u32[]{:S(2)}, u32[]{:S(2)}) %collective-permute-start.5) | collective-permute-done | bytes 65568 | tf_op jit(solution)/shard_map/ppermute | solution.py:33
  26.7 2.5 %collective-permute-done.4 = f32[16,1024]{1,0:T(8,128)S(1)} collective-permute-done((f32[16,1024]{1,0:T(8,128)S(1)}, f32[16,1024]{1,0:T(8,128)S(1)}, u32[]{:S(2)}, u32[]{:S(2)}) %collective-permute-start.4) | collective-permute-done | bytes 65568 | tf_op jit(solution)/shard_map/ppermute | solution.py:33
  29.3 5.0 %collective-permute-start.7 = (f32[16,1024]{1,0:T(8,128)S(1)}, f32[16,1024]{1,0:T(8,128)S(1)}, u32[]{:S(2)}, u32[]{:S(2)}) collective-permute-start(f32[16,1024]{1,0:T(8,128)S(1)} %select_select_fusion), channel_id=1, source_target_pairs={{0,48},{4,52},{8,56},{12,60},{16,32},{20,36},{24,40},{28,44},{32,1... | collective-permute-start | bytes 196616 | tf_op jit(solution)/shard_map/ppermute | solution.py:33
  34.3 2.0 %collective-permute-done.7 = f32[16,1024]{1,0:T(8,128)S(1)} collective-permute-done((f32[16,1024]{1,0:T(8,128)S(1)}, f32[16,1024]{1,0:T(8,128)S(1)}, u32[]{:S(2)}, u32[]{:S(2)}) %collective-permute-start.7) | collective-permute-done | bytes 65568 | tf_op jit(solution)/shard_map/ppermute | solution.py:33
  36.3 0.1 collective-permute-start.12
  36.4 0.1 collective-permute-start.11
  36.5 3.1 %collective-permute-start.10 = (f32[16,1024]{1,0:T(8,128)S(1)}, f32[16,1024]{1,0:T(8,128)S(1)}, u32[]{:S(2)}, u32[]{:S(2)}) collective-permute-start(f32[16,1024]{1,0:T(8,128)S(1)} %broadcast_select_fusion.refs_5_), channel_id=1, source_target_pairs={{0,64},{4,68},{8,72},{12,76},{16,80},{20,84},{24,88},{28,92},{32,9... | collective-permute-start | bytes 196616 | tf_op jit(solution)/shard_map/ppermute | solution.py:29
  39.6 0.3 all-to-all-done.refs_0_
  39.9 3.4 %mid.1 = (f32[1024,128]{1,0:T(8,128)S(1)}, f32[1024,128]{1,0:T(8,128)S(1)}, f32[1024,128]{1,0:T(8,128)S(1)}, f32[1024,128]{1,0:T(8,128)S(1)}, f32[8,128]{1,0:T(8,128)S(1)}) custom-call(s32[5]{0:T(128)S(1)} %stack.19.info, f32[4,1024,128]{2,1,0:T(8,128)S(1)} %all-to-all-done.refs_0_, f32[24,1024]{1,0:T(8,128)} %copy-done.2, f32[24,1024]{1,0:T(8,128)} %copy-done.3, ...), custom_call_target="tpu_custom_call" | custom-call | flops 10000000000 | bytes 1048576 | tf_op jit(solution)/shard_map/mid/pallas_call | solution.py:68
  43.3 0.0 collective-permute-done.12
  43.3 0.0 collective-permute-done.11
  43.3 0.0 collective-permute-done.10
  43.3 2.6 %collective-permute-start.15 = (f32[64,1024]{1,0:T(8,128)S(1)}, f32[64,1024]{1,0:T(8,128)S(1)}, u32[]{:S(2)}, u32[]{:S(2)}) collective-permute-start(f32[64,1024]{1,0:T(8,128)S(1)} %pad_maximum_fusion.token.refs_0_), channel_id=1, source_target_pairs={{0,3},{1,2},{2,1},{3,0},{4,7},{5,6},{6,5},{7,4},{8,11},{9,10},{10,... | collective-permute-start | bytes 786440 | tf_op jit(solution)/shard_map/ppermute | solution.py:37
  45.9 0.0 collective-permute-start.14
  45.9 0.1 collective-permute-start.8
  46.0 0.8 collective-permute-start.9
  46.8 2.2 %split_band.1 = (bf16[1024,1024]{1,0:T(8,128)(2,1)S(1)}, bf16[1024,1024]{1,0:T(8,128)(2,1)S(1)}) custom-call(s32[5]{0:T(128)S(1)} %stack.19.info, f32[8192,128]{1,0:T(8,128)S(1)} %bitcast.13, f32[64,1024]{1,0:T(8,128)S(1)} %pad_maximum_fusion.token.refs_0_), custom_call_target="tpu_custom_call" | custom-call | flops 1000000000 | bytes 1048576 | tf_op jit(solution)/shard_map/split_band/pallas_call | solution.py:68
  49.0 0.9 collective-permute-done.15.refs_1_
  49.9 1.5 %collective-permute-done.14.refs_0_ = f32[64,1024]{1,0:T(8,128)S(1)} collective-permute-done((f32[64,1024]{1,0:T(8,128)S(1)}, f32[64,1024]{1,0:T(8,128)S(1)}, u32[]{:S(2)}, u32[]{:S(2)}) %collective-permute-start.14) | collective-permute-done | bytes 262176 | tf_op jit(solution)/shard_map/ppermute | solution.py:37
  51.4 4.2 %collective-permute-start.17 = (f32[64,1024]{1,0:T(8,128)S(1)}, f32[64,1024]{1,0:T(8,128)S(1)}, u32[]{:S(2)}, u32[]{:S(2)}) collective-permute-start(f32[64,1024]{1,0:T(8,128)S(1)} %collective-permute-done.14.refs_0_), channel_id=1, source_target_pairs={{0,4},{4,0},{8,12},{12,8},{16,20},{20,16},{24,28},{28,24},{32,36},... | collective-permute-start | bytes 786440 | tf_op jit(solution)/shard_map/ppermute | solution.py:48
  55.6 0.0 collective-permute-start.18
  55.6 0.3 collective-permute-start.16
  55.9 0.8 collective-permute-done.17.refs_2_
  56.7 0.4 collective-permute-done.18.refs_3_
  57.1 2.5 %update.3 = (f32[128,1024]{1,0:T(8,128)S(1)}, f32[128,1024]{1,0:T(8,128)S(1)}, f32[128,1024]{1,0:T(8,128)S(1)}) custom-call(s32[5]{0:T(128)S(1)} %stack.19.info, f32[64,1024]{1,0:T(8,128)S(1)} %collective-permute-done.14.refs_0_, f32[64,1024]{1,0:T(8,128)S(1)} %collective-permute-done.15.refs_1_, f32[64,1024]{1,0:T(8,128)S(1)} %collective-permute-done.17.refs_2_, ...), custom_call_target="tpu_custom_call" | custom-call | flops 1 | bytes 1048576 | tf_op jit(solution)/shard_map/update/pallas_call | solution.py:68
  59.6 0.1 collective-permute-start.20
  59.7 1.7 %collective-permute-start.21 = (f32[128,1024]{1,0:T(8,128)S(1)}, f32[128,1024]{1,0:T(8,128)S(1)}, u32[]{:S(2)}, u32[]{:S(2)}) collective-permute-start(f32[128,1024]{1,0:T(8,128)S(1)} %get-tuple-element.59), channel_id=1, source_target_pairs={{0,3},{1,2},{2,1},{3,0},{4,7},{5,6},{6,5},{7,4},{8,11},{9,10},{10,... | collective-permute-start | bytes 1572872 | tf_op jit(solution)/shard_map/ppermute | solution.py:37
  61.5 3.0 %collective-permute-done.16.refs_0_ = f32[64,1024]{1,0:T(8,128)S(1)} collective-permute-done((f32[64,1024]{1,0:T(8,128)S(1)}, f32[64,1024]{1,0:T(8,128)S(1)}, u32[]{:S(2)}, u32[]{:S(2)}) %collective-permute-start.16) | collective-permute-done | bytes 262176 | tf_op jit(solution)/shard_map/ppermute | solution.py:37
  64.5 2.3 %collective-permute-start.19 = (f32[64,1024]{1,0:T(8,128)S(1)}, f32[64,1024]{1,0:T(8,128)S(1)}, u32[]{:S(2)}, u32[]{:S(2)}) collective-permute-start(f32[64,1024]{1,0:T(8,128)S(1)} %collective-permute-done.16.refs_0_), channel_id=1, source_target_pairs={{0,4},{4,0},{8,12},{12,8},{16,20},{20,16},{24,28},{28,24},{32,36},... | collective-permute-start | bytes 786440 | tf_op jit(solution)/shard_map/ppermute | solution.py:48
  66.8 0.0 collective-permute-done.8.refs_0_.refs_1_
  66.8 0.0 collective-permute-start.13
  66.8 0.0 collective-permute-done.9.refs_1_.refs_2_.refs_3_
  66.8 0.8 collective-permute-start.22
  67.6 0.5 mark.1.refs_4_
  68.1 0.0 collective-permute-done.19.refs_1_
  68.1 1.7 %update.4 = (f32[128,1024]{1,0:T(8,128)S(1)}, f32[128,1024]{1,0:T(8,128)S(1)}) custom-call(s32[5]{0:T(128)S(1)} %stack.19.info, f32[64,1024]{1,0:T(8,128)S(1)} %collective-permute-done.16.refs_0_, f32[64,1024]{1,0:T(8,128)S(1)} %collective-permute-done.19.refs_1_, bf16[1024,1024]{1,0:T(8,128)(2,1)S(1)} %get-tuple-element.48.refs_4_.refs_2_, ...), custom_call_target="tpu_custom_call" | custom-call | flops 1 | bytes 1048576 | tf_op jit(solution)/shard_map/update/pallas_call | solution.py:68
  69.8 0.8 collective-permute-start.23
  70.7 0.0 collective-permute-done.13.refs_1_
  70.7 1.7 %update.5 = (f32[128,1024]{1,0:T(8,128)S(1)}, f32[128,1024]{1,0:T(8,128)S(1)}) custom-call(s32[5]{0:T(128)S(1)} %stack.19.info, f32[64,1024]{1,0:T(8,128)S(1)} %pad_maximum_fusion.token.refs_0_, f32[64,1024]{1,0:T(8,128)S(1)} %collective-permute-done.13.refs_1_, bf16[1024,1024]{1,0:T(8,128)(2,1)S(1)} %get-tuple-element.48.refs_4_.refs_2_, ...), custom_call_target="tpu_custom_call" | custom-call | flops 1 | bytes 1048576 | tf_op jit(solution)/shard_map/update/pallas_call | solution.py:68
  72.3 1.9 %collective-permute-done.20.refs_5_.refs_6_ = f32[128,1024]{1,0:T(8,128)S(1)} collective-permute-done((f32[128,1024]{1,0:T(8,128)S(1)}, f32[128,1024]{1,0:T(8,128)S(1)}, u32[]{:S(2)}, u32[]{:S(2)}) %collective-permute-start.20) | collective-permute-done | bytes 524320 | tf_op jit(solution)/shard_map/ppermute | solution.py:37
  74.2 2.6 %collective-permute-done.21.refs_6_.refs_8_ = f32[128,1024]{1,0:T(8,128)S(1)} collective-permute-done((f32[128,1024]{1,0:T(8,128)S(1)}, f32[128,1024]{1,0:T(8,128)S(1)}, u32[]{:S(2)}, u32[]{:S(2)}) %collective-permute-start.21) | collective-permute-done | bytes 524320 | tf_op jit(solution)/shard_map/ppermute | solution.py:37
  76.8 1.7 %subtract.1.before = f32[4,1024,128]{2,1,0:T(8,128)} custom-call(s32[5]{0:T(128)S(1)} %stack.19.info, f32[1024,128]{1,0:T(8,128)S(1)} %get-tuple-element.41.refs_0_, f32[1024,128]{1,0:T(8,128)S(1)} %collective-permute-done.8.refs_0_.refs_1_, f32[1024,128]{1,0:T(8,128)S(1)} %collective-permute-done.9.refs_1_.refs_2_.refs_3_, ...), custom_call_target="tpu_custom_call" | custom-call | flops 3000000000 | bytes 1048576 | tf_op jit(solution)/shard_map/subtract/pallas_call | solution.py:68
  78.5 3.0 %collective-permute-done.22.refs_2_ = f32[1024,128]{1,0:T(8,128)S(1)} collective-permute-done((f32[1024,128]{1,0:T(8,128)S(1)}, f32[1024,128]{1,0:T(8,128)S(1)}, u32[]{:S(2)}, u32[]{:S(2)}) %collective-permute-start.22) | collective-permute-done | bytes 524320 | tf_op jit(solution)/shard_map/ppermute | solution.py:29
  81.5 5.5 %collective-permute-done.23.refs_7_ = f32[128,1024]{1,0:T(8,128)S(1)} collective-permute-done((f32[128,1024]{1,0:T(8,128)S(1)}, f32[128,1024]{1,0:T(8,128)S(1)}, u32[]{:S(2)}, u32[]{:S(2)}) %collective-permute-start.23) | collective-permute-done | bytes 524320 | tf_op jit(solution)/shard_map/ppermute | solution.py:37
  86.9 1.6 %last.1 = f32[4,1024,128]{2,1,0:T(8,128)} custom-call(s32[5]{0:T(128)S(1)} %stack.19.info, f32[4,1024,128]{2,1,0:T(8,128)} %subtract.1.before, f32[1024,128]{1,0:T(8,128)S(1)} %get-tuple-element.41.refs_0_, f32[1024,128]{1,0:T(8,128)S(1)} %collective-permute-done.8.refs_0_.refs_1_, ...), custom_call_target="tpu_custom_call", output_to_operand_aliasing={{}: (1, {})} | custom-call | tf_op jit(solution)/shard_map/last/pallas_call | solution.py:68
  (13 shorter events, 0.1 us)
Async XLA Ops:
  0.0 6.6 %copy-start.1 = (f32[2,4,1024]{2,1,0:T(4,128)S(1)}, f32[2,4,1024]{2,1,0:T(4,128)}, u32[]{:S(2)}) copy-start(f32[2,4,1024]{2,1,0:T(4,128)} %diag.1) | copy-start | bytes 98308
  2.0 4.5 %collective-permute-start = (f32[72,1024]{1,0:T(8,128)S(1)}, f32[72,1024]{1,0:T(8,128)S(1)}, u32[]{:S(2)}, u32[]{:S(2)}) collective-permute-start(f32[72,1024]{1,0:T(8,128)S(1)} %get-tuple-element.35), channel_id=1, source_target_pairs={{0,4},{4,0},{8,12},{12,8},{16,20},{20,16},{24,28},{28,24},{32,36},... | collective-permute-start | bytes 884744 | tf_op jit(solution)/shard_map/ppermute | solution.py:48
  7.2 9.3 %copy-start.2 = (f32[24,1024]{1,0:T(8,128)}, f32[24,1024]{1,0:T(8,128)S(1)}, u32[]{:S(2)}) copy-start(f32[24,1024]{1,0:T(8,128)S(1)} %get-tuple-element.36.refs_0_.refs_1_) | copy-start | bytes 294916
  7.2 7.6 %collective-permute-start.1 = (f32[24,1024]{1,0:T(8,128)S(1)}, f32[24,1024]{1,0:T(8,128)S(1)}, u32[]{:S(2)}, u32[]{:S(2)}) collective-permute-start(f32[24,1024]{1,0:T(8,128)S(1)} %get-tuple-element.38), channel_id=1, source_target_pairs={{0,64},{4,68},{8,72},{12,76},{16,80},{20,84},{24,88},{28,92},{32,9... | collective-permute-start | bytes 294920 | tf_op jit(solution)/shard_map/ppermute | solution.py:29
  7.3 7.5 %collective-permute-start.2 = (f32[24,1024]{1,0:T(8,128)S(1)}, f32[24,1024]{1,0:T(8,128)S(1)}, u32[]{:S(2)}, u32[]{:S(2)}) collective-permute-start(f32[24,1024]{1,0:T(8,128)S(1)} %get-tuple-element.39), channel_id=1, source_target_pairs={{0,128},{4,132},{8,136},{12,140},{16,144},{20,148},{24,152},{28,15... | collective-permute-start | bytes 294920 | tf_op jit(solution)/shard_map/ppermute | solution.py:29
  9.2 7.2 %collective-permute-start.3 = (f32[24,1024]{1,0:T(8,128)S(1)}, f32[24,1024]{1,0:T(8,128)S(1)}, u32[]{:S(2)}, u32[]{:S(2)}) collective-permute-start(f32[24,1024]{1,0:T(8,128)S(1)} %get-tuple-element.40), channel_id=1, source_target_pairs={{0,192},{4,196},{8,200},{12,204},{16,208},{20,212},{24,216},{28,22... | collective-permute-start | bytes 294920 | tf_op jit(solution)/shard_map/ppermute | solution.py:29
  11.2 28.7 %all-to-all-start = ((f32[4,1024,128]{2,1,0:T(8,128)}), f32[4,1024,128]{2,1,0:T(8,128)S(1)}, u32[]{:S(2)}, u32[]{:S(2)}) async-start(f32[4,1024,128]{2,1,0:T(8,128)} %slabs.1), calls=%async_computation | async-start | bytes 4194304 | tf_op jit(solution)/shard_map/all_to_all | solution.py:44
  14.8 4.7 %copy-start.3 = (f32[24,1024]{1,0:T(8,128)}, f32[24,1024]{1,0:T(8,128)S(1)}, u32[]{:S(2)}) copy-start(f32[24,1024]{1,0:T(8,128)S(1)} %collective-permute-done.1.refs_1_.refs_2_) | copy-start | bytes 294916
  14.8 4.7 %copy-start.4 = (f32[24,1024]{1,0:T(8,128)}, f32[24,1024]{1,0:T(8,128)S(1)}, u32[]{:S(2)}) copy-start(f32[24,1024]{1,0:T(8,128)S(1)} %collective-permute-done.2.refs_2_.refs_3_) | copy-start | bytes 294916
  16.5 3.1 %copy-start.5 = (f32[24,1024]{1,0:T(8,128)}, f32[24,1024]{1,0:T(8,128)S(1)}, u32[]{:S(2)}) copy-start(f32[24,1024]{1,0:T(8,128)S(1)} %collective-permute-done.3.refs_3_.refs_4_) | copy-start | bytes 294916
  19.5 4.7 %collective-permute-start.6 = (f32[16,1024]{1,0:T(8,128)S(1)}, f32[16,1024]{1,0:T(8,128)S(1)}, u32[]{:S(2)}, u32[]{:S(2)}) collective-permute-start(f32[16,1024]{1,0:T(8,128)S(1)} %solve.1), channel_id=1, source_target_pairs={{0,8},{4,12},{8,0},{12,4},{16,24},{20,28},{24,16},{28,20},{32,40},... | collective-permute-start | bytes 196616 | tf_op jit(solution)/shard_map/ppermute | solution.py:33
  21.3 5.5 %collective-permute-start.5 = (f32[16,1024]{1,0:T(8,128)S(1)}, f32[16,1024]{1,0:T(8,128)S(1)}, u32[]{:S(2)}, u32[]{:S(2)}) collective-permute-start(f32[16,1024]{1,0:T(8,128)S(1)} %solve.1), channel_id=1, source_target_pairs={{0,16},{4,20},{8,24},{12,28},{16,0},{20,4},{24,8},{28,12},{32,48},... | collective-permute-start | bytes 196616 | tf_op jit(solution)/shard_map/ppermute | solution.py:33
  24.2 5.0 %collective-permute-start.4 = (f32[16,1024]{1,0:T(8,128)S(1)}, f32[16,1024]{1,0:T(8,128)S(1)}, u32[]{:S(2)}, u32[]{:S(2)}) collective-permute-start(f32[16,1024]{1,0:T(8,128)S(1)} %solve.1), channel_id=1, source_target_pairs={{0,24},{4,28},{8,16},{12,20},{16,8},{20,12},{24,0},{28,4},{32,56},... | collective-permute-start | bytes 196616 | tf_op jit(solution)/shard_map/ppermute | solution.py:33
  29.3 7.0 %collective-permute-start.7 = (f32[16,1024]{1,0:T(8,128)S(1)}, f32[16,1024]{1,0:T(8,128)S(1)}, u32[]{:S(2)}, u32[]{:S(2)}) collective-permute-start(f32[16,1024]{1,0:T(8,128)S(1)} %select_select_fusion), channel_id=1, source_target_pairs={{0,48},{4,52},{8,56},{12,60},{16,32},{20,36},{24,40},{28,44},{32,1... | collective-permute-start | bytes 196616 | tf_op jit(solution)/shard_map/ppermute | solution.py:33
  36.3 7.0 %collective-permute-start.12 = (f32[16,1024]{1,0:T(8,128)S(1)}, f32[16,1024]{1,0:T(8,128)S(1)}, u32[]{:S(2)}, u32[]{:S(2)}) collective-permute-start(f32[16,1024]{1,0:T(8,128)S(1)} %broadcast_select_fusion.refs_5_), channel_id=1, source_target_pairs={{0,192},{4,196},{8,200},{12,204},{16,208},{20,212},{24,216},{28,22... | collective-permute-start | bytes 196616 | tf_op jit(solution)/shard_map/ppermute | solution.py:29
  36.4 6.9 %collective-permute-start.11 = (f32[16,1024]{1,0:T(8,128)S(1)}, f32[16,1024]{1,0:T(8,128)S(1)}, u32[]{:S(2)}, u32[]{:S(2)}) collective-permute-start(f32[16,1024]{1,0:T(8,128)S(1)} %broadcast_select_fusion.refs_5_), channel_id=1, source_target_pairs={{0,128},{4,132},{8,136},{12,140},{16,144},{20,148},{24,152},{28,15... | collective-permute-start | bytes 196616 | tf_op jit(solution)/shard_map/ppermute | solution.py:29
  36.5 6.8 %collective-permute-start.10 = (f32[16,1024]{1,0:T(8,128)S(1)}, f32[16,1024]{1,0:T(8,128)S(1)}, u32[]{:S(2)}, u32[]{:S(2)}) collective-permute-start(f32[16,1024]{1,0:T(8,128)S(1)} %broadcast_select_fusion.refs_5_), channel_id=1, source_target_pairs={{0,64},{4,68},{8,72},{12,76},{16,80},{20,84},{24,88},{28,92},{32,9... | collective-permute-start | bytes 196616 | tf_op jit(solution)/shard_map/ppermute | solution.py:29
  39.9 6.9 %copy-start = (f32[1024,4,256]{2,1,0:T(4,128)S(1)}, f32[1024,4,256]{2,1,0:T(4,128)}, u32[]{:S(2)}) copy-start(f32[1024,4,256]{2,1,0:T(4,128)} %param.7) | copy-start | bytes 12582916
  43.3 6.5 %collective-permute-start.15 = (f32[64,1024]{1,0:T(8,128)S(1)}, f32[64,1024]{1,0:T(8,128)S(1)}, u32[]{:S(2)}, u32[]{:S(2)}) collective-permute-start(f32[64,1024]{1,0:T(8,128)S(1)} %pad_maximum_fusion.token.refs_0_), channel_id=1, source_target_pairs={{0,3},{1,2},{2,1},{3,0},{4,7},{5,6},{6,5},{7,4},{8,11},{9,10},{10,... | collective-permute-start | bytes 786440 | tf_op jit(solution)/shard_map/ppermute | solution.py:37
  45.9 5.5 %collective-permute-start.14 = (f32[64,1024]{1,0:T(8,128)S(1)}, f32[64,1024]{1,0:T(8,128)S(1)}, u32[]{:S(2)}, u32[]{:S(2)}) collective-permute-start(f32[64,1024]{1,0:T(8,128)S(1)} %pad_maximum_fusion.token.refs_0_), channel_id=1, source_target_pairs={{0,1},{1,0},{2,3},{3,2},{4,5},{5,4},{6,7},{7,6},{8,9},{9,8},{10,11... | collective-permute-start | bytes 786440 | tf_op jit(solution)/shard_map/ppermute | solution.py:37
  45.9 20.9 %collective-permute-start.8 = (f32[1024,128]{1,0:T(8,128)S(1)}, f32[1024,128]{1,0:T(8,128)S(1)}, u32[]{:S(2)}, u32[]{:S(2)}) collective-permute-start(f32[1024,128]{1,0:T(8,128)S(1)} %get-tuple-element.42), channel_id=1, source_target_pairs={{0,64},{4,68},{8,72},{12,76},{16,80},{20,84},{24,88},{28,92},{32,9... | collective-permute-start | bytes 1572872 | tf_op jit(solution)/shard_map/ppermute | solution.py:29
  46.0 20.8 %collective-permute-start.9 = (f32[1024,128]{1,0:T(8,128)S(1)}, f32[1024,128]{1,0:T(8,128)S(1)}, u32[]{:S(2)}, u32[]{:S(2)}) collective-permute-start(f32[1024,128]{1,0:T(8,128)S(1)} %get-tuple-element.43), channel_id=1, source_target_pairs={{0,192},{4,196},{8,200},{12,204},{16,208},{20,212},{24,216},{28,22... | collective-permute-start | bytes 1572872 | tf_op jit(solution)/shard_map/ppermute | solution.py:29
  51.4 5.3 %collective-permute-start.17 = (f32[64,1024]{1,0:T(8,128)S(1)}, f32[64,1024]{1,0:T(8,128)S(1)}, u32[]{:S(2)}, u32[]{:S(2)}) collective-permute-start(f32[64,1024]{1,0:T(8,128)S(1)} %collective-permute-done.14.refs_0_), channel_id=1, source_target_pairs={{0,4},{4,0},{8,12},{12,8},{16,20},{20,16},{24,28},{28,24},{32,36},... | collective-permute-start | bytes 786440 | tf_op jit(solution)/shard_map/ppermute | solution.py:48
  55.6 1.5 %collective-permute-start.18 = (f32[64,1024]{1,0:T(8,128)S(1)}, f32[64,1024]{1,0:T(8,128)S(1)}, u32[]{:S(2)}, u32[]{:S(2)}) collective-permute-start(f32[64,1024]{1,0:T(8,128)S(1)} %collective-permute-done.15.refs_1_), channel_id=1, source_target_pairs={{0,4},{4,0},{8,12},{12,8},{16,20},{20,16},{24,28},{28,24},{32,36},... | collective-permute-start | bytes 786440 | tf_op jit(solution)/shard_map/ppermute | solution.py:48
  55.6 8.9 %collective-permute-start.16 = (f32[64,1024]{1,0:T(8,128)S(1)}, f32[64,1024]{1,0:T(8,128)S(1)}, u32[]{:S(2)}, u32[]{:S(2)}) collective-permute-start(f32[64,1024]{1,0:T(8,128)S(1)} %pad_maximum_fusion.token.refs_0_), channel_id=1, source_target_pairs={{0,2},{1,3},{2,0},{3,1},{4,6},{5,7},{6,4},{7,5},{8,10},{9,11},{10,... | collective-permute-start | bytes 786440 | tf_op jit(solution)/shard_map/ppermute | solution.py:37
  59.6 14.6 %collective-permute-start.20 = (f32[128,1024]{1,0:T(8,128)S(1)}, f32[128,1024]{1,0:T(8,128)S(1)}, u32[]{:S(2)}, u32[]{:S(2)}) collective-permute-start(f32[128,1024]{1,0:T(8,128)S(1)} %get-tuple-element.58), channel_id=1, source_target_pairs={{0,1},{1,0},{2,3},{3,2},{4,5},{5,4},{6,7},{7,6},{8,9},{9,8},{10,11... | collective-permute-start | bytes 1572872 | tf_op jit(solution)/shard_map/ppermute | solution.py:37
  59.7 17.0 %collective-permute-start.21 = (f32[128,1024]{1,0:T(8,128)S(1)}, f32[128,1024]{1,0:T(8,128)S(1)}, u32[]{:S(2)}, u32[]{:S(2)}) collective-permute-start(f32[128,1024]{1,0:T(8,128)S(1)} %get-tuple-element.59), channel_id=1, source_target_pairs={{0,3},{1,2},{2,1},{3,0},{4,7},{5,6},{6,5},{7,4},{8,11},{9,10},{10,... | collective-permute-start | bytes 1572872 | tf_op jit(solution)/shard_map/ppermute | solution.py:37
  64.5 3.7 %collective-permute-start.19 = (f32[64,1024]{1,0:T(8,128)S(1)}, f32[64,1024]{1,0:T(8,128)S(1)}, u32[]{:S(2)}, u32[]{:S(2)}) collective-permute-start(f32[64,1024]{1,0:T(8,128)S(1)} %collective-permute-done.16.refs_0_), channel_id=1, source_target_pairs={{0,4},{4,0},{8,12},{12,8},{16,20},{20,16},{24,28},{28,24},{32,36},... | collective-permute-start | bytes 786440 | tf_op jit(solution)/shard_map/ppermute | solution.py:48
  66.8 3.9 %collective-permute-start.13 = (f32[64,1024]{1,0:T(8,128)S(1)}, f32[64,1024]{1,0:T(8,128)S(1)}, u32[]{:S(2)}, u32[]{:S(2)}) collective-permute-start(f32[64,1024]{1,0:T(8,128)S(1)} %pad_maximum_fusion.token.refs_0_), channel_id=1, source_target_pairs={{0,4},{4,0},{8,12},{12,8},{16,20},{20,16},{24,28},{28,24},{32,36},... | collective-permute-start | bytes 786440 | tf_op jit(solution)/shard_map/ppermute | solution.py:48
  66.8 14.7 %collective-permute-start.22 = (f32[1024,128]{1,0:T(8,128)S(1)}, f32[1024,128]{1,0:T(8,128)S(1)}, u32[]{:S(2)}, u32[]{:S(2)}) collective-permute-start(f32[1024,128]{1,0:T(8,128)S(1)} %get-tuple-element.61), channel_id=1, source_target_pairs={{0,128},{4,132},{8,136},{12,140},{16,144},{20,148},{24,152},{28,15... | collective-permute-start | bytes 1572872 | tf_op jit(solution)/shard_map/ppermute | solution.py:29
  69.8 17.1 %collective-permute-start.23 = (f32[128,1024]{1,0:T(8,128)S(1)}, f32[128,1024]{1,0:T(8,128)S(1)}, u32[]{:S(2)}, u32[]{:S(2)}) collective-permute-start(f32[128,1024]{1,0:T(8,128)S(1)} %get-tuple-element.62), channel_id=1, source_target_pairs={{0,2},{1,3},{2,0},{3,1},{4,6},{5,7},{6,4},{7,5},{8,10},{9,11},{10,... | collective-permute-start | bytes 1572872 | tf_op jit(solution)/shard_map/ppermute | solution.py:37
